TPU v7x, 512 devices: a whole 4x8x8 slice. The times are simulated.
512 devices in a mesh: rep: 16 (over z, core), seq: 32 (over x, y).
Axes of the slice: x: 4, y: 8, z: 8, core: 2. Of those that a mesh axis runs over, the one named last changes fastest.
Arguments:
- normed_input: bfloat16 [16, 4096, 4096], P('rep', 'seq'), may hold values from -6 to 6
- document_index: int32 [16, 4096], P('rep', 'seq'), may hold values from 0 to 63, never falling along the last dimension, each value on 1 to 897 neighbouring positions
- frozen_query_state: bfloat16 [16, 4096, 2048], P('rep', 'seq'), may hold values from -5 to 5
- frozen_keyvalue_weight: bfloat16 [16, 4096, 1024], P('rep', 'seq'), may hold values from -5 to 5
- layer_output_gradient: bfloat16 [16, 4096, 4096], P('rep', 'seq'), may hold values from -0.75 to 0.75
- frozen_output_gradient: bfloat16 [16, 4096, 2048], P('rep', 'seq'), may hold values from -0.75 to 0.75
- adapter_down_weight: bfloat16 [3, 4096, 16], replicated, may hold values from -0.09375 to 0.09375
- query_up_weight: bfloat16 [16, 2048], replicated, may hold values from -1.5 to 1.5
- keyvalue_up_weight: bfloat16 [2, 16, 512], replicated, may hold values from -1.5 to 1.5
- output_down_weight: bfloat16 [2048, 16], replicated, may hold values from -0.125 to 0.125
- output_up_weight: bfloat16 [16, 4096], replicated, may hold values from -1.5 to 1.5
Outputs:
- grad_lora_down: bfloat16 [3, 4096, 16], replicated
- grad_query_up: bfloat16 [16, 2048], replicated
- grad_keyval_up: bfloat16 [2, 16, 512], replicated
- grad_output_down: bfloat16 [2048, 16], replicated
- grad_output_up: bfloat16 [16, 4096], replicated
Inputs may be any that keep to these rules, and one draw needn't show every extreme that they name: document_index never fall along a sequence; each document holds 1 to 897 consecutive positions, and one holds exactly 897.
All inputs are finite; a program needn't handle non-finite values.
Results may differ from a plain program's by a relative error of at most 0.03.
Values may be sent and summed in bfloat16 or wider, within the bound.
No kernel may reach another device: no remote copies, remote signals or barrier semaphores. Data moves between devices by JAX's collectives and lax.ppermute only.
A program may use at most 128 MiB of HBM per device.

v0:
```python
import jax
import jax.numpy as jnp
from jax import lax
from jax.sharding import PartitionSpec as P

QUERY_HEADS = 16
KEY_HEADS = 4
HEAD_SIZE = 128
KEY_COLUMNS = 512


def passed_along(array, axis, by):
    devices = lax.axis_size(axis)
    pairs = [(i, i + by) for i in range(devices) if 0 <= i + by < devices]
    return lax.ppermute(array, axis, pairs)


def masked_scores(query_head_rows, key_block, seen, inverse):
    raw = (
        jnp.einsum("pagd,kad->agpk", query_head_rows, key_block, preferred_element_type=jnp.float32)
        * inverse
    )
    return jnp.where(seen[None, None], raw, -1e30)


def block_dprobs(gradient_heads, value_block):
    return jnp.einsum(
        "pagd,kad->agpk", gradient_heads, value_block, preferred_element_type=jnp.float32
    )


def per_device(
    normed_input,
    document_index,
    frozen_query_state,
    frozen_keyvalue_weight,
    layer_output_gradient,
    frozen_output_gradient,
    adapter_down_weight,
    query_up_weight,
    keyvalue_up_weight,
    output_down_weight,
    output_up_weight,
):
    hidden_state = normed_input[0]
    documents = document_index[0]
    query_rows = frozen_query_state[0]
    keyval_rows = frozen_keyvalue_weight[0]
    outgrad = layer_output_gradient[0]
    frozen_rows = frozen_output_gradient[0]
    row_count = hidden_state.shape[0]
    group_factor = QUERY_HEADS // KEY_HEADS
    inverse = 1.0 / HEAD_SIZE**0.5
    span = lax.axis_size("seq") // 4
    position = lax.axis_index("seq")
    low_rank_state = jnp.einsum(
        "hy,wym->whm", hidden_state, adapter_down_weight, preferred_element_type=jnp.float32
    ).astype(jnp.bfloat16)
    query_matrix = (
        query_rows.astype(jnp.float32)
        + 0.5 * jnp.dot(low_rank_state[0], query_up_weight, preferred_element_type=jnp.float32)
    ).astype(jnp.bfloat16)
    key_delta = jnp.dot(
        low_rank_state[1], keyvalue_up_weight[0], preferred_element_type=jnp.float32
    )
    value_delta = jnp.dot(
        low_rank_state[2], keyvalue_up_weight[1], preferred_element_type=jnp.float32
    )
    keyvals = (
        keyval_rows.astype(jnp.float32) + 0.5 * jnp.concatenate([key_delta, value_delta], axis=1)
    ).astype(jnp.bfloat16)
    kv_list = [keyvals]
    doc_list = [documents]
    current_kv = keyvals
    current_doc = documents
    for offset in range(1, span):
        current_kv, current_doc = passed_along((current_kv, current_doc), "seq", 1)
        kv_list.append(current_kv)
        doc_list.append(current_doc)
    kv_window = jnp.stack(kv_list)
    doc_window = jnp.stack(doc_list)
    attention_window = span * row_count
    offsets = jnp.arange(span, dtype=jnp.int32)
    local_rows = jnp.arange(row_count, dtype=jnp.int32)
    key_pos = ((position - offsets)[:, None] * row_count + local_rows[None, :]).reshape(
        attention_window
    )
    query_pos = position * row_count + local_rows
    visible = (
        (doc_window.reshape(attention_window)[None, :] == documents[:, None])
        & (key_pos[None, :] <= query_pos[:, None])
        & (key_pos[None, :] >= 0)
    )
    keyvalue_flattened = kv_window.reshape(attention_window, 2 * KEY_COLUMNS)
    query_head_rows = query_matrix.reshape(row_count, KEY_HEADS, group_factor, HEAD_SIZE)
    key_head_rows = keyvalue_flattened[:, :KEY_COLUMNS].reshape(
        attention_window, KEY_HEADS, HEAD_SIZE
    )
    value_head_rows = keyvalue_flattened[:, KEY_COLUMNS:].reshape(
        attention_window, KEY_HEADS, HEAD_SIZE
    )
    back_out = jnp.einsum(
        "td,rd->tr", outgrad, output_up_weight, preferred_element_type=jnp.float32
    ).astype(jnp.bfloat16)
    attention_gradient = (
        frozen_rows.astype(jnp.float32)
        + 0.5
        * jnp.einsum("tr,cr->tc", back_out, output_down_weight, preferred_element_type=jnp.float32)
    ).astype(jnp.bfloat16)
    gradient_heads = attention_gradient.reshape(row_count, KEY_HEADS, group_factor, HEAD_SIZE)
    scores = masked_scores(query_head_rows, key_head_rows, visible, inverse)
    maxima = jnp.max(scores, axis=-1, keepdims=True)
    exponentials = jnp.exp(scores - maxima)
    softmax_probs = (exponentials / jnp.sum(exponentials, axis=-1, keepdims=True)).astype(
        jnp.bfloat16
    )
    attn_heads = jnp.einsum(
        "agpk,kad->pagd", softmax_probs, value_head_rows, preferred_element_type=jnp.float32
    ).astype(jnp.bfloat16)
    attended = attn_heads.reshape(row_count, QUERY_HEADS * HEAD_SIZE)
    deltas = jnp.einsum(
        "pagd,pagd->agp", gradient_heads, attn_heads, preferred_element_type=jnp.float32
    )
    dprobs = block_dprobs(gradient_heads, value_head_rows)
    dscores = (softmax_probs.astype(jnp.float32) * (dprobs - deltas[..., None]) * inverse).astype(
        jnp.bfloat16
    )
    dqueries = (
        jnp.einsum("agpk,kad->pagd", dscores, key_head_rows, preferred_element_type=jnp.float32)
        .astype(jnp.bfloat16)
        .reshape(row_count, QUERY_HEADS * HEAD_SIZE)
    )
    dkey_part = jnp.einsum(
        "agpk,pagd->kad", dscores, query_head_rows, preferred_element_type=jnp.float32
    ).reshape(span, row_count, KEY_COLUMNS)
    dvalue_part = jnp.einsum(
        "agpk,pagd->kad", softmax_probs, gradient_heads, preferred_element_type=jnp.float32
    ).reshape(span, row_count, KEY_COLUMNS)
    partials = jnp.concatenate([dkey_part, dvalue_part], axis=2)
    summed = partials[span - 1]
    for offset in range(span - 2, -1, -1):
        summed = (
            passed_along(summed.astype(jnp.bfloat16), "seq", -1).astype(summed.dtype)
            + partials[offset]
        )
    dkeyvals = summed.astype(jnp.bfloat16)
    back_query = jnp.einsum(
        "tc,rc->tr", dqueries, query_up_weight, preferred_element_type=jnp.float32
    ).astype(jnp.bfloat16)
    back_key = jnp.einsum(
        "tc,rc->tr",
        dkeyvals[:, :KEY_COLUMNS],
        keyvalue_up_weight[0],
        preferred_element_type=jnp.float32,
    ).astype(jnp.bfloat16)
    back_value = jnp.einsum(
        "tc,rc->tr",
        dkeyvals[:, KEY_COLUMNS:],
        keyvalue_up_weight[1],
        preferred_element_type=jnp.float32,
    ).astype(jnp.bfloat16)
    factor = 0.5 / lax.axis_size("rep")
    term_down = factor * jnp.stack(
        [
            jnp.einsum("td,tr->dr", hidden_state, piece, preferred_element_type=jnp.float32)
            for piece in (back_query, back_key, back_value)
        ]
    )
    term_query_up = factor * jnp.einsum(
        "tr,tc->rc", low_rank_state[0], dqueries, preferred_element_type=jnp.float32
    )
    term_keyval_up = factor * jnp.stack(
        [
            jnp.einsum(
                "tr,tc->rc",
                low_rank_state[1],
                dkeyvals[:, :KEY_COLUMNS],
                preferred_element_type=jnp.float32,
            ),
            jnp.einsum(
                "tr,tc->rc",
                low_rank_state[2],
                dkeyvals[:, KEY_COLUMNS:],
                preferred_element_type=jnp.float32,
            ),
        ]
    )
    low_out = jnp.dot(attended, output_down_weight, preferred_element_type=jnp.float32).astype(
        jnp.bfloat16
    )
    term_output_down = factor * jnp.einsum(
        "tc,tr->cr", attended, back_out, preferred_element_type=jnp.float32
    )
    term_output_up = factor * jnp.einsum(
        "tr,td->rd", low_out, outgrad, preferred_element_type=jnp.float32
    )
    totals = lax.psum(
        (term_down, term_query_up, term_keyval_up, term_output_down, term_output_up), ("rep", "seq")
    )
    return (
        totals[0].astype(jnp.bfloat16),
        totals[1].astype(jnp.bfloat16),
        totals[2].astype(jnp.bfloat16),
        totals[3].astype(jnp.bfloat16),
        totals[4].astype(jnp.bfloat16),
    )


def solution(mesh):
    placed = (
        P("rep", "seq", None),
        P("rep", "seq"),
        P("rep", "seq", None),
        P("rep", "seq", None),
        P("rep", "seq", None),
        P("rep", "seq", None),
        P(),
        P(),
        P(),
        P(),
        P(),
    )
    return jax.shard_map(
        per_device, mesh=mesh, in_specs=placed, out_specs=(P(), P(), P(), P(), P()), check_vma=False
    )
```

profile of v0, /device:TPU:1, one launch (start us, length us, event | category | flops | bytes accessed | tf_op | source)
XLA Modules:
  0.0 317.3 jit_solution(13651845521305641193)
XLA Ops:
  7.1 4.7 %collective-permute-start = (bf16[128,1024]{1,0:T(8,128)(2,1)}, bf16[128,1024]{1,0:T(8,128)(2,1)}, u32[]{:S(2)}, u32[]{:S(2)}) collective-permute-start(bf16[128,1024]{1,0:T(8,128)(2,1)} %fusion.23), channel_id=1, source_target_pairs={{0,1},{1,2},{2,3},{3,4},{4,5},{5,6},{6,7},{7,8},{8,9},{9,10},{10,1... | collective-permute-start | bytes 786440 | tf_op jit(solution)/shard_map/ppermute | solution.py:15
  11.9 2.5 collective-permute-start.7
  16.9 3.2 %collective-permute-start.8 = (s32[128]{0:T(128)S(1)}, s32[128]{0:T(128)S(1)}, u32[]{:S(2)}, u32[]{:S(2)}) collective-permute-start(s32[128]{0:T(128)S(1)} %collective-permute-done.7), channel_id=1, source_target_pairs={{0,1},{1,2},{2,3},{3,4},{4,5},{5,6},{6,7},{7,8},{8,9},{9,10},{10,1... | collective-permute-start | bytes 1544 | tf_op jit(solution)/shard_map/ppermute | solution.py:15
  20.1 2.2 fusion.12
  22.3 4.4 %collective-permute-start.9 = (s32[128]{0:T(128)S(1)}, s32[128]{0:T(128)S(1)}, u32[]{:S(2)}, u32[]{:S(2)}) collective-permute-start(s32[128]{0:T(128)S(1)} %collective-permute-done.8), channel_id=1, source_target_pairs={{0,1},{1,2},{2,3},{3,4},{4,5},{5,6},{6,7},{7,8},{8,9},{9,10},{10,1... | collective-permute-start | bytes 1544 | tf_op jit(solution)/shard_map/ppermute | solution.py:15
  26.7 3.5 %collective-permute-start.1 = (bf16[128,1024]{1,0:T(8,128)(2,1)}, bf16[128,1024]{1,0:T(8,128)(2,1)}, u32[]{:S(2)}, u32[]{:S(2)}) collective-permute-start(bf16[128,1024]{1,0:T(8,128)(2,1)} %collective-permute-done), channel_id=1, source_target_pairs={{0,1},{1,2},{2,3},{3,4},{4,5},{5,6},{6,7},{7,8},{8,9},{9,10},{10,1... | collective-permute-start | bytes 786440 | tf_op jit(solution)/shard_map/ppermute | solution.py:15
  30.9 4.6 %collective-permute-start.10 = (s32[128]{0:T(128)S(1)}, s32[128]{0:T(128)S(1)}, u32[]{:S(2)}, u32[]{:S(2)}) collective-permute-start(s32[128]{0:T(128)S(1)} %collective-permute-done.9), channel_id=1, source_target_pairs={{0,1},{1,2},{2,3},{3,4},{4,5},{5,6},{6,7},{7,8},{8,9},{9,10},{10,1... | collective-permute-start | bytes 1544 | tf_op jit(solution)/shard_map/ppermute | solution.py:15
  36.2 3.7 %collective-permute-start.11 = (s32[128]{0:T(128)S(1)}, s32[128]{0:T(128)S(1)}, u32[]{:S(2)}, u32[]{:S(2)}) collective-permute-start(s32[128]{0:T(128)S(1)} %collective-permute-done.10), channel_id=1, source_target_pairs={{0,1},{1,2},{2,3},{3,4},{4,5},{5,6},{6,7},{7,8},{8,9},{9,10},{10,1... | collective-permute-start | bytes 1544 | tf_op jit(solution)/shard_map/ppermute | solution.py:15
  40.0 3.6 %collective-permute-start.2 = (bf16[128,1024]{1,0:T(8,128)(2,1)}, bf16[128,1024]{1,0:T(8,128)(2,1)S(1)}, u32[]{:S(2)}, u32[]{:S(2)}) collective-permute-start(bf16[128,1024]{1,0:T(8,128)(2,1)} %collective-permute-done.1), channel_id=1, source_target_pairs={{0,1},{1,2},{2,3},{3,4},{4,5},{5,6},{6,7},{7,8},{8,9},{9,10},{10,1... | collective-permute-start | bytes 786440 | tf_op jit(solution)/shard_map/ppermute | solution.py:15
  43.7 1.9 collective-permute-start.12
  47.2 3.8 %collective-permute-start.13 = (s32[128]{0:T(128)S(1)}, s32[128]{0:T(128)S(1)}, u32[]{:S(2)}, u32[]{:S(2)}) collective-permute-start(s32[128]{0:T(128)S(1)} %collective-permute-done.12), channel_id=1, source_target_pairs={{0,1},{1,2},{2,3},{3,4},{4,5},{5,6},{6,7},{7,8},{8,9},{9,10},{10,1... | collective-permute-start | bytes 1544 | tf_op jit(solution)/shard_map/ppermute | solution.py:15
  51.0 2.8 collective-permute-start.3
  55.1 2.1 copy.74
  59.7 3.0 collective-permute-start.4
  67.0 3.8 %collective-permute-start.5 = (bf16[128,1024]{1,0:T(8,128)(2,1)S(1)}, bf16[128,1024]{1,0:T(8,128)(2,1)S(1)}, u32[]{:S(2)}, u32[]{:S(2)}) collective-permute-start(bf16[128,1024]{1,0:T(8,128)(2,1)S(1)} %collective-permute-done.4), channel_id=1, source_target_pairs={{0,1},{1,2},{2,3},{3,4},{4,5},{5,6},{6,7},{7,8},{8,9},{9,10},{10,1... | collective-permute-start | bytes 786440 | tf_op jit(solution)/shard_map/ppermute | solution.py:15
  72.2 3.9 %collective-permute-done.5 = bf16[128,1024]{1,0:T(8,128)(2,1)S(1)} collective-permute-done((bf16[128,1024]{1,0:T(8,128)(2,1)S(1)}, bf16[128,1024]{1,0:T(8,128)(2,1)S(1)}, u32[]{:S(2)}, u32[]{:S(2)}) %collective-permute-start.5) | collective-permute-done | bytes 262176 | tf_op jit(solution)/shard_map/ppermute | solution.py:15
  76.1 4.3 %collective-permute-start.6 = (bf16[128,1024]{1,0:T(8,128)(2,1)S(1)}, bf16[128,1024]{1,0:T(8,128)(2,1)S(1)}, u32[]{:S(2)}, u32[]{:S(2)}) collective-permute-start(bf16[128,1024]{1,0:T(8,128)(2,1)S(1)} %collective-permute-done.5), channel_id=1, source_target_pairs={{0,1},{1,2},{2,3},{3,4},{4,5},{5,6},{6,7},{7,8},{8,9},{9,10},{10,1... | collective-permute-start | bytes 786440 | tf_op jit(solution)/shard_map/ppermute | solution.py:15
  81.8 3.5 %collective-permute-done.6 = bf16[128,1024]{1,0:T(8,128)(2,1)S(1)} collective-permute-done((bf16[128,1024]{1,0:T(8,128)(2,1)S(1)}, bf16[128,1024]{1,0:T(8,128)(2,1)S(1)}, u32[]{:S(2)}, u32[]{:S(2)}) %collective-permute-start.6) | collective-permute-done | bytes 262176 | tf_op jit(solution)/shard_map/ppermute | solution.py:15
  86.1 2.7 fusion.61
  89.3 1.9 copy.73
  91.2 7.3 %fusion.62 = (f32[4,4,128]{2,1,0:T(4,128)S(1)}, f32[4,4,128,1024]{2,3,1,0:T(8,128)}) fusion(pred[128,1024]{0,1:T(8,128)(4,1)S(1)} %and_and_fusion, bf16[1024,4,128,1]{0,2,3,1:T(8,128)(2,1)S(1)} %bitcast.238, bf16[128,4,4,128]{0,3,2,1:T(8,128)(2,1)} %bitcast.246), kind=kOutput, calls=%fused_computation.110 | convolution fusion | flops 545260544 | bytes 10100736 | tf_op jit(solution)/shard_map/sub | solution.py:113
  98.4 4.5 %divide_convert_fusion = bf16[4,4,128,1024]{2,3,1,0:T(8,128)(2,1)S(1)} fusion(f32[4,4,128,1024]{2,3,1,0:T(8,128)} %get-tuple-element.20, f32[4,4,128]{2,1,0:T(4,128)S(1)} %get-tuple-element.19), kind=kLoop, calls=%fused_computation.6 | loop fusion | flops 4194304 | bytes 12591104 | tf_op jit(solution)/shard_map/convert_element_type | solution.py:114
  105.3 1.9 fusion.3
  111.8 3.2 %fusion.60 = (f32[1,128,1024]{1,0,2:T(1,128)S(1)}, f32[1,128,1024]{1,0,2:T(1,128)S(1)}, f32[1,128,1024]{1,0,2:T(1,128)S(1)}, f32[1,128,1024]{1,0,2:T(1,128)S(1)}...) fusion(f32[8,128,1024]{1,0,2:T(8,128)S(1)} %constant_dynamic-update-slice_fusion), kind=kLoop, calls=%fused_computation.108 | loop fusion | bytes 7340032 | tf_op jit(solution)/shard_map/slice | solution.py:144
  115.0 3.4 %collective-permute-done.14 = bf16[128,1024]{0,1:T(8,128)(2,1)S(1)} collective-permute-done((bf16[128,1024]{0,1:T(8,128)(2,1)S(1)}, bf16[128,1024]{0,1:T(8,128)(2,1)S(1)}, u32[]{:S(2)}, u32[]{:S(2)}) %collective-permute-start.14) | collective-permute-done | bytes 262176 | tf_op jit(solution)/shard_map/ppermute | solution.py:15
  119.8 7.8 %collective-permute-done.15 = bf16[128,1024]{0,1:T(8,128)(2,1)S(1)} collective-permute-done((bf16[128,1024]{0,1:T(8,128)(2,1)S(1)}, bf16[128,1024]{0,1:T(8,128)(2,1)S(1)}, u32[]{:S(2)}, u32[]{:S(2)}) %collective-permute-start.15) | collective-permute-done | bytes 262176 | tf_op jit(solution)/shard_map/ppermute | solution.py:15
  128.9 6.1 %collective-permute-done.16 = bf16[128,1024]{0,1:T(8,128)(2,1)S(1)} collective-permute-done((bf16[128,1024]{0,1:T(8,128)(2,1)S(1)}, bf16[128,1024]{0,1:T(8,128)(2,1)S(1)}, u32[]{:S(2)}, u32[]{:S(2)}) %collective-permute-start.16) | collective-permute-done | bytes 262176 | tf_op jit(solution)/shard_map/ppermute | solution.py:15
  136.6 9.8 %collective-permute-done.17 = bf16[128,1024]{0,1:T(8,128)(2,1)S(1)} collective-permute-done((bf16[128,1024]{0,1:T(8,128)(2,1)S(1)}, bf16[128,1024]{0,1:T(8,128)(2,1)S(1)}, u32[]{:S(2)}, u32[]{:S(2)}) %collective-permute-start.17) | collective-permute-done | bytes 262176 | tf_op jit(solution)/shard_map/ppermute | solution.py:15
  149.0 4.8 %collective-permute-done.18 = bf16[128,1024]{0,1:T(8,128)(2,1)S(1)} collective-permute-done((bf16[128,1024]{0,1:T(8,128)(2,1)S(1)}, bf16[128,1024]{0,1:T(8,128)(2,1)S(1)}, u32[]{:S(2)}, u32[]{:S(2)}) %collective-permute-start.18) | collective-permute-done | bytes 262176 | tf_op jit(solution)/shard_map/ppermute | solution.py:15
  157.5 4.7 %collective-permute-done.19 = bf16[128,1024]{0,1:T(8,128)(2,1)} collective-permute-done((bf16[128,1024]{0,1:T(8,128)(2,1)}, bf16[128,1024]{0,1:T(8,128)(2,1)}, u32[]{:S(2)}, u32[]{:S(2)}) %collective-permute-start.19) | collective-permute-done | bytes 262176 | tf_op jit(solution)/shard_map/ppermute | solution.py:15
  166.6 5.1 %collective-permute-done.20 = bf16[128,1024]{0,1:T(8,128)(2,1)S(1)} collective-permute-done((bf16[128,1024]{0,1:T(8,128)(2,1)S(1)}, bf16[128,1024]{0,1:T(8,128)(2,1)S(1)}, u32[]{:S(2)}, u32[]{:S(2)}) %collective-permute-start.20) | collective-permute-done | bytes 262176 | tf_op jit(solution)/shard_map/ppermute | solution.py:15
  174.3 143.0 %all-reduce.2 = (bf16[3,4096,16]{1,2,0:T(8,128)(2,1)}, bf16[16,2048]{1,0:T(8,128)(2,1)}, bf16[2,16,512]{2,1,0:T(8,128)(2,1)}, bf16[2048,16]{0,1:T(8,128)(2,1)}, bf16[16,4096]{1,0:T(8,128)(2,1)}) all-reduce(f32[3,4096,16]{1,2,0:T(8,128)S(1)} %maximum_multiply_fusion, ...), channel_id=1, replica_groups=mesh['rep'=16,'seq'=32] {'rep','seq'}, use_global_device_ids=true, to_apply=%region_2.3 | all-reduce | flops 344064 | bytes 2064384 | tf_op jit(solution)/shard_map/psum | solution.py:197
  (97 shorter events, 48.6 us)
Async XLA Ops:
  0.6 29.5 %copy-start.7 = (bf16[1,128,1024]{2,1,0:T(8,128)(2,1)S(1)}, bf16[1,128,1024]{2,1,0:T(8,128)(2,1)}, u32[]{:S(2)}) copy-start(bf16[1,128,1024]{2,1,0:T(8,128)(2,1)} %param.14) | copy-start | bytes 786436
  0.7 15.3 %copy-start.8 = (bf16[1,128,2048]{2,1,0:T(8,128)(2,1)S(1)}, bf16[1,128,2048]{2,1,0:T(8,128)(2,1)}, u32[]{:S(2)}) copy-start(bf16[1,128,2048]{2,1,0:T(8,128)(2,1)} %param.16) | copy-start | bytes 1572868
  0.7 15.3 %copy-start.9 = (bf16[2048,16]{0,1:T(8,128)(2,1)S(1)}, bf16[2048,16]{0,1:T(8,128)(2,1)}, u32[]{:S(2)}) copy-start(bf16[2048,16]{0,1:T(8,128)(2,1)} %param.20) | copy-start | bytes 196612
  2.0 18.0 %copy-start.10 = (bf16[16,2048]{1,0:T(8,128)(2,1)S(1)}, bf16[16,2048]{1,0:T(8,128)(2,1)}, u32[]{:S(2)}) copy-start(bf16[16,2048]{1,0:T(8,128)(2,1)} %param.18) | copy-start | bytes 196612
  7.1 19.6 %collective-permute-start = (bf16[128,1024]{1,0:T(8,128)(2,1)}, bf16[128,1024]{1,0:T(8,128)(2,1)}, u32[]{:S(2)}, u32[]{:S(2)}) collective-permute-start(bf16[128,1024]{1,0:T(8,128)(2,1)} %fusion.23), channel_id=1, source_target_pairs={{0,1},{1,2},{2,3},{3,4},{4,5},{5,6},{6,7},{7,8},{8,9},{9,10},{10,1... | collective-permute-start | bytes 786440 | tf_op jit(solution)/shard_map/ppermute | solution.py:15
  11.9 5.0 %collective-permute-start.7 = (s32[128]{0:T(128)}, s32[128]{0:T(128)S(1)}, u32[]{:S(2)}, u32[]{:S(2)}) collective-permute-start(s32[128]{0:T(128)} %bitcast.250), channel_id=1, source_target_pairs={{0,1},{1,2},{2,3},{3,4},{4,5},{5,6},{6,7},{7,8},{8,9},{9,10},{10,1... | collective-permute-start | bytes 1544 | tf_op jit(solution)/shard_map/ppermute | solution.py:15
  16.7 42.1 %copy-start.12 = (s32[1,128]{1,0:T(1,128)S(1)}, s32[1,128]{1,0:T(1,128)}, u32[]{:S(2)}) copy-start(s32[1,128]{1,0:T(1,128)} %param.12) | copy-start | bytes 1540
  16.9 5.4 %collective-permute-start.8 = (s32[128]{0:T(128)S(1)}, s32[128]{0:T(128)S(1)}, u32[]{:S(2)}, u32[]{:S(2)}) collective-permute-start(s32[128]{0:T(128)S(1)} %collective-permute-done.7), channel_id=1, source_target_pairs={{0,1},{1,2},{2,3},{3,4},{4,5},{5,6},{6,7},{7,8},{8,9},{9,10},{10,1... | collective-permute-start | bytes 1544 | tf_op jit(solution)/shard_map/ppermute | solution.py:15
  22.3 8.7 %collective-permute-start.9 = (s32[128]{0:T(128)S(1)}, s32[128]{0:T(128)S(1)}, u32[]{:S(2)}, u32[]{:S(2)}) collective-permute-start(s32[128]{0:T(128)S(1)} %collective-permute-done.8), channel_id=1, source_target_pairs={{0,1},{1,2},{2,3},{3,4},{4,5},{5,6},{6,7},{7,8},{8,9},{9,10},{10,1... | collective-permute-start | bytes 1544 | tf_op jit(solution)/shard_map/ppermute | solution.py:15
  26.7 13.3 %collective-permute-start.1 = (bf16[128,1024]{1,0:T(8,128)(2,1)}, bf16[128,1024]{1,0:T(8,128)(2,1)}, u32[]{:S(2)}, u32[]{:S(2)}) collective-permute-start(bf16[128,1024]{1,0:T(8,128)(2,1)} %collective-permute-done), channel_id=1, source_target_pairs={{0,1},{1,2},{2,3},{3,4},{4,5},{5,6},{6,7},{7,8},{8,9},{9,10},{10,1... | collective-permute-start | bytes 786440 | tf_op jit(solution)/shard_map/ppermute | solution.py:15
  30.9 5.3 %collective-permute-start.10 = (s32[128]{0:T(128)S(1)}, s32[128]{0:T(128)S(1)}, u32[]{:S(2)}, u32[]{:S(2)}) collective-permute-start(s32[128]{0:T(128)S(1)} %collective-permute-done.9), channel_id=1, source_target_pairs={{0,1},{1,2},{2,3},{3,4},{4,5},{5,6},{6,7},{7,8},{8,9},{9,10},{10,1... | collective-permute-start | bytes 1544 | tf_op jit(solution)/shard_map/ppermute | solution.py:15
  36.2 7.4 %collective-permute-start.11 = (s32[128]{0:T(128)S(1)}, s32[128]{0:T(128)S(1)}, u32[]{:S(2)}, u32[]{:S(2)}) collective-permute-start(s32[128]{0:T(128)S(1)} %collective-permute-done.10), channel_id=1, source_target_pairs={{0,1},{1,2},{2,3},{3,4},{4,5},{5,6},{6,7},{7,8},{8,9},{9,10},{10,1... | collective-permute-start | bytes 1544 | tf_op jit(solution)/shard_map/ppermute | solution.py:15
  40.0 11.0 %collective-permute-start.2 = (bf16[128,1024]{1,0:T(8,128)(2,1)}, bf16[128,1024]{1,0:T(8,128)(2,1)S(1)}, u32[]{:S(2)}, u32[]{:S(2)}) collective-permute-start(bf16[128,1024]{1,0:T(8,128)(2,1)} %collective-permute-done.1), channel_id=1, source_target_pairs={{0,1},{1,2},{2,3},{3,4},{4,5},{5,6},{6,7},{7,8},{8,9},{9,10},{10,1... | collective-permute-start | bytes 786440 | tf_op jit(solution)/shard_map/ppermute | solution.py:15
  43.7 3.5 %collective-permute-start.12 = (s32[128]{0:T(128)S(1)}, s32[128]{0:T(128)S(1)}, u32[]{:S(2)}, u32[]{:S(2)}) collective-permute-start(s32[128]{0:T(128)S(1)} %collective-permute-done.11), channel_id=1, source_target_pairs={{0,1},{1,2},{2,3},{3,4},{4,5},{5,6},{6,7},{7,8},{8,9},{9,10},{10,1... | collective-permute-start | bytes 1544 | tf_op jit(solution)/shard_map/ppermute | solution.py:15
  47.2 11.5 %collective-permute-start.13 = (s32[128]{0:T(128)S(1)}, s32[128]{0:T(128)S(1)}, u32[]{:S(2)}, u32[]{:S(2)}) collective-permute-start(s32[128]{0:T(128)S(1)} %collective-permute-done.12), channel_id=1, source_target_pairs={{0,1},{1,2},{2,3},{3,4},{4,5},{5,6},{6,7},{7,8},{8,9},{9,10},{10,1... | collective-permute-start | bytes 1544 | tf_op jit(solution)/shard_map/ppermute | solution.py:15
  51.0 8.7 %collective-permute-start.3 = (bf16[128,1024]{1,0:T(8,128)(2,1)S(1)}, bf16[128,1024]{1,0:T(8,128)(2,1)S(1)}, u32[]{:S(2)}, u32[]{:S(2)}) collective-permute-start(bf16[128,1024]{1,0:T(8,128)(2,1)S(1)} %collective-permute-done.2), channel_id=1, source_target_pairs={{0,1},{1,2},{2,3},{3,4},{4,5},{5,6},{6,7},{7,8},{8,9},{9,10},{10,1... | collective-permute-start | bytes 786440 | tf_op jit(solution)/shard_map/ppermute | solution.py:15
  59.7 7.3 %collective-permute-start.4 = (bf16[128,1024]{1,0:T(8,128)(2,1)S(1)}, bf16[128,1024]{1,0:T(8,128)(2,1)S(1)}, u32[]{:S(2)}, u32[]{:S(2)}) collective-permute-start(bf16[128,1024]{1,0:T(8,128)(2,1)S(1)} %collective-permute-done.3), channel_id=1, source_target_pairs={{0,1},{1,2},{2,3},{3,4},{4,5},{5,6},{6,7},{7,8},{8,9},{9,10},{10,1... | collective-permute-start | bytes 786440 | tf_op jit(solution)/shard_map/ppermute | solution.py:15
  67.0 9.1 %collective-permute-start.5 = (bf16[128,1024]{1,0:T(8,128)(2,1)S(1)}, bf16[128,1024]{1,0:T(8,128)(2,1)S(1)}, u32[]{:S(2)}, u32[]{:S(2)}) collective-permute-start(bf16[128,1024]{1,0:T(8,128)(2,1)S(1)} %collective-permute-done.4), channel_id=1, source_target_pairs={{0,1},{1,2},{2,3},{3,4},{4,5},{5,6},{6,7},{7,8},{8,9},{9,10},{10,1... | collective-permute-start | bytes 786440 | tf_op jit(solution)/shard_map/ppermute | solution.py:15
  76.1 9.3 %collective-permute-start.6 = (bf16[128,1024]{1,0:T(8,128)(2,1)S(1)}, bf16[128,1024]{1,0:T(8,128)(2,1)S(1)}, u32[]{:S(2)}, u32[]{:S(2)}) collective-permute-start(bf16[128,1024]{1,0:T(8,128)(2,1)S(1)} %collective-permute-done.5), channel_id=1, source_target_pairs={{0,1},{1,2},{2,3},{3,4},{4,5},{5,6},{6,7},{7,8},{8,9},{9,10},{10,1... | collective-permute-start | bytes 786440 | tf_op jit(solution)/shard_map/ppermute | solution.py:15
  89.3 9.1 %copy-start.2 = (bf16[1024,512]{0,1:T(8,128)(2,1)}, bf16[1024,512]{0,1:T(8,128)(2,1)S(1)}, u32[]{:S(2)}) copy-start(bf16[1024,512]{0,1:T(8,128)(2,1)S(1)} %copy.72) | copy-start | bytes 3145732
  98.4 4.5 %copy-start.6 = (bf16[128,4,4,128]{0,3,2,1:T(8,128)(2,1)S(1)}, bf16[128,4,4,128]{0,3,2,1:T(8,128)(2,1)}, u32[]{:S(2)}) copy-start(bf16[128,4,4,128]{0,3,2,1:T(8,128)(2,1)} %copy.43) | copy-start | bytes 1572868
  105.3 1.9 copy-start.5
  110.4 37.6 %copy-start.3 = (bf16[1024,512]{0,1:T(8,128)(2,1)S(1)}, bf16[1024,512]{0,1:T(8,128)(2,1)}, u32[]{:S(2)}) copy-start(bf16[1024,512]{0,1:T(8,128)(2,1)} %copy-done.2) | copy-start | bytes 3145732
  110.4 8.0 %collective-permute-start.14 = (bf16[128,1024]{0,1:T(8,128)(2,1)S(1)}, bf16[128,1024]{0,1:T(8,128)(2,1)S(1)}, u32[]{:S(2)}, u32[]{:S(2)}) collective-permute-start(bf16[128,1024]{0,1:T(8,128)(2,1)S(1)} %bitcast.248), channel_id=1, source_target_pairs={{1,0},{2,1},{3,2},{4,3},{5,4},{6,5},{7,6},{8,7},{9,8},{10,9},{11,1... | collective-permute-start | bytes 786440 | tf_op jit(solution)/shard_map/ppermute | solution.py:15
  118.5 9.1 %collective-permute-start.15 = (bf16[128,1024]{0,1:T(8,128)(2,1)S(1)}, bf16[128,1024]{0,1:T(8,128)(2,1)S(1)}, u32[]{:S(2)}, u32[]{:S(2)}) collective-permute-start(bf16[128,1024]{0,1:T(8,128)(2,1)S(1)} %fusion.35), channel_id=1, source_target_pairs={{1,0},{2,1},{3,2},{4,3},{5,4},{6,5},{7,6},{8,7},{9,8},{10,9},{11,1... | collective-permute-start | bytes 786440 | tf_op jit(solution)/shard_map/ppermute | solution.py:15
  127.6 7.4 %collective-permute-start.16 = (bf16[128,1024]{0,1:T(8,128)(2,1)S(1)}, bf16[128,1024]{0,1:T(8,128)(2,1)S(1)}, u32[]{:S(2)}, u32[]{:S(2)}) collective-permute-start(bf16[128,1024]{0,1:T(8,128)(2,1)S(1)} %fusion.33), channel_id=1, source_target_pairs={{1,0},{2,1},{3,2},{4,3},{5,4},{6,5},{7,6},{8,7},{9,8},{10,9},{11,1... | collective-permute-start | bytes 786440 | tf_op jit(solution)/shard_map/ppermute | solution.py:15
  135.1 11.4 %collective-permute-start.17 = (bf16[128,1024]{0,1:T(8,128)(2,1)S(1)}, bf16[128,1024]{0,1:T(8,128)(2,1)S(1)}, u32[]{:S(2)}, u32[]{:S(2)}) collective-permute-start(bf16[128,1024]{0,1:T(8,128)(2,1)S(1)} %fusion.31), channel_id=1, source_target_pairs={{1,0},{2,1},{3,2},{4,3},{5,4},{6,5},{7,6},{8,7},{9,8},{10,9},{11,1... | collective-permute-start | bytes 786440 | tf_op jit(solution)/shard_map/ppermute | solution.py:15
  146.5 9.4 %copy-start.1 = (bf16[1,128,4096]{2,1,0:T(8,128)(2,1)S(1)}, bf16[1,128,4096]{2,1,0:T(8,128)(2,1)}, u32[]{:S(2)}) copy-start(bf16[1,128,4096]{2,1,0:T(8,128)(2,1)} %param.15) | copy-start | bytes 3145732
  146.5 7.2 %collective-permute-start.18 = (bf16[128,1024]{0,1:T(8,128)(2,1)S(1)}, bf16[128,1024]{0,1:T(8,128)(2,1)S(1)}, u32[]{:S(2)}, u32[]{:S(2)}) collective-permute-start(bf16[128,1024]{0,1:T(8,128)(2,1)S(1)} %fusion.29), channel_id=1, source_target_pairs={{1,0},{2,1},{3,2},{4,3},{5,4},{6,5},{7,6},{8,7},{9,8},{10,9},{11,1... | collective-permute-start | bytes 786440 | tf_op jit(solution)/shard_map/ppermute | solution.py:15
  154.5 7.7 %collective-permute-start.19 = (bf16[128,1024]{0,1:T(8,128)(2,1)}, bf16[128,1024]{0,1:T(8,128)(2,1)}, u32[]{:S(2)}, u32[]{:S(2)}) collective-permute-start(bf16[128,1024]{0,1:T(8,128)(2,1)} %fusion.27), channel_id=1, source_target_pairs={{1,0},{2,1},{3,2},{4,3},{5,4},{6,5},{7,6},{8,7},{9,8},{10,9},{11,1... | collective-permute-start | bytes 786440 | tf_op jit(solution)/shard_map/ppermute | solution.py:15
  157.5 15.6 %copy-start.11 = (bf16[2,16,512]{2,1,0:T(8,128)(2,1)S(1)}, bf16[2,16,512]{2,1,0:T(8,128)(2,1)}, u32[]{:S(2)}) copy-start(bf16[2,16,512]{2,1,0:T(8,128)(2,1)} %param.19) | copy-start | bytes 98308
  163.4 8.3 %collective-permute-start.20 = (bf16[128,1024]{0,1:T(8,128)(2,1)S(1)}, bf16[128,1024]{0,1:T(8,128)(2,1)S(1)}, u32[]{:S(2)}, u32[]{:S(2)}) collective-permute-start(bf16[128,1024]{0,1:T(8,128)(2,1)S(1)} %fusion.25), channel_id=1, source_target_pairs={{1,0},{2,1},{3,2},{4,3},{5,4},{6,5},{7,6},{8,7},{9,8},{10,9},{11,1... | collective-permute-start | bytes 786440 | tf_op jit(solution)/shard_map/ppermute | solution.py:15
  (2 other events, 2.9 us)
where the time goes:
time: 319 us; the launch traced here: 317 us
  blocking collectives  143 us (45%)
  starting transfers between devices  59.4 us (19%)
  waiting for transfers between devices  52.3 us (16%)
  matrix products  26.3 us (8%)
  local copies, waits for them, and re-layouts  23.7 us (7%)
  other arithmetic  11.4 us (4%)
    psum x1, blocking collectives, per_device(): lax.psum((term_down, term_query_up, term_keyval_up, term_output_down, ter...  143 us
    ppermute x21, starting transfers between devices, passed_along(): return lax.ppermute(array, axis, pairs)  59.4 us
    ppermute x21, waiting for transfers between devices, passed_along(): return lax.ppermute(array, axis, pairs)  52.3 us
    unnamed x39, local copies, waits for them, and re-layouts  12.8 us
    sub x1, matrix products, per_device(): exponentials = jnp.exp(scores - maxima)  7.26 us
  transfers between devices with their start and end apart: 21, of which 12 were waited for; matrix products, arithmetic and copies ran while one was open for 8% of the time, Pallas kernels for 0%

commit v1 on v0

v1 whole, which is shorter than its diff:
```python
import jax
import jax.numpy as jnp
from jax import lax
from jax.experimental import pallas as pl
from jax.experimental.pallas import tpu as pltpu
from jax.sharding import Mesh, PartitionSpec as P

QUERY_HEADS = 16
KEY_HEADS = 4
HEAD_SIZE = 128
KEY_COLUMNS = 512
ROWS = 128
RANK = 16
SPAN = 8
GROUP = QUERY_HEADS // KEY_HEADS
WIDTH = 4096
QUERY_COLUMNS = QUERY_HEADS * HEAD_SIZE
PACK_ROWS = ROWS + 16
BF = jnp.bfloat16
F32 = jnp.float32
INVERSE = 1.0 / HEAD_SIZE**0.5

NT = (((1,), (1,)), ((), ()))
TN = (((0,), (0,)), ((), ()))
NN = (((1,), (0,)), ((), ()))


def dot(a, b, dims=NN):
    return lax.dot_general(a, b, dims, preferred_element_type=F32)


def keyval_kernel(x_ref, down_ref, keyval_ref, up_ref, doc_ref, low_ref, pack_ref):
    low = dot(down_ref[...], x_ref[...], NT).astype(BF)
    low_ref[...] = low
    for c in range(2):
        part = pl.ds(c * KEY_COLUMNS, KEY_COLUMNS)
        delta = dot(low[(c + 1) * RANK : (c + 2) * RANK], up_ref[c], TN)
        pack_ref[pl.ds(0, ROWS), part] = (
            keyval_ref[:, part].astype(F32) + 0.5 * delta
        ).astype(BF)
    documents = jnp.broadcast_to(doc_ref[...].astype(F32), (RANK, ROWS)).astype(BF)
    pack_ref[pl.ds(ROWS, RANK), :] = jnp.concatenate(
        [low[RANK : 2 * RANK], low[2 * RANK :], documents, jnp.zeros((RANK, 5 * ROWS), BF)], axis=1
    )


def query_kernel(low_ref, query_ref, query_up_ref, outgrad_ref, out_up_ref, frozen_ref, out_down_ref,
                 q_ref, grad_ref, back_out_ref):
    q_ref[...] = (
        query_ref[...].astype(F32) + 0.5 * dot(low_ref[pl.ds(0, RANK), :], query_up_ref[...], TN)
    ).astype(BF)
    back_out = dot(out_up_ref[...], outgrad_ref[...], NT).astype(BF)
    back_out_ref[...] = back_out
    grad_ref[...] = (
        frozen_ref[...].astype(F32) + 0.5 * dot(back_out, out_down_ref[...], TN)
    ).astype(BF)


def attention_kernel(place_ref, doc_ref, low_ref, q_ref, grad_ref, back_out_ref, query_up_ref, up_ref,
                     out_down_ref, *rest):
    blocks = rest[:SPAN]
    parts_ref, back_query_ref, low_out_ref, query_term_ref, keyval_term_ref, out_term_ref = rest[
        SPAN : SPAN + 6
    ]
    bias, keys, values, low_keys, low_values, back_parts = rest[SPAN + 6 :]
    position, column = place_ref[0], place_ref[1]
    own = jnp.transpose(jnp.broadcast_to(doc_ref[...].astype(F32), (ROWS, ROWS)))
    row = lax.broadcasted_iota(jnp.int32, (ROWS, ROWS), 0)
    col = lax.broadcasted_iota(jnp.int32, (ROWS, ROWS), 1)
    for o in range(SPAN):
        span = pl.ds(o * ROWS, ROWS)
        extra = blocks[o][pl.ds(ROWS, RANK), :]
        low_keys[:, span] = extra[:, :ROWS]
        low_values[:, span] = extra[:, ROWS : 2 * ROWS]
        document = jnp.broadcast_to(extra[:1, 2 * ROWS : 3 * ROWS].astype(F32), (ROWS, ROWS))
        seen = own == document
        if o == 0:
            seen = seen & (col <= row)
        else:
            seen = seen & (jnp.broadcast_to(position, (ROWS, ROWS)) >= o)
        bias[:, span] = jnp.where(seen, 0.0, -1e30)
    back_parts[...] = jnp.zeros_like(back_parts)
    low_zero = low_ref[pl.ds(0, RANK), :]
    back_out = back_out_ref[...]

    def one_group(g, sums):
        back_query, low_out = sums
        at = pl.ds(pl.multiple_of(g * HEAD_SIZE, HEAD_SIZE), HEAD_SIZE)
        value_at = pl.ds(pl.multiple_of(KEY_COLUMNS + g * HEAD_SIZE, HEAD_SIZE), HEAD_SIZE)
        for o in range(SPAN):
            span = pl.ds(o * ROWS, ROWS)
            keys[span, :] = blocks[o][pl.ds(0, ROWS), at]
            values[span, :] = blocks[o][pl.ds(0, ROWS), value_at]
        heads = [
            pl.ds(pl.multiple_of((g * GROUP + i) * HEAD_SIZE, HEAD_SIZE), HEAD_SIZE)
            for i in range(GROUP)
        ]
        q = jnp.concatenate([q_ref[:, h] for h in heads], axis=0)
        grad = jnp.concatenate([grad_ref[:, h] for h in heads], axis=0)
        k, v = keys[...], values[...]
        scores = dot(q, k, NT).reshape(GROUP, ROWS, SPAN * ROWS) * INVERSE + bias[...][None]
        scores = scores.reshape(GROUP * ROWS, SPAN * ROWS)
        powers = jnp.exp(scores - jnp.max(scores, axis=-1, keepdims=True))
        probs = (powers * (1.0 / jnp.sum(powers, axis=-1, keepdims=True))).astype(BF)
        attn = dot(probs, v).astype(BF)
        delta = jnp.sum(grad.astype(F32) * attn.astype(F32), axis=-1, keepdims=True)
        dprobs = dot(grad, v, NT)
        dscores = (probs.astype(F32) * ((dprobs - delta) * INVERSE)).astype(BF)
        dq = dot(dscores, k).astype(BF)
        dkeys = dot(q, dscores, TN).astype(BF)
        dvalues = dot(grad, probs, TN).astype(BF)
        back_parts[pl.ds(0, RANK), :] += dot(up_ref[0, :, at], dkeys)
        back_parts[pl.ds(RANK, RANK), :] += dot(up_ref[1, :, at], dvalues)
        keyval_term_ref[pl.ds(0, RANK), at] = dot(low_keys[...], dkeys, NT)
        keyval_term_ref[pl.ds(RANK, RANK), at] = dot(low_values[...], dvalues, NT)
        for i, h in enumerate(heads):
            mine = slice(i * ROWS, (i + 1) * ROWS)
            query_term_ref[:, h] = dot(low_zero, dq[mine])
            out_term_ref[:, h] = dot(back_out, attn[mine])
            back_query = back_query + dot(query_up_ref[:, h], dq[mine], NT)
            low_out = low_out + dot(out_down_ref[:, h], attn[mine], NT)
        return back_query, low_out

    zero = jnp.zeros((RANK, ROWS), F32)
    back_query, low_out = lax.fori_loop(0, KEY_HEADS, one_group, (zero, zero))
    back_query_ref[...] = back_query.astype(BF)
    low_out_ref[...] = low_out.astype(BF)
    for o in range(SPAN):
        parts_ref[lax.rem(column + (SPAN - o), SPAN)] = back_parts[:, pl.ds(o * ROWS, ROWS)].astype(BF)


def term_kernel(place_ref, x_ref, outgrad_ref, back_query_ref, here_ref, there_ref, low_out_ref,
                query_term_ref, keyval_term_ref, out_term_ref, kept_ref, sent_ref, both):
    core = place_ref[2]
    back_keyval = (here_ref[...] + there_ref[...].astype(F32)).astype(BF)
    back = jnp.concatenate([back_query_ref[...], back_keyval], axis=0)
    down = dot(back, x_ref[...]).astype(BF)
    up = dot(low_out_ref[...], outgrad_ref[...]).astype(BF)
    query_term = query_term_ref[...].astype(BF)
    keyval_term = keyval_term_ref[...].astype(BF)
    out_term = out_term_ref[...].astype(BF)

    def put(half, tile, value):
        both[half, tile // 3, pl.ds(tile % 3 * RANK, RANK), :] = value

    def tiles(half, first, array):
        for t in range(array.shape[1] // ROWS):
            put(half, first + t, array[:, t * ROWS : (t + 1) * ROWS])
        return first + array.shape[1] // ROWS

    first = 0
    for c in range(3):
        first = tiles(0, first, down[c * RANK : (c + 1) * RANK])
    first = tiles(1, 0, query_term)
    first = tiles(1, first, keyval_term[:RANK])
    first = tiles(1, first, keyval_term[RANK:])
    first = tiles(1, first, out_term)
    first = tiles(1, first, up)
    for t in range(first, 96):
        put(1, t, jnp.zeros((RANK, ROWS), BF))
    kept_ref[...] = both[core]
    sent_ref[...] = both[1 - core]


def unpack_kernel(place_ref, kept_ref, sent_ref, down_ref, query_ref, keyval_ref, out_down_ref, out_up_ref, both):
    core = place_ref[2]
    both[core] = kept_ref[...]
    both[1 - core] = sent_ref[...]

    def get(half, tile):
        return both[half, tile // 3, pl.ds(tile % 3 * RANK, RANK), :]

    for c in range(3):
        for t in range(WIDTH // ROWS):
            down_ref[c, :, pl.ds(t * ROWS, ROWS)] = get(0, c * (WIDTH // ROWS) + t)
    first = 0
    for ref, lead in ((query_ref, None), (keyval_ref, 0), (keyval_ref, 1), (out_down_ref, None), (out_up_ref, None)):
        count = ref.shape[-1] // ROWS
        for t in range(count):
            if lead is None:
                ref[:, pl.ds(t * ROWS, ROWS)] = get(1, first + t)
            else:
                ref[lead, :, pl.ds(t * ROWS, ROWS)] = get(1, first + t)
        first += count


VMEM = pl.BlockSpec(memory_space=pltpu.VMEM)
SMEM = pl.BlockSpec(memory_space=pltpu.SMEM)


def call(kernel, name, outs, args, scratch=(), flops=0, size=0, smem_first=False, limit=32 << 20):
    specs = [SMEM if smem_first and i == 0 else VMEM for i in range(len(args))]
    return pl.pallas_call(
        kernel,
        name=name,
        out_shape=outs,
        in_specs=specs,
        out_specs=jax.tree.map(lambda _: VMEM, outs),
        scratch_shapes=list(scratch),
        compiler_params=pltpu.CompilerParams(vmem_limit_bytes=limit),
        cost_estimate=pl.CostEstimate(flops=flops, bytes_accessed=size, transcendentals=0),
    )(*args)


def shape(dims, dtype=BF):
    return jax.ShapeDtypeStruct(dims, dtype)


def per_device(
    normed_input,
    document_index,
    frozen_query_state,
    frozen_keyvalue_weight,
    layer_output_gradient,
    frozen_output_gradient,
    adapter_down_weight,
    query_up_weight,
    keyvalue_up_weight,
    output_down_weight,
    output_up_weight,
):
    x = normed_input[0]
    outgrad = layer_output_gradient[0]
    down = adapter_down_weight.transpose(0, 2, 1).reshape(3 * RANK, WIDTH)
    out_down = output_down_weight.T
    seq = ("x", "y")
    length = lax.axis_size("x") * lax.axis_size("y")
    column = lax.axis_index("y")
    place = jnp.stack([lax.axis_index(seq), column, lax.axis_index("core")]).astype(jnp.int32)

    low, pack = call(
        keyval_kernel, "keyval", (shape((3 * RANK, ROWS)), shape((PACK_ROWS, 2 * KEY_COLUMNS))),
        (x, down, frozen_keyvalue_weight[0], keyvalue_up_weight, document_index),
        flops=10**8, size=2 * 10**6,
    )

    def shifted(array, by):
        return lax.ppermute(array, seq, [(i, (i + by) % length) for i in range(length)])

    blocks = {0: pack}
    for step in range(1, 5):
        blocks[step] = shifted(blocks[step - 1], 1)
        if step < 4:
            blocks[8 - step] = shifted(pack, 7) if step == 1 else shifted(blocks[9 - step], -1)

    q, grad, back_out = call(
        query_kernel, "query",
        (shape((ROWS, QUERY_COLUMNS)), shape((ROWS, QUERY_COLUMNS)), shape((RANK, ROWS))),
        (low, frozen_query_state[0], query_up_weight, outgrad, output_up_weight, frozen_output_gradient[0], out_down),
        flops=10**8, size=4 * 10**6,
    )

    window = SPAN * ROWS
    parts, back_query, low_out, query_term, keyval_term, out_term = call(
        attention_kernel, "attention",
        (
            shape((SPAN, 2 * RANK, ROWS)),
            shape((RANK, ROWS)),
            shape((RANK, ROWS)),
            shape((RANK, QUERY_COLUMNS), F32),
            shape((2 * RANK, KEY_COLUMNS), F32),
            shape((RANK, QUERY_COLUMNS), F32),
        ),
        (place, document_index, low, q, grad, back_out, query_up_weight, keyvalue_up_weight, out_down,
         *[blocks[o] for o in range(SPAN)]),
        scratch=(
            pltpu.VMEM((ROWS, window), F32),
            pltpu.VMEM((window, HEAD_SIZE), BF),
            pltpu.VMEM((window, HEAD_SIZE), BF),
            pltpu.VMEM((RANK, window), BF),
            pltpu.VMEM((RANK, window), BF),
            pltpu.VMEM((2 * RANK, window), F32),
        ),
        flops=4 * 10**9, size=4 * 10**6, smem_first=True,
    )

    parts = lax.all_to_all(parts, "y", 0, 0, tiled=False).astype(F32)
    here = (jnp.arange(SPAN) >= column)[:, None, None]
    kept_back = jnp.sum(jnp.where(here, parts, 0.0), axis=0)
    sent_back = jnp.sum(jnp.where(here, 0.0, parts), axis=0).astype(BF)
    rows_x = lax.axis_size("x")
    there = lax.ppermute(sent_back, "x", [(i, (i - 1) % rows_x) for i in range(rows_x)])

    half = (length, 3 * RANK, ROWS)
    kept, sent = call(
        term_kernel, "terms", (shape(half), shape(half)),
        (place, x, outgrad, back_query, kept_back, there, low_out, query_term, keyval_term, out_term),
        scratch=(pltpu.VMEM((2, *half), BF),),
        flops=10**8, size=4 * 10**6, smem_first=True,
    )

    swap = [(0, 1), (1, 0)]
    total = (kept.astype(F32) + lax.ppermute(sent, "core", swap).astype(F32)).astype(BF)
    total = lax.all_to_all(total, seq, 0, 0, tiled=False)
    total = jnp.sum(total.astype(F32), axis=0).astype(BF)
    depth = lax.axis_size("z")
    total = lax.all_to_all(jnp.broadcast_to(total, (depth, *total.shape)), "z", 0, 0, tiled=False)
    scale = 0.5 / (depth * lax.axis_size("core"))
    total = (jnp.sum(total.astype(F32), axis=0) * scale).astype(BF)
    total = lax.all_to_all(jnp.broadcast_to(total, half), seq, 0, 0, tiled=False)
    other = lax.ppermute(total, "core", swap)

    lora, query_up, keyval_up, output_down, output_up = call(
        unpack_kernel, "unpack",
        (
            shape((3, RANK, WIDTH)),
            shape((RANK, QUERY_COLUMNS)),
            shape((2, RANK, KEY_COLUMNS)),
            shape((RANK, QUERY_COLUMNS)),
            shape((RANK, WIDTH)),
        ),
        (place, total, other),
        scratch=(pltpu.VMEM((2, *half), BF),),
        size=2 * 10**6, smem_first=True,
    )
    return lora.transpose(0, 2, 1), query_up, keyval_up, output_down.T, output_up


def solution(mesh):
    named = Mesh(mesh.devices.reshape(8, 2, 4, 8), ("z", "core", "x", "y"))
    rep, seq = ("z", "core"), ("x", "y")
    split = P(rep, seq, None)
    placed = (split, P(rep, seq), split, split, split, split, P(), P(), P(), P(), P())
    return jax.shard_map(
        per_device, mesh=named, in_specs=placed, out_specs=(P(), P(), P(), P(), P()), check_vma=False
    )
```

time: 319 us -> 159 us (0.50)
  blocking collectives: 143 us -> 48.4 us
  matrix products: 26.3 us -> 0 us
  waiting for transfers between devices: 52.3 us -> 29.4 us
  Pallas kernels: 0 us -> 17.7 us
  local copies, waits for them, and re-layouts: 23.7 us -> 7.51 us
  other arithmetic: 11.4 us -> 0.39 us
  starting transfers between devices: 59.4 us -> 54.1 us
    psum x1 -> x0, blocking collectives: 143 us -> none  [per_device(): lax.psum((term_down, term_query_up, term_keyval_up, term_output_down, ter...]
    all_to_all x0 -> x3, blocking collectives: none -> 48.4 us  [the longest x1 17.1 us: per_device(): lax.all_to_all(jnp.broadcast_to(total, half), seq, 0, 0, tiled=False)]
    ppermute x21 -> x10, waiting for transfers between devices: 52.3 us -> 22.2 us  [the longest x7 17.1 us: shifted(): lax.ppermute(array, seq, [(i, (i + by) % length) for i in range(length)])]
    dot_general x19 -> x0, matrix products: 19.1 us -> none  [the longest x3 2.8 us: per_device(): jnp.einsum('td,tr->dr', hidden_state, piece, preferred_element_type=jnp.f...]
    pallas_call x0 -> x5, Pallas kernels: none -> 17.7 us  [call(): pl.pallas_call(kernel, name=name, out_shape=outs, in_specs=specs, out_spe...]
    convert_element_type x9 -> x2, other arithmetic: 9.41 us -> 0.13 us  [the longest x1 0.13 us: per_device(): (kept.astype(F32) + lax.ppermute(sent, 'core', swap).astype(F32)).astype(BF)]
    ppermute x21 -> x10, starting transfers between devices: 59.4 us -> 50.8 us  [the longest x7 27.1 us: shifted(): lax.ppermute(array, seq, [(i, (i + by) % length) for i in range(length)])]
    sub x1 -> x0, matrix products: 7.26 us -> none  [per_device(): exponentials = jnp.exp(scores - maxima)]
  transfers between devices with their start and end apart: 21 -> 11, of which waited for: 12 -> 9; matrix products, arithmetic and copies ran while one was open for 8% -> 0% of each run, Pallas kernels for 0% -> 1%
where the time goes in v1:
time: 159 us; the launch traced here: 158 us
  starting transfers between devices  54.1 us (34%)
  blocking collectives  48.4 us (30%)
  waiting for transfers between devices  29.4 us (18%)
  Pallas kernels  17.7 us (11%)
  local copies, waits for them, and re-layouts  7.51 us (5%)
    ppermute x7, starting transfers between devices, shifted(): lax.ppermute(array, seq, [(i, (i + by) % length) for i in range(length)])  27.1 us
    pallas_call x5, Pallas kernels, call(): pl.pallas_call(kernel, name=name, out_shape=outs, in_specs=specs, out_spe...  17.7 us
    ppermute x7, waiting for transfers between devices, shifted(): lax.ppermute(array, seq, [(i, (i + by) % length) for i in range(length)])  17.1 us
    all_to_all x1, blocking collectives, per_device(): lax.all_to_all(jnp.broadcast_to(total, half), seq, 0, 0, tiled=False)  17.1 us
    all_to_all x1, blocking collectives, per_device(): lax.all_to_all(jnp.broadcast_to(total, (depth, *total.shape)), 'z', 0, 0,...  16 us
    all_to_all x1, blocking collectives, per_device(): total = lax.all_to_all(total, seq, 0, 0, tiled=False)  15.3 us
    ppermute x1, starting transfers between devices, per_device(): lax.ppermute(sent, 'core', swap).astype(F32)  14.6 us
    unnamed x32, local copies, waits for them, and re-layouts  7.44 us
  transfers between devices with their start and end apart: 11, of which 9 were waited for; matrix products, arithmetic and copies ran while one was open for 0% of the time, Pallas kernels for 1%

profile of v1, /device:TPU:1, one launch (start us, length us, event | category | flops | bytes accessed | tf_op | source)
XLA Modules:
  0.0 158.3 jit_solution(824902940832092212)
XLA Ops:
  1.3 1.2 copy-done
  2.5 1.0 copy-done.5
  3.5 0.9 copy-done.6
  6.1 4.0 %collective-permute-start = (bf16[144,1024]{1,0:T(8,128)(2,1)S(1)}, bf16[144,1024]{1,0:T(8,128)(2,1)S(1)}, u32[]{:S(2)}, u32[]{:S(2)}) collective-permute-start(bf16[144,1024]{1,0:T(8,128)(2,1)S(1)} %get-tuple-element.27.rest_0_), channel_id=1, source_target_pairs={{0,1},{1,2},{2,3},{3,4},{4,5},{5,6},{6,7},{7,8},{8,9},{9,10},{10,1... | collective-permute-start | bytes 884744 | tf_op jit(solution)/shard_map/ppermute | solution.py:238
  10.1 4.2 %collective-permute-start.4 = (bf16[144,1024]{1,0:T(8,128)(2,1)S(1)}, bf16[144,1024]{1,0:T(8,128)(2,1)S(1)}, u32[]{:S(2)}, u32[]{:S(2)}) collective-permute-start(bf16[144,1024]{1,0:T(8,128)(2,1)S(1)} %get-tuple-element.27.rest_0_), channel_id=1, source_target_pairs={{0,7},{1,8},{2,9},{3,10},{4,11},{5,12},{6,13},{7,14},{8,15},{9,16}... | collective-permute-start | bytes 884744 | tf_op jit(solution)/shard_map/ppermute | solution.py:238
  14.3 5.3 %collective-permute-done.rest_1_ = bf16[144,1024]{1,0:T(8,128)(2,1)S(1)} collective-permute-done((bf16[144,1024]{1,0:T(8,128)(2,1)S(1)}, bf16[144,1024]{1,0:T(8,128)(2,1)S(1)}, u32[]{:S(2)}, u32[]{:S(2)}) %collective-permute-start) | collective-permute-done | bytes 294944 | tf_op jit(solution)/shard_map/ppermute | solution.py:238
  19.7 1.9 %collective-permute-start.1 = (bf16[144,1024]{1,0:T(8,128)(2,1)S(1)}, bf16[144,1024]{1,0:T(8,128)(2,1)S(1)}, u32[]{:S(2)}, u32[]{:S(2)}) collective-permute-start(bf16[144,1024]{1,0:T(8,128)(2,1)S(1)} %collective-permute-done.rest_1_), channel_id=1, source_target_pairs={{0,1},{1,2},{2,3},{3,4},{4,5},{5,6},{6,7},{7,8},{8,9},{9,10},{10,1... | collective-permute-start | bytes 884744 | tf_op jit(solution)/shard_map/ppermute | solution.py:238
  21.8 6.5 %collective-permute-start.5 = (bf16[144,1024]{1,0:T(8,128)(2,1)S(1)}, bf16[144,1024]{1,0:T(8,128)(2,1)}, u32[]{:S(2)}, u32[]{:S(2)}) collective-permute-start(bf16[144,1024]{1,0:T(8,128)(2,1)S(1)} %collective-permute-done.4.rest_7_), channel_id=1, source_target_pairs={{0,31},{1,0},{2,1},{3,2},{4,3},{5,4},{6,5},{7,6},{8,7},{9,8},{10,9... | collective-permute-start | bytes 884744 | tf_op jit(solution)/shard_map/ppermute | solution.py:238
  28.3 2.6 %collective-permute-done.1.rest_2_ = bf16[144,1024]{1,0:T(8,128)(2,1)S(1)} collective-permute-done((bf16[144,1024]{1,0:T(8,128)(2,1)S(1)}, bf16[144,1024]{1,0:T(8,128)(2,1)S(1)}, u32[]{:S(2)}, u32[]{:S(2)}) %collective-permute-start.1) | collective-permute-done | bytes 294944 | tf_op jit(solution)/shard_map/ppermute | solution.py:238
  30.9 1.9 %collective-permute-start.2 = (bf16[144,1024]{1,0:T(8,128)(2,1)S(1)}, bf16[144,1024]{1,0:T(8,128)(2,1)}, u32[]{:S(2)}, u32[]{:S(2)}) collective-permute-start(bf16[144,1024]{1,0:T(8,128)(2,1)S(1)} %collective-permute-done.1.rest_2_), channel_id=1, source_target_pairs={{0,1},{1,2},{2,3},{3,4},{4,5},{5,6},{6,7},{7,8},{8,9},{9,10},{10,1... | collective-permute-start | bytes 884744 | tf_op jit(solution)/shard_map/ppermute | solution.py:238
  32.8 6.7 %collective-permute-start.6 = (bf16[144,1024]{1,0:T(8,128)(2,1)}, bf16[144,1024]{1,0:T(8,128)(2,1)}, u32[]{:S(2)}, u32[]{:S(2)}) collective-permute-start(bf16[144,1024]{1,0:T(8,128)(2,1)} %collective-permute-done.5.rest_6_), channel_id=1, source_target_pairs={{0,31},{1,0},{2,1},{3,2},{4,3},{5,4},{6,5},{7,6},{8,7},{9,8},{10,9... | collective-permute-start | bytes 884744 | tf_op jit(solution)/shard_map/ppermute | solution.py:238
  39.5 2.3 %collective-permute-done.2.rest_3_ = bf16[144,1024]{1,0:T(8,128)(2,1)} collective-permute-done((bf16[144,1024]{1,0:T(8,128)(2,1)S(1)}, bf16[144,1024]{1,0:T(8,128)(2,1)}, u32[]{:S(2)}, u32[]{:S(2)}) %collective-permute-start.2) | collective-permute-done | bytes 294944 | tf_op jit(solution)/shard_map/ppermute | solution.py:238
  41.8 1.9 %collective-permute-start.3 = (bf16[144,1024]{1,0:T(8,128)(2,1)}, bf16[144,1024]{1,0:T(8,128)(2,1)}, u32[]{:S(2)}, u32[]{:S(2)}) collective-permute-start(bf16[144,1024]{1,0:T(8,128)(2,1)} %collective-permute-done.2.rest_3_), channel_id=1, source_target_pairs={{0,1},{1,2},{2,3},{3,4},{4,5},{5,6},{6,7},{7,8},{8,9},{9,10},{10,1... | collective-permute-start | bytes 884744 | tf_op jit(solution)/shard_map/ppermute | solution.py:238
  43.8 1.0 copy-done.4
  44.8 0.8 copy-done.9
  45.7 1.1 query.1
  46.9 6.7 %collective-permute-done.3.rest_4_ = bf16[144,1024]{1,0:T(8,128)(2,1)} collective-permute-done((bf16[144,1024]{1,0:T(8,128)(2,1)}, bf16[144,1024]{1,0:T(8,128)(2,1)}, u32[]{:S(2)}, u32[]{:S(2)}) %collective-permute-start.3) | collective-permute-done | bytes 294944 | tf_op jit(solution)/shard_map/ppermute | solution.py:238
  53.6 1.0 copy-done.15
  54.5 13.2 %attention.1 = (bf16[8,32,128]{2,1,0:T(8,128)(2,1)}, bf16[16,128]{1,0:T(8,128)(2,1)S(1)}, bf16[16,128]{1,0:T(8,128)(2,1)S(1)}, f32[16,2048]{1,0:T(8,128)S(1)}, f...) custom-call(s32[3]{0:T(128)S(1)} %pad_add_fusion.place_ref, s32[1,128]{1,0:T(1,128)S(1)} %copy-done.13, ...), custom_call_target="tpu_custom_call" | custom-call | flops 4000000000 | bytes 4000000 | tf_op jit(solution)/shard_map/attention/pallas_call | solution.py:193
  67.7 3.4 %all-to-all-start = ((bf16[8,32,128]{2,1,0:T(8,128)(2,1)}), bf16[8,32,128]{2,1,0:T(8,128)(2,1)S(1)}, u32[]{:S(2)}, u32[]{:S(2)}) async-start(bf16[8,32,128]{2,1,0:T(8,128)(2,1)} %get-tuple-element.29), calls=%async_computation | async-start | bytes 131072 | tf_op jit(solution)/shard_map/all_to_all | solution.py:277
  71.1 7.1 %all-to-all-done = bf16[8,32,128]{2,1,0:T(8,128)(2,1)S(1)} async-done(((bf16[8,32,128]{2,1,0:T(8,128)(2,1)}), bf16[8,32,128]{2,1,0:T(8,128)(2,1)S(1)}, u32[]{:S(2)}, u32[]{:S(2)}) %all-to-all-start) | async-done | bytes 65568 | tf_op jit(solution)/shard_map/all_to_all | solution.py:277
  78.3 1.9 %collective-permute-start.7 = (bf16[32,128]{1,0:T(8,128)(2,1)S(1)}, bf16[32,128]{1,0:T(8,128)(2,1)S(1)}, u32[]{:S(2)}, u32[]{:S(2)}) collective-permute-start(bf16[32,128]{1,0:T(8,128)(2,1)S(1)} %get-tuple-element.41), channel_id=1, source_target_pairs={{0,24},{8,0},{16,8},{24,16},{1,25},{9,1},{17,9},{25,17},{2,26},{10... | collective-permute-start | bytes 24584 | tf_op jit(solution)/shard_map/ppermute | solution.py:282
  80.2 2.5 %collective-permute-done.7.there_ref = bf16[32,128]{1,0:T(8,128)(2,1)S(1)} collective-permute-done((bf16[32,128]{1,0:T(8,128)(2,1)S(1)}, bf16[32,128]{1,0:T(8,128)(2,1)S(1)}, u32[]{:S(2)}, u32[]{:S(2)}) %collective-permute-start.7) | collective-permute-done | bytes 8224 | tf_op jit(solution)/shard_map/ppermute | solution.py:282
  82.7 1.0 terms.1
  83.7 14.6 %collective-permute-start.8 = (bf16[32,48,128]{2,1,0:T(8,128)(2,1)S(1)}, bf16[32,48,128]{2,1,0:T(8,128)(2,1)S(1)}, u32[]{:S(2)}, u32[]{:S(2)}) collective-permute-start(bf16[32,48,128]{2,1,0:T(8,128)(2,1)S(1)} %get-tuple-element.35), channel_id=1, source_target_pairs={{0,32},{32,0},{1,33},{33,1},{2,34},{34,2},{3,35},{35,3},{4,36},{36... | collective-permute-start | bytes 1179656 | tf_op jit(solution)/shard_map/ppermute | solution.py:293
  98.3 1.3 collective-permute-done.8
  99.8 15.3 %all_to_all.20 = bf16[32,48,128]{2,1,0:T(8,128)(2,1)S(1)} all-to-all(bf16[32,48,128]{2,1,0:T(8,128)(2,1)S(1)} %add_convert_fusion), channel_id=1, replica_groups=mesh['z'=8,'core'=2,'x'=4,'y'=8] {'x','y'}, dimensions={0} | all-to-all | bytes 786432 | tf_op jit(solution)/shard_map/all_to_all | solution.py:294
  115.1 16.0 %all_to_all.21 = bf16[8,48,128]{2,1,0:T(8,128)(2,1)S(1)} all-to-all(bf16[8,48,128]{2,1,0:T(8,128)(2,1)S(1)} %broadcast_in_dim.29), channel_id=1, replica_groups=mesh['z'=8,'core'=2,'x'=4,'y'=8] {'z'}, dimensions={0} | all-to-all | bytes 196608 | tf_op jit(solution)/shard_map/all_to_all | solution.py:297
  131.3 17.1 %all_to_all.22.kept_ref = bf16[32,48,128]{2,1,0:T(8,128)(2,1)S(1)} all-to-all(bf16[32,48,128]{2,1,0:T(8,128)(2,1)S(1)} %broadcast_in_dim.30), channel_id=1, replica_groups=mesh['z'=8,'core'=2,'x'=4,'y'=8] {'x','y'}, dimensions={0} | all-to-all | bytes 786432 | tf_op jit(solution)/shard_map/all_to_all | solution.py:300
  148.4 7.2 %collective-permute-start.9 = (bf16[32,48,128]{2,1,0:T(8,128)(2,1)S(1)}, bf16[32,48,128]{2,1,0:T(8,128)(2,1)S(1)}, u32[]{:S(2)}, u32[]{:S(2)}) collective-permute-start(bf16[32,48,128]{2,1,0:T(8,128)(2,1)S(1)} %all_to_all.22.kept_ref), channel_id=1, source_target_pairs={{0,32},{32,0},{1,33},{33,1},{2,34},{34,2},{3,35},{35,3},{4,36},{36... | collective-permute-start | bytes 1179656 | tf_op jit(solution)/shard_map/ppermute | solution.py:301
  155.5 1.3 collective-permute-done.9.sent_ref
  156.8 1.5 unpack.1
  (39 shorter events, 2.9 us)
Async XLA Ops:
  0.6 0.7 copy-start.13
  1.3 1.2 copy-start
  2.5 1.0 copy-start.5
  3.5 0.9 copy-start.6
  4.5 0.8 copy-start.11
  5.2 38.5 %copy-start.2 = (bf16[1,128,4096]{2,1,0:T(8,128)(2,1)S(1)}, bf16[1,128,4096]{2,1,0:T(8,128)(2,1)}, u32[]{:S(2)}) copy-start(bf16[1,128,4096]{2,1,0:T(8,128)(2,1)} %param.15) | copy-start | bytes 3145732
  5.2 38.5 %copy-start.3 = (bf16[1,128,2048]{2,1,0:T(8,128)(2,1)S(1)}, bf16[1,128,2048]{2,1,0:T(8,128)(2,1)}, u32[]{:S(2)}) copy-start(bf16[1,128,2048]{2,1,0:T(8,128)(2,1)} %param.13) | copy-start | bytes 1572868
  5.2 38.5 %copy-start.7 = (bf16[16,4096]{1,0:T(8,128)(2,1)S(1)}, bf16[16,4096]{1,0:T(8,128)(2,1)}, u32[]{:S(2)}) copy-start(bf16[16,4096]{1,0:T(8,128)(2,1)} %out_up_ref.1) | copy-start | bytes 393220
  5.2 38.5 %copy-start.8 = (bf16[16,2048]{1,0:T(8,128)(2,1)S(1)}, bf16[16,2048]{1,0:T(8,128)(2,1)}, u32[]{:S(2)}) copy-start(bf16[16,2048]{1,0:T(8,128)(2,1)} %query_up_ref.3) | copy-start | bytes 196612
  6.1 13.6 %collective-permute-start = (bf16[144,1024]{1,0:T(8,128)(2,1)S(1)}, bf16[144,1024]{1,0:T(8,128)(2,1)S(1)}, u32[]{:S(2)}, u32[]{:S(2)}) collective-permute-start(bf16[144,1024]{1,0:T(8,128)(2,1)S(1)} %get-tuple-element.27.rest_0_), channel_id=1, source_target_pairs={{0,1},{1,2},{2,3},{3,4},{4,5},{5,6},{6,7},{7,8},{8,9},{9,10},{10,1... | collective-permute-start | bytes 884744 | tf_op jit(solution)/shard_map/ppermute | solution.py:238
  10.1 11.7 %collective-permute-start.4 = (bf16[144,1024]{1,0:T(8,128)(2,1)S(1)}, bf16[144,1024]{1,0:T(8,128)(2,1)S(1)}, u32[]{:S(2)}, u32[]{:S(2)}) collective-permute-start(bf16[144,1024]{1,0:T(8,128)(2,1)S(1)} %get-tuple-element.27.rest_0_), channel_id=1, source_target_pairs={{0,7},{1,8},{2,9},{3,10},{4,11},{5,12},{6,13},{7,14},{8,15},{9,16}... | collective-permute-start | bytes 884744 | tf_op jit(solution)/shard_map/ppermute | solution.py:238
  19.7 11.3 %collective-permute-start.1 = (bf16[144,1024]{1,0:T(8,128)(2,1)S(1)}, bf16[144,1024]{1,0:T(8,128)(2,1)S(1)}, u32[]{:S(2)}, u32[]{:S(2)}) collective-permute-start(bf16[144,1024]{1,0:T(8,128)(2,1)S(1)} %collective-permute-done.rest_1_), channel_id=1, source_target_pairs={{0,1},{1,2},{2,3},{3,4},{4,5},{5,6},{6,7},{7,8},{8,9},{9,10},{10,1... | collective-permute-start | bytes 884744 | tf_op jit(solution)/shard_map/ppermute | solution.py:238
  21.8 11.0 %collective-permute-start.5 = (bf16[144,1024]{1,0:T(8,128)(2,1)S(1)}, bf16[144,1024]{1,0:T(8,128)(2,1)}, u32[]{:S(2)}, u32[]{:S(2)}) collective-permute-start(bf16[144,1024]{1,0:T(8,128)(2,1)S(1)} %collective-permute-done.4.rest_7_), channel_id=1, source_target_pairs={{0,31},{1,0},{2,1},{3,2},{4,3},{5,4},{6,5},{7,6},{8,7},{9,8},{10,9... | collective-permute-start | bytes 884744 | tf_op jit(solution)/shard_map/ppermute | solution.py:238
  30.9 15.9 %copy-start.14 = (bf16[144,1024]{1,0:T(8,128)(2,1)}, bf16[144,1024]{1,0:T(8,128)(2,1)S(1)}, u32[]{:S(2)}) copy-start(bf16[144,1024]{1,0:T(8,128)(2,1)S(1)} %collective-permute-done.1.rest_2_) | copy-start | bytes 884740
  30.9 10.9 %collective-permute-start.2 = (bf16[144,1024]{1,0:T(8,128)(2,1)S(1)}, bf16[144,1024]{1,0:T(8,128)(2,1)}, u32[]{:S(2)}, u32[]{:S(2)}) collective-permute-start(bf16[144,1024]{1,0:T(8,128)(2,1)S(1)} %collective-permute-done.1.rest_2_), channel_id=1, source_target_pairs={{0,1},{1,2},{2,3},{3,4},{4,5},{5,6},{6,7},{7,8},{8,9},{9,10},{10,1... | collective-permute-start | bytes 884744 | tf_op jit(solution)/shard_map/ppermute | solution.py:238
  32.8 14.0 %collective-permute-start.6 = (bf16[144,1024]{1,0:T(8,128)(2,1)}, bf16[144,1024]{1,0:T(8,128)(2,1)}, u32[]{:S(2)}, u32[]{:S(2)}) collective-permute-start(bf16[144,1024]{1,0:T(8,128)(2,1)} %collective-permute-done.5.rest_6_), channel_id=1, source_target_pairs={{0,31},{1,0},{2,1},{3,2},{4,3},{5,4},{6,5},{7,6},{8,7},{9,8},{10,9... | collective-permute-start | bytes 884744 | tf_op jit(solution)/shard_map/ppermute | solution.py:238
  41.8 11.7 %collective-permute-start.3 = (bf16[144,1024]{1,0:T(8,128)(2,1)}, bf16[144,1024]{1,0:T(8,128)(2,1)}, u32[]{:S(2)}, u32[]{:S(2)}) collective-permute-start(bf16[144,1024]{1,0:T(8,128)(2,1)} %collective-permute-done.2.rest_3_), channel_id=1, source_target_pairs={{0,1},{1,2},{2,3},{3,4},{4,5},{5,6},{6,7},{7,8},{8,9},{9,10},{10,1... | collective-permute-start | bytes 884744 | tf_op jit(solution)/shard_map/ppermute | solution.py:238
  43.8 1.0 copy-start.4
  44.8 0.8 copy-start.9
  45.7 7.9 %copy-start.10 = (bf16[2048,16]{0,1:T(8,128)(2,1)S(1)}, bf16[2048,16]{0,1:T(8,128)(2,1)}, u32[]{:S(2)}) copy-start(bf16[2048,16]{0,1:T(8,128)(2,1)} %param.20) | copy-start | bytes 196612
  45.7 7.9 %copy-start.12 = (bf16[2,16,512]{2,1,0:T(8,128)(2,1)S(1)}, bf16[2,16,512]{2,1,0:T(8,128)(2,1)}, u32[]{:S(2)}) copy-start(bf16[2,16,512]{2,1,0:T(8,128)(2,1)} %up_ref.3) | copy-start | bytes 98308
  53.6 1.0 copy-start.15
  54.5 28.2 %copy-start.1 = (bf16[1,128,4096]{2,1,0:T(8,128)(2,1)S(1)}, bf16[1,128,4096]{2,1,0:T(8,128)(2,1)}, u32[]{:S(2)}) copy-start(bf16[1,128,4096]{2,1,0:T(8,128)(2,1)} %param.11) | copy-start | bytes 3145732
  67.7 10.5 %all-to-all-start = ((bf16[8,32,128]{2,1,0:T(8,128)(2,1)}), bf16[8,32,128]{2,1,0:T(8,128)(2,1)S(1)}, u32[]{:S(2)}, u32[]{:S(2)}) async-start(bf16[8,32,128]{2,1,0:T(8,128)(2,1)} %get-tuple-element.29), calls=%async_computation | async-start | bytes 131072 | tf_op jit(solution)/shard_map/all_to_all | solution.py:277
  78.3 4.4 %collective-permute-start.7 = (bf16[32,128]{1,0:T(8,128)(2,1)S(1)}, bf16[32,128]{1,0:T(8,128)(2,1)S(1)}, u32[]{:S(2)}, u32[]{:S(2)}) collective-permute-start(bf16[32,128]{1,0:T(8,128)(2,1)S(1)} %get-tuple-element.41), channel_id=1, source_target_pairs={{0,24},{8,0},{16,8},{24,16},{1,25},{9,1},{17,9},{25,17},{2,26},{10... | collective-permute-start | bytes 24584 | tf_op jit(solution)/shard_map/ppermute | solution.py:282
  83.7 15.9 %collective-permute-start.8 = (bf16[32,48,128]{2,1,0:T(8,128)(2,1)S(1)}, bf16[32,48,128]{2,1,0:T(8,128)(2,1)S(1)}, u32[]{:S(2)}, u32[]{:S(2)}) collective-permute-start(bf16[32,48,128]{2,1,0:T(8,128)(2,1)S(1)} %get-tuple-element.35), channel_id=1, source_target_pairs={{0,32},{32,0},{1,33},{33,1},{2,34},{34,2},{3,35},{35,3},{4,36},{36... | collective-permute-start | bytes 1179656 | tf_op jit(solution)/shard_map/ppermute | solution.py:293
  148.4 8.5 %collective-permute-start.9 = (bf16[32,48,128]{2,1,0:T(8,128)(2,1)S(1)}, bf16[32,48,128]{2,1,0:T(8,128)(2,1)S(1)}, u32[]{:S(2)}, u32[]{:S(2)}) collective-permute-start(bf16[32,48,128]{2,1,0:T(8,128)(2,1)S(1)} %all_to_all.22.kept_ref), channel_id=1, source_target_pairs={{0,32},{32,0},{1,33},{33,1},{2,34},{34,2},{3,35},{35,3},{4,36},{36... | collective-permute-start | bytes 1179656 | tf_op jit(solution)/shard_map/ppermute | solution.py:301

commit v2 on v1

--- a/solution.py
+++ b/solution.py
@@ -19,6 +19,8 @@
 BF = jnp.bfloat16
 F32 = jnp.float32
 INVERSE = 1.0 / HEAD_SIZE**0.5
+LOG2E = 1.4426950408889634
+DEVICES = 32
 
 NT = (((1,), (1,)), ((), ()))
 TN = (((0,), (0,)), ((), ()))
@@ -29,9 +31,18 @@
     return lax.dot_general(a, b, dims, preferred_element_type=F32)
 
 
-def keyval_kernel(x_ref, down_ref, keyval_ref, up_ref, doc_ref, low_ref, pack_ref):
+def keyval_kernel(x_any, down_any, keyval_any, up_any, doc_any, low_ref, pack_ref,
+                  x_ref, down_ref, keyval_ref, up_ref, doc_ref, sems):
+    pairs = ((x_any, x_ref), (down_any, down_ref), (keyval_any, keyval_ref), (up_any, up_ref), (doc_any, doc_ref))
+    copies = [pltpu.make_async_copy(a, b, sems.at[i]) for i, (a, b) in enumerate(pairs)]
+    for copy in copies:
+        copy.start()
+    copies[0].wait()
+    copies[1].wait()
     low = dot(down_ref[...], x_ref[...], NT).astype(BF)
     low_ref[...] = low
+    for copy in copies[2:]:
+        copy.wait()
     for c in range(2):
         part = pl.ds(c * KEY_COLUMNS, KEY_COLUMNS)
         delta = dot(low[(c + 1) * RANK : (c + 2) * RANK], up_ref[c], TN)
@@ -59,12 +70,10 @@
 def attention_kernel(place_ref, doc_ref, low_ref, q_ref, grad_ref, back_out_ref, query_up_ref, up_ref,
                      out_down_ref, *rest):
     blocks = rest[:SPAN]
-    parts_ref, back_query_ref, low_out_ref, query_term_ref, keyval_term_ref, out_term_ref = rest[
-        SPAN : SPAN + 6
-    ]
+    parts_ref, back_query_ref, low_out_ref, query_term_ref, keyval_term_ref, out_term_ref = rest[SPAN : SPAN + 6]
     bias, keys, values, low_keys, low_values, back_parts = rest[SPAN + 6 :]
-    position, column = place_ref[0], place_ref[1]
-    own = jnp.transpose(jnp.broadcast_to(doc_ref[...].astype(F32), (ROWS, ROWS)))
+    position = place_ref[0]
+    own = jnp.broadcast_to(doc_ref[...].astype(F32), (ROWS, ROWS))
     row = lax.broadcasted_iota(jnp.int32, (ROWS, ROWS), 0)
     col = lax.broadcasted_iota(jnp.int32, (ROWS, ROWS), 1)
     for o in range(SPAN):
@@ -72,13 +81,15 @@
         extra = blocks[o][pl.ds(ROWS, RANK), :]
         low_keys[:, span] = extra[:, :ROWS]
         low_values[:, span] = extra[:, ROWS : 2 * ROWS]
-        document = jnp.broadcast_to(extra[:1, 2 * ROWS : 3 * ROWS].astype(F32), (ROWS, ROWS))
+        document = jnp.transpose(jnp.broadcast_to(extra[:1, 2 * ROWS : 3 * ROWS].astype(F32), (ROWS, ROWS)))
         seen = own == document
         if o == 0:
-            seen = seen & (col <= row)
+            seen = seen & (row <= col)
         else:
             seen = seen & (jnp.broadcast_to(position, (ROWS, ROWS)) >= o)
-        bias[:, span] = jnp.where(seen, 0.0, -1e30)
+        one = jnp.where(seen, 0.0, -1e30)
+        for i in range(GROUP):
+            bias[span, pl.ds(i*ROWS, ROWS)] = one
     back_parts[...] = jnp.zeros_like(back_parts)
     low_zero = low_ref[pl.ds(0, RANK), :]
     back_out = back_out_ref[...]
@@ -91,48 +102,53 @@
             span = pl.ds(o * ROWS, ROWS)
             keys[span, :] = blocks[o][pl.ds(0, ROWS), at]
             values[span, :] = blocks[o][pl.ds(0, ROWS), value_at]
-        heads = [
-            pl.ds(pl.multiple_of((g * GROUP + i) * HEAD_SIZE, HEAD_SIZE), HEAD_SIZE)
-            for i in range(GROUP)
-        ]
+        heads = [pl.ds(pl.multiple_of((g * GROUP + i) * HEAD_SIZE, HEAD_SIZE), HEAD_SIZE) for i in range(GROUP)]
         q = jnp.concatenate([q_ref[:, h] for h in heads], axis=0)
         grad = jnp.concatenate([grad_ref[:, h] for h in heads], axis=0)
+        qT = jnp.transpose(q.astype(F32))
+        gradT = jnp.transpose(grad.astype(F32))
         k, v = keys[...], values[...]
-        scores = dot(q, k, NT).reshape(GROUP, ROWS, SPAN * ROWS) * INVERSE + bias[...][None]
-        scores = scores.reshape(GROUP * ROWS, SPAN * ROWS)
-        powers = jnp.exp(scores - jnp.max(scores, axis=-1, keepdims=True))
-        probs = (powers * (1.0 / jnp.sum(powers, axis=-1, keepdims=True))).astype(BF)
-        attn = dot(probs, v).astype(BF)
-        delta = jnp.sum(grad.astype(F32) * attn.astype(F32), axis=-1, keepdims=True)
-        dprobs = dot(grad, v, NT)
-        dscores = (probs.astype(F32) * ((dprobs - delta) * INVERSE)).astype(BF)
-        dq = dot(dscores, k).astype(BF)
-        dkeys = dot(q, dscores, TN).astype(BF)
-        dvalues = dot(grad, probs, TN).astype(BF)
-        back_parts[pl.ds(0, RANK), :] += dot(up_ref[0, :, at], dkeys)
-        back_parts[pl.ds(RANK, RANK), :] += dot(up_ref[1, :, at], dvalues)
-        keyval_term_ref[pl.ds(0, RANK), at] = dot(low_keys[...], dkeys, NT)
-        keyval_term_ref[pl.ds(RANK, RANK), at] = dot(low_values[...], dvalues, NT)
+        scores = dot(k, qT.astype(BF)) * (INVERSE * LOG2E) + bias[...]
+        powers = jnp.exp2(scores - jnp.max(scores, axis=0, keepdims=True))
+        recip = 1.0 / jnp.sum(powers, axis=0, keepdims=True)
+        powers = powers.astype(BF)
+        attn = (dot(v, powers, TN) * recip).astype(BF)
+        delta = jnp.sum(gradT * attn.astype(F32), axis=0, keepdims=True)
+        dprobs = dot(v, gradT.astype(BF))
+        dscores = powers * (dprobs - delta).astype(BF)
+        dq = (dot(k, dscores, TN) * (recip * INVERSE)).astype(BF)
+        scaled_q = jnp.transpose(qT * (recip * INVERSE)).astype(BF)
+        scaled_grad = jnp.transpose(gradT * recip).astype(BF)
+        dkeys = dot(dscores, scaled_q).astype(BF)
+        dvalues = dot(powers, scaled_grad).astype(BF)
+        back_parts[pl.ds(0, RANK), :] += dot(up_ref[0, :, at], dkeys, NT)
+        back_parts[pl.ds(RANK, RANK), :] += dot(up_ref[1, :, at], dvalues, NT)
+        keyval_term_ref[pl.ds(0, RANK), at] = dot(low_keys[...], dkeys)
+        keyval_term_ref[pl.ds(RANK, RANK), at] = dot(low_values[...], dvalues)
         for i, h in enumerate(heads):
             mine = slice(i * ROWS, (i + 1) * ROWS)
-            query_term_ref[:, h] = dot(low_zero, dq[mine])
-            out_term_ref[:, h] = dot(back_out, attn[mine])
-            back_query = back_query + dot(query_up_ref[:, h], dq[mine], NT)
-            low_out = low_out + dot(out_down_ref[:, h], attn[mine], NT)
+            query_term_ref[:, h] = dot(low_zero, dq[:, mine], NT)
+            out_term_ref[:, h] = dot(back_out, attn[:, mine], NT)
+            back_query = back_query + dot(query_up_ref[:, h], dq[:, mine])
+            low_out = low_out + dot(out_down_ref[:, h], attn[:, mine])
         return back_query, low_out
 
     zero = jnp.zeros((RANK, ROWS), F32)
-    back_query, low_out = lax.fori_loop(0, KEY_HEADS, one_group, (zero, zero))
+    back_query, low_out = lax.fori_loop(0, KEY_HEADS, one_group, (zero, zero), unroll=True)
     back_query_ref[...] = back_query.astype(BF)
     low_out_ref[...] = low_out.astype(BF)
+    parts_ref[...] = jnp.zeros_like(parts_ref)
     for o in range(SPAN):
-        parts_ref[lax.rem(column + (SPAN - o), SPAN)] = back_parts[:, pl.ds(o * ROWS, ROWS)].astype(BF)
-
-
-def term_kernel(place_ref, x_ref, outgrad_ref, back_query_ref, here_ref, there_ref, low_out_ref,
+        parts_ref[lax.rem(position + (DEVICES - o), DEVICES)] = back_parts[:, pl.ds(o * ROWS, ROWS)].astype(BF)
+
+
+def term_kernel(place_ref, x_ref, outgrad_ref, back_query_ref, parts_ref, low_out_ref,
                 query_term_ref, keyval_term_ref, out_term_ref, kept_ref, sent_ref, both):
-    core = place_ref[2]
-    back_keyval = (here_ref[...] + there_ref[...].astype(F32)).astype(BF)
+    core = place_ref[1]
+    back_keyval = parts_ref[0].astype(F32)
+    for i in range(1, DEVICES):
+        back_keyval = back_keyval + parts_ref[i].astype(F32)
+    back_keyval = back_keyval.astype(BF)
     back = jnp.concatenate([back_query_ref[...], back_keyval], axis=0)
     down = dot(back, x_ref[...]).astype(BF)
     up = dot(low_out_ref[...], outgrad_ref[...]).astype(BF)
@@ -163,7 +179,7 @@
 
 
 def unpack_kernel(place_ref, kept_ref, sent_ref, down_ref, query_ref, keyval_ref, out_down_ref, out_up_ref, both):
-    core = place_ref[2]
+    core = place_ref[1]
     both[core] = kept_ref[...]
     both[1 - core] = sent_ref[...]
 
@@ -188,8 +204,8 @@
 SMEM = pl.BlockSpec(memory_space=pltpu.SMEM)
 
 
-def call(kernel, name, outs, args, scratch=(), flops=0, size=0, smem_first=False, limit=32 << 20):
-    specs = [SMEM if smem_first and i == 0 else VMEM for i in range(len(args))]
+def call(kernel, name, outs, args, scratch=(), flops=0, size=0, smem_first=False, limit=32 << 20, kind=None):
+    specs = [SMEM if smem_first and i == 0 else (kind or VMEM) for i in range(len(args))]
     return pl.pallas_call(
         kernel,
         name=name,
@@ -225,23 +241,30 @@
     out_down = output_down_weight.T
     seq = ("x", "y")
     length = lax.axis_size("x") * lax.axis_size("y")
-    column = lax.axis_index("y")
-    place = jnp.stack([lax.axis_index(seq), column, lax.axis_index("core")]).astype(jnp.int32)
+    place = jnp.stack([lax.axis_index(seq), lax.axis_index("core")]).astype(jnp.int32)
 
     low, pack = call(
         keyval_kernel, "keyval", (shape((3 * RANK, ROWS)), shape((PACK_ROWS, 2 * KEY_COLUMNS))),
         (x, down, frozen_keyvalue_weight[0], keyvalue_up_weight, document_index),
-        flops=10**8, size=2 * 10**6,
+        scratch=(
+            pltpu.VMEM((ROWS, WIDTH), BF),
+            pltpu.VMEM((3 * RANK, WIDTH), BF),
+            pltpu.VMEM((ROWS, 2 * KEY_COLUMNS), BF),
+            pltpu.VMEM((2, RANK, KEY_COLUMNS), BF),
+            pltpu.VMEM((1, ROWS), jnp.int32),
+            pltpu.SemaphoreType.DMA((5,)),
+        ),
+        flops=10**8, size=2 * 10**6, limit=56 << 20, kind=pl.BlockSpec(memory_space=pl.ANY),
     )
 
     def shifted(array, by):
         return lax.ppermute(array, seq, [(i, (i + by) % length) for i in range(length)])
 
     blocks = {0: pack}
-    for step in range(1, 5):
+    for step in range(1, 4):
         blocks[step] = shifted(blocks[step - 1], 1)
-        if step < 4:
-            blocks[8 - step] = shifted(pack, 7) if step == 1 else shifted(blocks[9 - step], -1)
+        blocks[8 - step] = shifted(pack, 7) if step == 1 else shifted(blocks[9 - step], -1)
+    blocks[4] = shifted(blocks[2], 2)
 
     q, grad, back_out = call(
         query_kernel, "query",
@@ -254,7 +277,7 @@
     parts, back_query, low_out, query_term, keyval_term, out_term = call(
         attention_kernel, "attention",
         (
-            shape((SPAN, 2 * RANK, ROWS)),
+            shape((DEVICES, 2 * RANK, ROWS)),
             shape((RANK, ROWS)),
             shape((RANK, ROWS)),
             shape((RANK, QUERY_COLUMNS), F32),
@@ -264,7 +287,7 @@
         (place, document_index, low, q, grad, back_out, query_up_weight, keyvalue_up_weight, out_down,
          *[blocks[o] for o in range(SPAN)]),
         scratch=(
-            pltpu.VMEM((ROWS, window), F32),
+            pltpu.VMEM((window, GROUP * ROWS), F32),
             pltpu.VMEM((window, HEAD_SIZE), BF),
             pltpu.VMEM((window, HEAD_SIZE), BF),
             pltpu.VMEM((RANK, window), BF),
@@ -274,17 +297,12 @@
         flops=4 * 10**9, size=4 * 10**6, smem_first=True,
     )
 
-    parts = lax.all_to_all(parts, "y", 0, 0, tiled=False).astype(F32)
-    here = (jnp.arange(SPAN) >= column)[:, None, None]
-    kept_back = jnp.sum(jnp.where(here, parts, 0.0), axis=0)
-    sent_back = jnp.sum(jnp.where(here, 0.0, parts), axis=0).astype(BF)
-    rows_x = lax.axis_size("x")
-    there = lax.ppermute(sent_back, "x", [(i, (i - 1) % rows_x) for i in range(rows_x)])
+    parts = lax.all_to_all(parts, seq, 0, 0, tiled=False)
 
     half = (length, 3 * RANK, ROWS)
     kept, sent = call(
         term_kernel, "terms", (shape(half), shape(half)),
-        (place, x, outgrad, back_query, kept_back, there, low_out, query_term, keyval_term, out_term),
+        (place, x, outgrad, back_query, parts, low_out, query_term, keyval_term, out_term),
         scratch=(pltpu.VMEM((2, *half), BF),),
         flops=10**8, size=4 * 10**6, smem_first=True,
     )

time: 159 us -> 152 us (0.956)
  blocking collectives: 48.4 us -> 69.9 us
  waiting for transfers between devices: 29.4 us -> 17.3 us
  starting transfers between devices: 54.1 us -> 42.2 us
  local copies, waits for them, and re-layouts: 7.51 us -> 3.33 us
    all_to_all x0 -> x1, blocking collectives: none -> 18.8 us  [per_device(): parts = lax.all_to_all(parts, seq, 0, 0, tiled=False)]
    ppermute x1, starting transfers between devices: 14.6 us -> 5.6 us  [per_device(): lax.ppermute(sent, 'core', swap).astype(F32)]
    all_to_all x1 -> x0, waiting for transfers between devices: 7.13 us -> none  [per_device(): parts = lax.all_to_all(parts, 'y', 0, 0, tiled=False).astype(F32)]
    unnamed x32 -> x24, local copies, waits for them, and re-layouts: 7.44 us -> 3.26 us
    all_to_all x1 -> x0, starting transfers between devices: 3.35 us -> none  [per_device(): parts = lax.all_to_all(parts, 'y', 0, 0, tiled=False).astype(F32)]
    ppermute x7, waiting for transfers between devices: 17.1 us -> 14.6 us  [shifted(): lax.ppermute(array, seq, [(i, (i + by) % length) for i in range(length)])]
    ppermute x1 -> x0, waiting for transfers between devices: 2.47 us -> none  [per_device(): lax.ppermute(sent_back, 'x', [(i, (i - 1) % rows_x) for i in range(rows_x)])]
    ppermute x7, starting transfers between devices: 27.1 us -> 29.5 us  [shifted(): lax.ppermute(array, seq, [(i, (i + by) % length) for i in range(length)])]
  transfers between devices with their start and end apart: 11 -> 9, of which waited for: 9 -> 8; matrix products, arithmetic and copies ran while one was open for 0% -> 0% of each run, Pallas kernels for 1% -> 1%
where the time goes in v2:
time: 152 us; the launch traced here: 151 us
  blocking collectives  69.9 us (46%)
  starting transfers between devices  42.2 us (28%)
  Pallas kernels  17.3 us (11%)
  waiting for transfers between devices  17.3 us (11%)
  local copies, waits for them, and re-layouts  3.33 us (2%)
    ppermute x7, starting transfers between devices, shifted(): lax.ppermute(array, seq, [(i, (i + by) % length) for i in range(length)])  29.5 us
    all_to_all x1, blocking collectives, per_device(): parts = lax.all_to_all(parts, seq, 0, 0, tiled=False)  18.8 us
    all_to_all x1, blocking collectives, per_device(): lax.all_to_all(jnp.broadcast_to(total, half), seq, 0, 0, tiled=False)  17.7 us
    all_to_all x1, blocking collectives, per_device(): lax.all_to_all(jnp.broadcast_to(total, (depth, *total.shape)), 'z', 0, 0,...  17.6 us
    pallas_call x5, Pallas kernels, call(): pl.pallas_call(kernel, name=name, out_shape=outs, in_specs=specs, out_spe...  17.3 us
    all_to_all x1, blocking collectives, per_device(): total = lax.all_to_all(total, seq, 0, 0, tiled=False)  15.8 us
    ppermute x7, waiting for transfers between devices, shifted(): lax.ppermute(array, seq, [(i, (i + by) % length) for i in range(length)])  14.6 us
    ppermute x1, starting transfers between devices, per_device(): other = lax.ppermute(total, 'core', swap)  7.15 us
  transfers between devices with their start and end apart: 9, of which 8 were waited for; matrix products, arithmetic and copies ran while one was open for 0% of the time, Pallas kernels for 1%

profile of v2, /device:TPU:1, one launch (start us, length us, event | category | flops | bytes accessed | tf_op | source)
XLA Modules:
  0.0 151.1 jit_solution(614444414401775761)
XLA Ops:
  0.7 3.0 %keyval.1 = (bf16[48,128]{1,0:T(8,128)(2,1)}, bf16[144,1024]{1,0:T(8,128)(2,1)}) custom-call(bf16[128,4096]{1,0:T(8,128)(2,1)} %bitcast.13, bf16[48,4096]{1,0:T(8,128)(2,1)} %bitcast.21, bf16[128,1024]{1,0:T(8,128)(2,1)} %bitcast.22, bf16[2,16,512]{2,1,0:T(8,128)(2,1)} %up_ref.1, s32[1,128]{1,0:T(1,128)} %doc_ref.1), custom_call_target="tpu_custom_call" | custom-call | flops 100000000 | bytes 2000000 | tf_op jit(solution)/shard_map/keyval/pallas_call | solution.py:209
  3.7 5.9 %collective-permute-start.4 = (bf16[144,1024]{1,0:T(8,128)(2,1)}, bf16[144,1024]{1,0:T(8,128)(2,1)S(1)}, u32[]{:S(2)}, u32[]{:S(2)}) collective-permute-start(bf16[144,1024]{1,0:T(8,128)(2,1)} %get-tuple-element.27.rest_0_), channel_id=1, source_target_pairs={{0,7},{1,8},{2,9},{3,10},{4,11},{5,12},{6,13},{7,14},{8,15},{9,16}... | collective-permute-start | bytes 884744 | tf_op jit(solution)/shard_map/ppermute | solution.py:261
  9.6 1.9 %collective-permute-start = (bf16[144,1024]{1,0:T(8,128)(2,1)}, bf16[144,1024]{1,0:T(8,128)(2,1)S(1)}, u32[]{:S(2)}, u32[]{:S(2)}) collective-permute-start(bf16[144,1024]{1,0:T(8,128)(2,1)} %get-tuple-element.27.rest_0_), channel_id=1, source_target_pairs={{0,1},{1,2},{2,3},{3,4},{4,5},{5,6},{6,7},{7,8},{8,9},{9,10},{10,1... | collective-permute-start | bytes 884744 | tf_op jit(solution)/shard_map/ppermute | solution.py:261
  11.6 2.7 %collective-permute-done.4.rest_7_ = bf16[144,1024]{1,0:T(8,128)(2,1)S(1)} collective-permute-done((bf16[144,1024]{1,0:T(8,128)(2,1)}, bf16[144,1024]{1,0:T(8,128)(2,1)S(1)}, u32[]{:S(2)}, u32[]{:S(2)}) %collective-permute-start.4) | collective-permute-done | bytes 294944 | tf_op jit(solution)/shard_map/ppermute | solution.py:261
  14.2 8.8 %collective-permute-start.5 = (bf16[144,1024]{1,0:T(8,128)(2,1)S(1)}, bf16[144,1024]{1,0:T(8,128)(2,1)S(1)}, u32[]{:S(2)}, u32[]{:S(2)}) collective-permute-start(bf16[144,1024]{1,0:T(8,128)(2,1)S(1)} %collective-permute-done.4.rest_7_), channel_id=1, source_target_pairs={{0,31},{1,0},{2,1},{3,2},{4,3},{5,4},{6,5},{7,6},{8,7},{9,8},{10,9... | collective-permute-start | bytes 884744 | tf_op jit(solution)/shard_map/ppermute | solution.py:261
  23.0 0.2 collective-permute-done.rest_1_
  23.2 1.9 %collective-permute-start.1 = (bf16[144,1024]{1,0:T(8,128)(2,1)S(1)}, bf16[144,1024]{1,0:T(8,128)(2,1)S(1)}, u32[]{:S(2)}, u32[]{:S(2)}) collective-permute-start(bf16[144,1024]{1,0:T(8,128)(2,1)S(1)} %collective-permute-done.rest_1_), channel_id=1, source_target_pairs={{0,1},{1,2},{2,3},{3,4},{4,5},{5,6},{6,7},{7,8},{8,9},{9,10},{10,1... | collective-permute-start | bytes 884744 | tf_op jit(solution)/shard_map/ppermute | solution.py:261
  25.1 1.5 %collective-permute-done.5.rest_6_ = bf16[144,1024]{1,0:T(8,128)(2,1)S(1)} collective-permute-done((bf16[144,1024]{1,0:T(8,128)(2,1)S(1)}, bf16[144,1024]{1,0:T(8,128)(2,1)S(1)}, u32[]{:S(2)}, u32[]{:S(2)}) %collective-permute-start.5) | collective-permute-done | bytes 294944 | tf_op jit(solution)/shard_map/ppermute | solution.py:261
  26.7 7.1 %collective-permute-start.6 = (bf16[144,1024]{1,0:T(8,128)(2,1)S(1)}, bf16[144,1024]{1,0:T(8,128)(2,1)S(1)}, u32[]{:S(2)}, u32[]{:S(2)}) collective-permute-start(bf16[144,1024]{1,0:T(8,128)(2,1)S(1)} %collective-permute-done.5.rest_6_), channel_id=1, source_target_pairs={{0,31},{1,0},{2,1},{3,2},{4,3},{5,4},{6,5},{7,6},{8,7},{9,8},{10,9... | collective-permute-start | bytes 884744 | tf_op jit(solution)/shard_map/ppermute | solution.py:261
  33.8 0.2 collective-permute-done.1.rest_2_
  34.0 1.9 %collective-permute-start.3 = (bf16[144,1024]{1,0:T(8,128)(2,1)S(1)}, bf16[144,1024]{1,0:T(8,128)(2,1)S(1)}, u32[]{:S(2)}, u32[]{:S(2)}) collective-permute-start(bf16[144,1024]{1,0:T(8,128)(2,1)S(1)} %collective-permute-done.1.rest_2_), channel_id=1, source_target_pairs={{0,2},{1,3},{2,4},{3,5},{4,6},{5,7},{6,8},{7,9},{8,10},{9,11},{10,... | collective-permute-start | bytes 884744 | tf_op jit(solution)/shard_map/ppermute | solution.py:261
  35.9 1.9 %collective-permute-start.2 = (bf16[144,1024]{1,0:T(8,128)(2,1)S(1)}, bf16[144,1024]{1,0:T(8,128)(2,1)}, u32[]{:S(2)}, u32[]{:S(2)}) collective-permute-start(bf16[144,1024]{1,0:T(8,128)(2,1)S(1)} %collective-permute-done.1.rest_2_), channel_id=1, source_target_pairs={{0,1},{1,2},{2,3},{3,4},{4,5},{5,6},{6,7},{7,8},{8,9},{9,10},{10,1... | collective-permute-start | bytes 884744 | tf_op jit(solution)/shard_map/ppermute | solution.py:261
  37.9 1.0 copy-done.3
  38.9 0.8 copy-done.6
  39.8 0.7 copy-done.9
  40.5 1.1 query.1
  41.6 0.1 pad_add_fusion.place_ref
  41.7 4.8 %collective-permute-done.3.rest_4_ = bf16[144,1024]{1,0:T(8,128)(2,1)S(1)} collective-permute-done((bf16[144,1024]{1,0:T(8,128)(2,1)S(1)}, bf16[144,1024]{1,0:T(8,128)(2,1)S(1)}, u32[]{:S(2)}, u32[]{:S(2)}) %collective-permute-start.3) | collective-permute-done | bytes 294944 | tf_op jit(solution)/shard_map/ppermute | solution.py:261
  46.5 5.2 %collective-permute-done.2.rest_3_ = bf16[144,1024]{1,0:T(8,128)(2,1)} collective-permute-done((bf16[144,1024]{1,0:T(8,128)(2,1)S(1)}, bf16[144,1024]{1,0:T(8,128)(2,1)}, u32[]{:S(2)}, u32[]{:S(2)}) %collective-permute-start.2) | collective-permute-done | bytes 294944 | tf_op jit(solution)/shard_map/ppermute | solution.py:261
  51.7 0.6 copy-done.10
  52.4 10.6 %attention.1 = (bf16[32,32,128]{2,1,0:T(8,128)(2,1)S(1)}, bf16[16,128]{1,0:T(8,128)(2,1)S(1)}, bf16[16,128]{1,0:T(8,128)(2,1)S(1)}, f32[16,2048]{1,0:T(8,128)S(1...) custom-call(s32[2]{0:T(128)S(1)} %pad_add_fusion.place_ref, s32[1,128]{1,0:T(1,128)S(1)} %copy-done.10, ...), custom_call_target="tpu_custom_call" | custom-call | flops 4000000000 | bytes 4000000 | tf_op jit(solution)/shard_map/attention/pallas_call | solution.py:209
  63.0 18.8 %all_to_all.20.parts_ref = bf16[32,32,128]{2,1,0:T(8,128)(2,1)S(1)} all-to-all(bf16[32,32,128]{2,1,0:T(8,128)(2,1)S(1)} %get-tuple-element.29), channel_id=1, replica_groups=mesh['z'=8,'core'=2,'x'=4,'y'=8] {'x','y'}, dimensions={0} | all-to-all | bytes 524288 | tf_op jit(solution)/shard_map/all_to_all | solution.py:300
  81.7 1.0 terms.1
  82.8 5.6 %collective-permute-start.7 = (bf16[32,48,128]{2,1,0:T(8,128)(2,1)S(1)}, bf16[32,48,128]{2,1,0:T(8,128)(2,1)S(1)}, u32[]{:S(2)}, u32[]{:S(2)}) collective-permute-start(bf16[32,48,128]{2,1,0:T(8,128)(2,1)S(1)} %get-tuple-element.35), channel_id=1, source_target_pairs={{0,32},{32,0},{1,33},{33,1},{2,34},{34,2},{3,35},{35,3},{4,36},{36... | collective-permute-start | bytes 1179656 | tf_op jit(solution)/shard_map/ppermute | solution.py:311
  88.4 1.3 collective-permute-done.7
  89.7 0.1 add_convert_fusion
  89.8 15.8 %all_to_all.21 = bf16[32,48,128]{2,1,0:T(8,128)(2,1)S(1)} all-to-all(bf16[32,48,128]{2,1,0:T(8,128)(2,1)S(1)} %add_convert_fusion), channel_id=1, replica_groups=mesh['z'=8,'core'=2,'x'=4,'y'=8] {'x','y'}, dimensions={0} | all-to-all | bytes 786432 | tf_op jit(solution)/shard_map/all_to_all | solution.py:312
  105.7 17.6 %all_to_all.22 = bf16[8,48,128]{2,1,0:T(8,128)(2,1)S(1)} all-to-all(bf16[8,48,128]{2,1,0:T(8,128)(2,1)S(1)} %broadcast_in_dim.6), channel_id=1, replica_groups=mesh['z'=8,'core'=2,'x'=4,'y'=8] {'z'}, dimensions={0} | all-to-all | bytes 196608 | tf_op jit(solution)/shard_map/all_to_all | solution.py:315
  123.4 17.7 %all_to_all.23.kept_ref = bf16[32,48,128]{2,1,0:T(8,128)(2,1)S(1)} all-to-all(bf16[32,48,128]{2,1,0:T(8,128)(2,1)S(1)} %broadcast_in_dim.7), channel_id=1, replica_groups=mesh['z'=8,'core'=2,'x'=4,'y'=8] {'x','y'}, dimensions={0} | all-to-all | bytes 786432 | tf_op jit(solution)/shard_map/all_to_all | solution.py:318
  141.1 7.2 %collective-permute-start.8 = (bf16[32,48,128]{2,1,0:T(8,128)(2,1)S(1)}, bf16[32,48,128]{2,1,0:T(8,128)(2,1)S(1)}, u32[]{:S(2)}, u32[]{:S(2)}) collective-permute-start(bf16[32,48,128]{2,1,0:T(8,128)(2,1)S(1)} %all_to_all.23.kept_ref), channel_id=1, source_target_pairs={{0,32},{32,0},{1,33},{33,1},{2,34},{34,2},{3,35},{35,3},{4,36},{36... | collective-permute-start | bytes 1179656 | tf_op jit(solution)/shard_map/ppermute | solution.py:319
  148.3 1.3 collective-permute-done.8.sent_ref
  149.6 1.5 unpack.1
  (26 shorter events, 0.2 us)
Async XLA Ops:
  0.6 37.2 %copy-start.1 = (bf16[1,128,4096]{2,1,0:T(8,128)(2,1)S(1)}, bf16[1,128,4096]{2,1,0:T(8,128)(2,1)}, u32[]{:S(2)}) copy-start(bf16[1,128,4096]{2,1,0:T(8,128)(2,1)} %param.15) | copy-start | bytes 3145732
  0.6 37.2 %copy-start.2 = (bf16[1,128,2048]{2,1,0:T(8,128)(2,1)S(1)}, bf16[1,128,2048]{2,1,0:T(8,128)(2,1)}, u32[]{:S(2)}) copy-start(bf16[1,128,2048]{2,1,0:T(8,128)(2,1)} %param.13) | copy-start | bytes 1572868
  0.7 37.2 %copy-start.4 = (bf16[16,4096]{1,0:T(8,128)(2,1)S(1)}, bf16[16,4096]{1,0:T(8,128)(2,1)}, u32[]{:S(2)}) copy-start(bf16[16,4096]{1,0:T(8,128)(2,1)} %out_up_ref.1) | copy-start | bytes 393220
  0.7 37.2 %copy-start.5 = (bf16[16,2048]{1,0:T(8,128)(2,1)S(1)}, bf16[16,2048]{1,0:T(8,128)(2,1)}, u32[]{:S(2)}) copy-start(bf16[16,2048]{1,0:T(8,128)(2,1)} %query_up_ref.3) | copy-start | bytes 196612
  3.7 10.5 %collective-permute-start.4 = (bf16[144,1024]{1,0:T(8,128)(2,1)}, bf16[144,1024]{1,0:T(8,128)(2,1)S(1)}, u32[]{:S(2)}, u32[]{:S(2)}) collective-permute-start(bf16[144,1024]{1,0:T(8,128)(2,1)} %get-tuple-element.27.rest_0_), channel_id=1, source_target_pairs={{0,7},{1,8},{2,9},{3,10},{4,11},{5,12},{6,13},{7,14},{8,15},{9,16}... | collective-permute-start | bytes 884744 | tf_op jit(solution)/shard_map/ppermute | solution.py:261
  9.6 13.6 %collective-permute-start = (bf16[144,1024]{1,0:T(8,128)(2,1)}, bf16[144,1024]{1,0:T(8,128)(2,1)S(1)}, u32[]{:S(2)}, u32[]{:S(2)}) collective-permute-start(bf16[144,1024]{1,0:T(8,128)(2,1)} %get-tuple-element.27.rest_0_), channel_id=1, source_target_pairs={{0,1},{1,2},{2,3},{3,4},{4,5},{5,6},{6,7},{7,8},{8,9},{9,10},{10,1... | collective-permute-start | bytes 884744 | tf_op jit(solution)/shard_map/ppermute | solution.py:261
  14.2 12.4 %collective-permute-start.5 = (bf16[144,1024]{1,0:T(8,128)(2,1)S(1)}, bf16[144,1024]{1,0:T(8,128)(2,1)S(1)}, u32[]{:S(2)}, u32[]{:S(2)}) collective-permute-start(bf16[144,1024]{1,0:T(8,128)(2,1)S(1)} %collective-permute-done.4.rest_7_), channel_id=1, source_target_pairs={{0,31},{1,0},{2,1},{3,2},{4,3},{5,4},{6,5},{7,6},{8,7},{9,8},{10,9... | collective-permute-start | bytes 884744 | tf_op jit(solution)/shard_map/ppermute | solution.py:261
  23.2 10.8 %collective-permute-start.1 = (bf16[144,1024]{1,0:T(8,128)(2,1)S(1)}, bf16[144,1024]{1,0:T(8,128)(2,1)S(1)}, u32[]{:S(2)}, u32[]{:S(2)}) collective-permute-start(bf16[144,1024]{1,0:T(8,128)(2,1)S(1)} %collective-permute-done.rest_1_), channel_id=1, source_target_pairs={{0,1},{1,2},{2,3},{3,4},{4,5},{5,6},{6,7},{7,8},{8,9},{9,10},{10,1... | collective-permute-start | bytes 884744 | tf_op jit(solution)/shard_map/ppermute | solution.py:261
  26.7 15.1 %collective-permute-start.6 = (bf16[144,1024]{1,0:T(8,128)(2,1)S(1)}, bf16[144,1024]{1,0:T(8,128)(2,1)S(1)}, u32[]{:S(2)}, u32[]{:S(2)}) collective-permute-start(bf16[144,1024]{1,0:T(8,128)(2,1)S(1)} %collective-permute-done.5.rest_6_), channel_id=1, source_target_pairs={{0,31},{1,0},{2,1},{3,2},{4,3},{5,4},{6,5},{7,6},{8,7},{9,8},{10,9... | collective-permute-start | bytes 884744 | tf_op jit(solution)/shard_map/ppermute | solution.py:261
  34.0 12.5 %collective-permute-start.3 = (bf16[144,1024]{1,0:T(8,128)(2,1)S(1)}, bf16[144,1024]{1,0:T(8,128)(2,1)S(1)}, u32[]{:S(2)}, u32[]{:S(2)}) collective-permute-start(bf16[144,1024]{1,0:T(8,128)(2,1)S(1)} %collective-permute-done.1.rest_2_), channel_id=1, source_target_pairs={{0,2},{1,3},{2,4},{3,5},{4,6},{5,7},{6,8},{7,9},{8,10},{9,11},{10,... | collective-permute-start | bytes 884744 | tf_op jit(solution)/shard_map/ppermute | solution.py:261
  35.9 15.8 %collective-permute-start.2 = (bf16[144,1024]{1,0:T(8,128)(2,1)S(1)}, bf16[144,1024]{1,0:T(8,128)(2,1)}, u32[]{:S(2)}, u32[]{:S(2)}) collective-permute-start(bf16[144,1024]{1,0:T(8,128)(2,1)S(1)} %collective-permute-done.1.rest_2_), channel_id=1, source_target_pairs={{0,1},{1,2},{2,3},{3,4},{4,5},{5,6},{6,7},{7,8},{8,9},{9,10},{10,1... | collective-permute-start | bytes 884744 | tf_op jit(solution)/shard_map/ppermute | solution.py:261
  37.9 1.0 copy-start.3
  38.9 0.8 copy-start.6
  39.8 0.7 copy-start.9
  40.5 11.2 %copy-start.7 = (bf16[2048,16]{0,1:T(8,128)(2,1)S(1)}, bf16[2048,16]{0,1:T(8,128)(2,1)}, u32[]{:S(2)}) copy-start(bf16[2048,16]{0,1:T(8,128)(2,1)} %param.20) | copy-start | bytes 196612
  40.5 11.2 %copy-start.8 = (bf16[2,16,512]{2,1,0:T(8,128)(2,1)S(1)}, bf16[2,16,512]{2,1,0:T(8,128)(2,1)}, u32[]{:S(2)}) copy-start(bf16[2,16,512]{2,1,0:T(8,128)(2,1)} %up_ref.1) | copy-start | bytes 98308
  40.5 11.2 %copy-start.11 = (bf16[144,1024]{1,0:T(8,128)(2,1)S(1)}, bf16[144,1024]{1,0:T(8,128)(2,1)}, u32[]{:S(2)}) copy-start(bf16[144,1024]{1,0:T(8,128)(2,1)} %get-tuple-element.27.rest_0_) | copy-start | bytes 884740
  51.7 0.7 copy-start.10
  52.4 29.4 %copy-start = (bf16[1,128,4096]{2,1,0:T(8,128)(2,1)S(1)}, bf16[1,128,4096]{2,1,0:T(8,128)(2,1)}, u32[]{:S(2)}) copy-start(bf16[1,128,4096]{2,1,0:T(8,128)(2,1)} %param.11) | copy-start | bytes 3145732
  82.8 6.9 %collective-permute-start.7 = (bf16[32,48,128]{2,1,0:T(8,128)(2,1)S(1)}, bf16[32,48,128]{2,1,0:T(8,128)(2,1)S(1)}, u32[]{:S(2)}, u32[]{:S(2)}) collective-permute-start(bf16[32,48,128]{2,1,0:T(8,128)(2,1)S(1)} %get-tuple-element.35), channel_id=1, source_target_pairs={{0,32},{32,0},{1,33},{33,1},{2,34},{34,2},{3,35},{35,3},{4,36},{36... | collective-permute-start | bytes 1179656 | tf_op jit(solution)/shard_map/ppermute | solution.py:311
  141.1 8.5 %collective-permute-start.8 = (bf16[32,48,128]{2,1,0:T(8,128)(2,1)S(1)}, bf16[32,48,128]{2,1,0:T(8,128)(2,1)S(1)}, u32[]{:S(2)}, u32[]{:S(2)}) collective-permute-start(bf16[32,48,128]{2,1,0:T(8,128)(2,1)S(1)} %all_to_all.23.kept_ref), channel_id=1, source_target_pairs={{0,32},{32,0},{1,33},{33,1},{2,34},{34,2},{3,35},{35,3},{4,36},{36... | collective-permute-start | bytes 1179656 | tf_op jit(solution)/shard_map/ppermute | solution.py:319

commit v3 on v2

--- a/solution.py
+++ b/solution.py
@@ -19,8 +19,8 @@
 BF = jnp.bfloat16
 F32 = jnp.float32
 INVERSE = 1.0 / HEAD_SIZE**0.5
+DEVICES = 32
 LOG2E = 1.4426950408889634
-DEVICES = 32
 
 NT = (((1,), (1,)), ((), ()))
 TN = (((0,), (0,)), ((), ()))
@@ -55,25 +55,36 @@
     )
 
 
-def query_kernel(low_ref, query_ref, query_up_ref, outgrad_ref, out_up_ref, frozen_ref, out_down_ref,
-                 q_ref, grad_ref, back_out_ref):
+def query_kernel(low_any, query_any, query_up_any, outgrad_any, out_up_any, frozen_any, out_down_any,
+                 q_ref, grad_ref, back_out_ref,
+                 low_ref, query_ref, query_up_ref, outgrad_ref, out_up_ref, frozen_ref, out_down_ref, sems):
+    pairs = ((outgrad_any, outgrad_ref), (out_up_any, out_up_ref), (low_any, low_ref), (query_up_any, query_up_ref),
+             (query_any, query_ref), (out_down_any, out_down_ref), (frozen_any, frozen_ref))
+    copies = [pltpu.make_async_copy(a, b, sems.at[i]) for i, (a, b) in enumerate(pairs)]
+    for copy in copies:
+        copy.start()
+    for copy in copies[:5]:
+        copy.wait()
+    back_out = dot(out_up_ref[...], outgrad_ref[...], NT).astype(BF)
+    back_out_ref[...] = back_out
     q_ref[...] = (
         query_ref[...].astype(F32) + 0.5 * dot(low_ref[pl.ds(0, RANK), :], query_up_ref[...], TN)
     ).astype(BF)
-    back_out = dot(out_up_ref[...], outgrad_ref[...], NT).astype(BF)
-    back_out_ref[...] = back_out
+    for copy in copies[5:]:
+        copy.wait()
     grad_ref[...] = (
         frozen_ref[...].astype(F32) + 0.5 * dot(back_out, out_down_ref[...], TN)
     ).astype(BF)
 
 
-def attention_kernel(place_ref, doc_ref, low_ref, q_ref, grad_ref, back_out_ref, query_up_ref, up_ref,
+def attention_kernel(low_ref, q_ref, grad_ref, back_out_ref, query_up_ref, up_ref,
                      out_down_ref, *rest):
     blocks = rest[:SPAN]
     parts_ref, back_query_ref, low_out_ref, query_term_ref, keyval_term_ref, out_term_ref = rest[SPAN : SPAN + 6]
     bias, keys, values, low_keys, low_values, back_parts = rest[SPAN + 6 :]
-    position = place_ref[0]
-    own = jnp.broadcast_to(doc_ref[...].astype(F32), (ROWS, ROWS))
+    position = lax.axis_index("x") * SPAN + lax.axis_index("y")
+    own = blocks[0][pl.ds(ROWS, RANK), pl.ds(2 * ROWS, ROWS)][:1]
+    own = jnp.broadcast_to(own.astype(F32), (ROWS, ROWS))
     row = lax.broadcasted_iota(jnp.int32, (ROWS, ROWS), 0)
     col = lax.broadcasted_iota(jnp.int32, (ROWS, ROWS), 1)
     for o in range(SPAN):
@@ -142,14 +153,13 @@
         parts_ref[lax.rem(position + (DEVICES - o), DEVICES)] = back_parts[:, pl.ds(o * ROWS, ROWS)].astype(BF)
 
 
-def term_kernel(place_ref, x_ref, outgrad_ref, back_query_ref, parts_ref, low_out_ref,
+def term_kernel(x_ref, outgrad_ref, back_query_ref, parts_ref, low_out_ref,
                 query_term_ref, keyval_term_ref, out_term_ref, kept_ref, sent_ref, both):
-    core = place_ref[1]
+    core = lax.axis_index("core")
     back_keyval = parts_ref[0].astype(F32)
     for i in range(1, DEVICES):
         back_keyval = back_keyval + parts_ref[i].astype(F32)
-    back_keyval = back_keyval.astype(BF)
-    back = jnp.concatenate([back_query_ref[...], back_keyval], axis=0)
+    back = jnp.concatenate([back_query_ref[...], back_keyval.astype(BF)], axis=0)
     down = dot(back, x_ref[...]).astype(BF)
     up = dot(low_out_ref[...], outgrad_ref[...]).astype(BF)
     query_term = query_term_ref[...].astype(BF)
@@ -178,8 +188,8 @@
     sent_ref[...] = both[1 - core]
 
 
-def unpack_kernel(place_ref, kept_ref, sent_ref, down_ref, query_ref, keyval_ref, out_down_ref, out_up_ref, both):
-    core = place_ref[1]
+def unpack_kernel(kept_ref, sent_ref, down_ref, query_ref, keyval_ref, out_down_ref, out_up_ref, both):
+    core = lax.axis_index("core")
     both[core] = kept_ref[...]
     both[1 - core] = sent_ref[...]
 
@@ -201,11 +211,10 @@
 
 
 VMEM = pl.BlockSpec(memory_space=pltpu.VMEM)
-SMEM = pl.BlockSpec(memory_space=pltpu.SMEM)
-
-
-def call(kernel, name, outs, args, scratch=(), flops=0, size=0, smem_first=False, limit=32 << 20, kind=None):
-    specs = [SMEM if smem_first and i == 0 else (kind or VMEM) for i in range(len(args))]
+
+
+def call(kernel, name, outs, args, scratch=(), flops=0, size=0, limit=32 << 20, kind=None):
+    specs = [kind or VMEM] * len(args)
     return pl.pallas_call(
         kernel,
         name=name,
@@ -220,6 +229,18 @@
 
 def shape(dims, dtype=BF):
     return jax.ShapeDtypeStruct(dims, dtype)
+
+
+def chain_pairs(length):
+    up = [[(i, i + 1) for i in range(step, length - 1)] for step in range(SPAN // 2)]
+    down, wanted = [], {(place - 5, place) for place in range(5, length)}
+    for _ in range(2):
+        down.insert(0, sorted(((place + 1) % length, place) for _, place in wanted))
+        earlier = {(block, (place + 1) % length) for block, place in wanted}
+        offset = 5 + len(down)
+        wanted = earlier | {(place - offset, place) for place in range(offset, length)}
+    down.insert(0, sorted(wanted))
+    return up, down
 
 
 def per_device(
@@ -241,7 +262,6 @@
     out_down = output_down_weight.T
     seq = ("x", "y")
     length = lax.axis_size("x") * lax.axis_size("y")
-    place = jnp.stack([lax.axis_index(seq), lax.axis_index("core")]).astype(jnp.int32)
 
     low, pack = call(
         keyval_kernel, "keyval", (shape((3 * RANK, ROWS)), shape((PACK_ROWS, 2 * KEY_COLUMNS))),
@@ -257,21 +277,33 @@
         flops=10**8, size=2 * 10**6, limit=56 << 20, kind=pl.BlockSpec(memory_space=pl.ANY),
     )
 
-    def shifted(array, by):
-        return lax.ppermute(array, seq, [(i, (i + by) % length) for i in range(length)])
-
     blocks = {0: pack}
-    for step in range(1, 4):
-        blocks[step] = shifted(blocks[step - 1], 1)
-        blocks[8 - step] = shifted(pack, 7) if step == 1 else shifted(blocks[9 - step], -1)
-    blocks[4] = shifted(blocks[2], 2)
+    up, down = chain_pairs(length)
+    for step in range(1, 3):
+        blocks[step] = lax.ppermute(blocks[step - 1], seq, up[step - 1])
+        blocks[8 - step] = lax.ppermute(blocks[(9 - step) % SPAN], seq, down[step - 1])
 
     q, grad, back_out = call(
         query_kernel, "query",
         (shape((ROWS, QUERY_COLUMNS)), shape((ROWS, QUERY_COLUMNS)), shape((RANK, ROWS))),
         (low, frozen_query_state[0], query_up_weight, outgrad, output_up_weight, frozen_output_gradient[0], out_down),
-        flops=10**8, size=4 * 10**6,
-    )
+        scratch=(
+            pltpu.VMEM((3 * RANK, ROWS), BF),
+            pltpu.VMEM((ROWS, QUERY_COLUMNS), BF),
+            pltpu.VMEM((RANK, QUERY_COLUMNS), BF),
+            pltpu.VMEM((ROWS, WIDTH), BF),
+            pltpu.VMEM((RANK, WIDTH), BF),
+            pltpu.VMEM((ROWS, QUERY_COLUMNS), BF),
+            pltpu.VMEM((RANK, QUERY_COLUMNS), BF),
+            pltpu.SemaphoreType.DMA((7,)),
+        ),
+        flops=10**8, size=4 * 10**6, limit=56 << 20, kind=pl.BlockSpec(memory_space=pl.ANY),
+    )
+
+    blocks[2], _ = lax.optimization_barrier((blocks[2], back_out))
+    blocks[3] = lax.ppermute(blocks[2], seq, up[2])
+    blocks[5] = lax.ppermute(blocks[6], seq, down[2])
+    blocks[4] = lax.ppermute(blocks[3], seq, up[3])
 
     window = SPAN * ROWS
     parts, back_query, low_out, query_term, keyval_term, out_term = call(
@@ -284,7 +316,7 @@
             shape((2 * RANK, KEY_COLUMNS), F32),
             shape((RANK, QUERY_COLUMNS), F32),
         ),
-        (place, document_index, low, q, grad, back_out, query_up_weight, keyvalue_up_weight, out_down,
+        (low, q, grad, back_out, query_up_weight, keyvalue_up_weight, out_down,
          *[blocks[o] for o in range(SPAN)]),
         scratch=(
             pltpu.VMEM((window, GROUP * ROWS), F32),
@@ -294,7 +326,7 @@
             pltpu.VMEM((RANK, window), BF),
             pltpu.VMEM((2 * RANK, window), F32),
         ),
-        flops=4 * 10**9, size=4 * 10**6, smem_first=True,
+        flops=4 * 10**9, size=4 * 10**6,
     )
 
     parts = lax.all_to_all(parts, seq, 0, 0, tiled=False)
@@ -302,9 +334,9 @@
     half = (length, 3 * RANK, ROWS)
     kept, sent = call(
         term_kernel, "terms", (shape(half), shape(half)),
-        (place, x, outgrad, back_query, parts, low_out, query_term, keyval_term, out_term),
+        (x, outgrad, back_query, parts, low_out, query_term, keyval_term, out_term),
         scratch=(pltpu.VMEM((2, *half), BF),),
-        flops=10**8, size=4 * 10**6, smem_first=True,
+        flops=10**8, size=4 * 10**6,
     )
 
     swap = [(0, 1), (1, 0)]
@@ -327,9 +359,9 @@
             shape((RANK, QUERY_COLUMNS)),
             shape((RANK, WIDTH)),
         ),
-        (place, total, other),
+        (total, other),
         scratch=(pltpu.VMEM((2, *half), BF),),
-        size=2 * 10**6, smem_first=True,
+        size=2 * 10**6,
     )
     return lora.transpose(0, 2, 1), query_up, keyval_up, output_down.T, output_up
 

time: 152 us -> 146 us (0.961)
  waiting for transfers between devices: 17.3 us -> 11 us
  blocking collectives: 69.9 us -> 72 us
    ppermute x7, waiting for transfers between devices: 14.6 us -> 8.31 us  [the longest x2 5.37 us: per_device(): lax.ppermute(blocks[(9 - step) % SPAN], seq, down[step - 1])]
    ppermute x7, starting transfers between devices: 29.5 us -> 26.8 us  [the longest x2 13.3 us: per_device(): lax.ppermute(blocks[(9 - step) % SPAN], seq, down[step - 1])]
    ppermute x1, starting transfers between devices: 5.6 us -> 8.06 us  [per_device(): lax.ppermute(sent, 'core', swap).astype(F32)]
    all_to_all x1, blocking collectives: 18.8 us -> 20.9 us  [per_device(): parts = lax.all_to_all(parts, seq, 0, 0, tiled=False)]
    unnamed x24 -> x20, local copies, waits for them, and re-layouts: 3.26 us -> 2.12 us
  transfers between devices with their start and end apart: 9 -> 9, of which waited for: 8 -> 5; matrix products, arithmetic and copies ran while one was open for 0% -> 0% of each run, Pallas kernels for 1% -> 2%
where the time goes in v3:
time: 146 us
  blocking collectives  72 us (49%)
  starting transfers between devices  42 us (29%)
  Pallas kernels  17.3 us (12%)
  waiting for transfers between devices  11 us (8%)
  local copies, waits for them, and re-layouts  2.19 us (2%)
    all_to_all x1, blocking collectives, per_device(): parts = lax.all_to_all(parts, seq, 0, 0, tiled=False)  20.9 us
    all_to_all x1, blocking collectives, per_device(): lax.all_to_all(jnp.broadcast_to(total, half), seq, 0, 0, tiled=False)  17.7 us
    all_to_all x1, blocking collectives, per_device(): lax.all_to_all(jnp.broadcast_to(total, (depth, *total.shape)), 'z', 0, 0,...  17.4 us
    pallas_call x5, Pallas kernels, call(): pl.pallas_call(kernel, name=name, out_shape=outs, in_specs=specs, out_spe...  17.3 us
    all_to_all x1, blocking collectives, per_device(): total = lax.all_to_all(total, seq, 0, 0, tiled=False)  16 us
    ppermute x2, starting transfers between devices, per_device(): lax.ppermute(blocks[(9 - step) % SPAN], seq, down[step - 1])  13.3 us
    ppermute x1, starting transfers between devices, per_device(): lax.ppermute(sent, 'core', swap).astype(F32)  8.06 us
    ppermute x1, starting transfers between devices, per_device(): blocks[5] = lax.ppermute(blocks[6], seq, down[2])  7.43 us
  transfers between devices with their start and end apart: 9, of which 5 were waited for; matrix products, arithmetic and copies ran while one was open for 0% of the time, Pallas kernels for 2%

profile of v3, /device:TPU:1, one launch (start us, length us, event | category | flops | bytes accessed | tf_op | source)
XLA Modules:
  0.0 145.6 jit_solution(1456315153592200314)
XLA Ops:
  0.6 2.9 %keyval.1 = (bf16[48,128]{1,0:T(8,128)(2,1)}, bf16[144,1024]{1,0:T(8,128)(2,1)}) custom-call(bf16[128,4096]{1,0:T(8,128)(2,1)} %bitcast.11, bf16[48,4096]{1,0:T(8,128)(2,1)} %bitcast.19, bf16[128,1024]{1,0:T(8,128)(2,1)} %bitcast.20, bf16[2,16,512]{2,1,0:T(8,128)(2,1)} %up_ref.1, s32[1,128]{1,0:T(1,128)} %doc_any.1), custom_call_target="tpu_custom_call" | custom-call | flops 100000000 | bytes 2000000 | tf_op jit(solution)/shard_map/keyval/pallas_call | solution.py:218
  3.5 4.1 %collective-permute-start = (bf16[144,1024]{1,0:T(8,128)(2,1)}, bf16[144,1024]{1,0:T(8,128)(2,1)S(1)}, u32[]{:S(2)}, u32[]{:S(2)}) collective-permute-start(bf16[144,1024]{1,0:T(8,128)(2,1)} %get-tuple-element.28.rest_0_), channel_id=1, source_target_pairs={{0,1},{1,2},{2,3},{3,4},{4,5},{5,6},{6,7},{7,8},{8,9},{9,10},{10,1... | collective-permute-start | bytes 884744 | tf_op jit(solution)/shard_map/ppermute | solution.py:283
  7.6 4.2 %collective-permute-start.4 = (bf16[144,1024]{1,0:T(8,128)(2,1)}, bf16[144,1024]{1,0:T(8,128)(2,1)S(1)}, u32[]{:S(2)}, u32[]{:S(2)}) collective-permute-start(bf16[144,1024]{1,0:T(8,128)(2,1)} %get-tuple-element.28.rest_0_), channel_id=1, source_target_pairs={{0,7},{1,8},{2,9},{3,10},{4,11},{5,12},{6,13},{7,14},{8,15},{9,16}... | collective-permute-start | bytes 884744 | tf_op jit(solution)/shard_map/ppermute | solution.py:284
  11.8 0.7 collective-permute-start.1
  12.5 0.0 copy-start.2
  12.5 0.0 copy-start.3
  12.5 0.0 copy-start.8
  12.6 3.5 %query.1 = (bf16[128,2048]{1,0:T(8,128)(2,1)}, bf16[128,2048]{1,0:T(8,128)(2,1)}, bf16[16,128]{1,0:T(8,128)(2,1)}) custom-call(bf16[48,128]{1,0:T(8,128)(2,1)} %get-tuple-element.24.low_any.low_ref, bf16[128,2048]{1,0:T(8,128)(2,1)} %bitcast.17, bf16[16,2048]{1,0:T(8,128)(2,1)} %query_up_ref.1, bf16[128,4096]{1,0:T(8,128)(2,1)} %bitcast.13, ...), custom_call_target="tpu_custom_call" | custom-call | flops 100000000 | bytes 4000000 | tf_op jit(solution)/shard_map/query/pallas_call | solution.py:218
  16.0 0.0 copy-start.9
  16.0 1.3 collective-permute-done.4.rest_7_
  17.4 9.1 %collective-permute-start.5 = (bf16[144,1024]{1,0:T(8,128)(2,1)S(1)}, bf16[144,1024]{1,0:T(8,128)(2,1)S(1)}, u32[]{:S(2)}, u32[]{:S(2)}) collective-permute-start(bf16[144,1024]{1,0:T(8,128)(2,1)S(1)} %collective-permute-done.4.rest_7_), channel_id=1, source_target_pairs={{0,31},{1,0},{7,6},{8,7},{9,8},{10,9},{11,10},{12,11},{13,12},{14,... | collective-permute-start | bytes 884744 | tf_op jit(solution)/shard_map/ppermute | solution.py:284
  26.5 0.7 collective-permute-start.2
  27.2 4.0 %collective-permute-done.5.rest_6_ = bf16[144,1024]{1,0:T(8,128)(2,1)S(1)} collective-permute-done((bf16[144,1024]{1,0:T(8,128)(2,1)S(1)}, bf16[144,1024]{1,0:T(8,128)(2,1)S(1)}, u32[]{:S(2)}, u32[]{:S(2)}) %collective-permute-start.5) | collective-permute-done | bytes 294944 | tf_op jit(solution)/shard_map/ppermute | solution.py:284
  31.2 7.4 %collective-permute-start.6 = (bf16[144,1024]{1,0:T(8,128)(2,1)S(1)}, bf16[144,1024]{1,0:T(8,128)(2,1)S(1)}, u32[]{:S(2)}, u32[]{:S(2)}) collective-permute-start(bf16[144,1024]{1,0:T(8,128)(2,1)S(1)} %collective-permute-done.5.rest_6_), channel_id=1, source_target_pairs={{0,31},{6,5},{7,6},{8,7},{9,8},{10,9},{11,10},{12,11},{13,12},{14,... | collective-permute-start | bytes 884744 | tf_op jit(solution)/shard_map/ppermute | solution.py:305
  38.6 0.7 collective-permute-start.3
  39.3 2.9 %collective-permute-done.6.rest_5_ = bf16[144,1024]{1,0:T(8,128)(2,1)S(1)} collective-permute-done((bf16[144,1024]{1,0:T(8,128)(2,1)S(1)}, bf16[144,1024]{1,0:T(8,128)(2,1)S(1)}, u32[]{:S(2)}, u32[]{:S(2)}) %collective-permute-start.6) | collective-permute-done | bytes 294944 | tf_op jit(solution)/shard_map/ppermute | solution.py:305
  42.3 1.0 copy-done.6
  43.3 1.0 copy-done.7
  44.4 9.6 %attention.1 = (bf16[32,32,128]{2,1,0:T(8,128)(2,1)S(1)}, bf16[16,128]{1,0:T(8,128)(2,1)S(1)}, bf16[16,128]{1,0:T(8,128)(2,1)S(1)}, f32[16,2048]{1,0:T(8,128)S(1...) custom-call(bf16[48,128]{1,0:T(8,128)(2,1)S(1)} %copy-done.5, bf16[128,2048]{1,0:T(8,128)(2,1)S(1)} %copy-done.6, ...), custom_call_target="tpu_custom_call" | custom-call | flops 4000000000 | bytes 4000000 | tf_op jit(solution)/shard_map/attention/pallas_call | solution.py:218
  54.0 20.9 %all_to_all.20.parts_ref = bf16[32,32,128]{2,1,0:T(8,128)(2,1)S(1)} all-to-all(bf16[32,32,128]{2,1,0:T(8,128)(2,1)S(1)} %get-tuple-element.31), channel_id=1, replica_groups=mesh['z'=8,'core'=2,'x'=4,'y'=8] {'x','y'}, dimensions={0} | all-to-all | bytes 524288 | tf_op jit(solution)/shard_map/all_to_all | solution.py:332
  74.9 0.4 terms.1
  75.3 8.1 %collective-permute-start.7 = (bf16[32,48,128]{2,1,0:T(8,128)(2,1)S(1)}, bf16[32,48,128]{2,1,0:T(8,128)(2,1)S(1)}, u32[]{:S(2)}, u32[]{:S(2)}) collective-permute-start(bf16[32,48,128]{2,1,0:T(8,128)(2,1)S(1)} %get-tuple-element.37), channel_id=1, source_target_pairs={{0,32},{32,0},{1,33},{33,1},{2,34},{34,2},{3,35},{35,3},{4,36},{36... | collective-permute-start | bytes 1179656 | tf_op jit(solution)/shard_map/ppermute | solution.py:343
  83.4 1.3 collective-permute-done.7
  84.7 0.1 add_convert_fusion
  84.9 16.0 %all_to_all.21 = bf16[32,48,128]{2,1,0:T(8,128)(2,1)S(1)} all-to-all(bf16[32,48,128]{2,1,0:T(8,128)(2,1)S(1)} %add_convert_fusion), channel_id=1, replica_groups=mesh['z'=8,'core'=2,'x'=4,'y'=8] {'x','y'}, dimensions={0} | all-to-all | bytes 786432 | tf_op jit(solution)/shard_map/all_to_all | solution.py:344
  100.8 0.1 reduce_sum.21
  100.9 17.4 %all_to_all.22 = bf16[8,48,128]{2,1,0:T(8,128)(2,1)S(1)} all-to-all(bf16[8,48,128]{2,1,0:T(8,128)(2,1)S(1)} %broadcast_in_dim.6), channel_id=1, replica_groups=mesh['z'=8,'core'=2,'x'=4,'y'=8] {'z'}, dimensions={0} | all-to-all | bytes 196608 | tf_op jit(solution)/shard_map/all_to_all | solution.py:347
  118.4 0.1 broadcast_in_dim.7
  118.4 17.7 %all_to_all.23.kept_ref = bf16[32,48,128]{2,1,0:T(8,128)(2,1)S(1)} all-to-all(bf16[32,48,128]{2,1,0:T(8,128)(2,1)S(1)} %broadcast_in_dim.7), channel_id=1, replica_groups=mesh['z'=8,'core'=2,'x'=4,'y'=8] {'x','y'}, dimensions={0} | all-to-all | bytes 786432 | tf_op jit(solution)/shard_map/all_to_all | solution.py:350
  136.1 7.2 %collective-permute-start.8 = (bf16[32,48,128]{2,1,0:T(8,128)(2,1)S(1)}, bf16[32,48,128]{2,1,0:T(8,128)(2,1)S(1)}, u32[]{:S(2)}, u32[]{:S(2)}) collective-permute-start(bf16[32,48,128]{2,1,0:T(8,128)(2,1)S(1)} %all_to_all.23.kept_ref), channel_id=1, source_target_pairs={{0,32},{32,0},{1,33},{33,1},{2,34},{34,2},{3,35},{35,3},{4,36},{36... | collective-permute-start | bytes 1179656 | tf_op jit(solution)/shard_map/ppermute | solution.py:351
  143.3 1.3 collective-permute-done.8.sent_ref
  144.6 1.0 unpack.1
  (21 shorter events, 0.1 us)
Async XLA Ops:
  3.5 8.3 %collective-permute-start = (bf16[144,1024]{1,0:T(8,128)(2,1)}, bf16[144,1024]{1,0:T(8,128)(2,1)S(1)}, u32[]{:S(2)}, u32[]{:S(2)}) collective-permute-start(bf16[144,1024]{1,0:T(8,128)(2,1)} %get-tuple-element.28.rest_0_), channel_id=1, source_target_pairs={{0,1},{1,2},{2,3},{3,4},{4,5},{5,6},{6,7},{7,8},{8,9},{9,10},{10,1... | collective-permute-start | bytes 884744 | tf_op jit(solution)/shard_map/ppermute | solution.py:283
  7.6 9.8 %collective-permute-start.4 = (bf16[144,1024]{1,0:T(8,128)(2,1)}, bf16[144,1024]{1,0:T(8,128)(2,1)S(1)}, u32[]{:S(2)}, u32[]{:S(2)}) collective-permute-start(bf16[144,1024]{1,0:T(8,128)(2,1)} %get-tuple-element.28.rest_0_), channel_id=1, source_target_pairs={{0,7},{1,8},{2,9},{3,10},{4,11},{5,12},{6,13},{7,14},{8,15},{9,16}... | collective-permute-start | bytes 884744 | tf_op jit(solution)/shard_map/ppermute | solution.py:284
  11.8 14.7 %collective-permute-start.1 = (bf16[144,1024]{1,0:T(8,128)(2,1)S(1)}, bf16[144,1024]{1,0:T(8,128)(2,1)S(1)}, u32[]{:S(2)}, u32[]{:S(2)}) collective-permute-start(bf16[144,1024]{1,0:T(8,128)(2,1)S(1)} %collective-permute-done.rest_1_), channel_id=1, source_target_pairs={{1,2},{2,3},{3,4},{4,5},{5,6},{6,7},{7,8},{8,9},{9,10},{10,11},{11... | collective-permute-start | bytes 884744 | tf_op jit(solution)/shard_map/ppermute | solution.py:283
  12.5 29.8 %copy-start.2 = (bf16[16,2048]{1,0:T(8,128)(2,1)S(1)}, bf16[16,2048]{1,0:T(8,128)(2,1)}, u32[]{:S(2)}) copy-start(bf16[16,2048]{1,0:T(8,128)(2,1)} %query_up_ref.1) | copy-start | bytes 196612
  12.5 29.8 %copy-start.3 = (bf16[2048,16]{0,1:T(8,128)(2,1)S(1)}, bf16[2048,16]{0,1:T(8,128)(2,1)}, u32[]{:S(2)}) copy-start(bf16[2048,16]{0,1:T(8,128)(2,1)} %param.20) | copy-start | bytes 196612
  12.5 29.8 %copy-start.4 = (bf16[2,16,512]{2,1,0:T(8,128)(2,1)S(1)}, bf16[2,16,512]{2,1,0:T(8,128)(2,1)}, u32[]{:S(2)}) copy-start(bf16[2,16,512]{2,1,0:T(8,128)(2,1)} %up_ref.1) | copy-start | bytes 98308
  12.5 29.7 %copy-start.5 = (bf16[48,128]{1,0:T(8,128)(2,1)S(1)}, bf16[48,128]{1,0:T(8,128)(2,1)}, u32[]{:S(2)}) copy-start(bf16[48,128]{1,0:T(8,128)(2,1)} %get-tuple-element.24.low_any.low_ref) | copy-start | bytes 36868
  12.5 29.7 %copy-start.8 = (bf16[144,1024]{1,0:T(8,128)(2,1)S(1)}, bf16[144,1024]{1,0:T(8,128)(2,1)}, u32[]{:S(2)}) copy-start(bf16[144,1024]{1,0:T(8,128)(2,1)} %get-tuple-element.28.rest_0_) | copy-start | bytes 884740
  16.0 26.3 %copy-start.9 = (bf16[16,128]{1,0:T(8,128)(2,1)S(1)}, bf16[16,128]{1,0:T(8,128)(2,1)}, u32[]{:S(2)}) copy-start(bf16[16,128]{1,0:T(8,128)(2,1)} %get-tuple-element.27.back_out_ref) | copy-start | bytes 12292
  17.4 13.8 %collective-permute-start.5 = (bf16[144,1024]{1,0:T(8,128)(2,1)S(1)}, bf16[144,1024]{1,0:T(8,128)(2,1)S(1)}, u32[]{:S(2)}, u32[]{:S(2)}) collective-permute-start(bf16[144,1024]{1,0:T(8,128)(2,1)S(1)} %collective-permute-done.4.rest_7_), channel_id=1, source_target_pairs={{0,31},{1,0},{7,6},{8,7},{9,8},{10,9},{11,10},{12,11},{13,12},{14,... | collective-permute-start | bytes 884744 | tf_op jit(solution)/shard_map/ppermute | solution.py:284
  26.5 12.2 %collective-permute-start.2 = (bf16[144,1024]{1,0:T(8,128)(2,1)S(1)}, bf16[144,1024]{1,0:T(8,128)(2,1)S(1)}, u32[]{:S(2)}, u32[]{:S(2)}) collective-permute-start(bf16[144,1024]{1,0:T(8,128)(2,1)S(1)} %collective-permute-done.1.rest_2_), channel_id=1, source_target_pairs={{2,3},{3,4},{4,5},{5,6},{6,7},{7,8},{8,9},{9,10},{10,11},{11,12},{... | collective-permute-start | bytes 884744 | tf_op jit(solution)/shard_map/ppermute | solution.py:304
  31.2 11.1 %collective-permute-start.6 = (bf16[144,1024]{1,0:T(8,128)(2,1)S(1)}, bf16[144,1024]{1,0:T(8,128)(2,1)S(1)}, u32[]{:S(2)}, u32[]{:S(2)}) collective-permute-start(bf16[144,1024]{1,0:T(8,128)(2,1)S(1)} %collective-permute-done.5.rest_6_), channel_id=1, source_target_pairs={{0,31},{6,5},{7,6},{8,7},{9,8},{10,9},{11,10},{12,11},{13,12},{14,... | collective-permute-start | bytes 884744 | tf_op jit(solution)/shard_map/ppermute | solution.py:305
  38.6 3.6 %collective-permute-start.3 = (bf16[144,1024]{1,0:T(8,128)(2,1)S(1)}, bf16[144,1024]{1,0:T(8,128)(2,1)S(1)}, u32[]{:S(2)}, u32[]{:S(2)}) collective-permute-start(bf16[144,1024]{1,0:T(8,128)(2,1)S(1)} %collective-permute-done.2.rest_3_), channel_id=1, source_target_pairs={{3,4},{4,5},{5,6},{6,7},{7,8},{8,9},{9,10},{10,11},{11,12},{12,13}... | collective-permute-start | bytes 884744 | tf_op jit(solution)/shard_map/ppermute | solution.py:306
  42.3 1.0 copy-start.6
  43.3 1.0 copy-start.7
  44.4 30.5 %copy-start = (bf16[1,128,4096]{2,1,0:T(8,128)(2,1)S(1)}, bf16[1,128,4096]{2,1,0:T(8,128)(2,1)}, u32[]{:S(2)}) copy-start(bf16[1,128,4096]{2,1,0:T(8,128)(2,1)} %param.11) | copy-start | bytes 3145732
  44.4 30.5 %copy-start.1 = (bf16[1,128,4096]{2,1,0:T(8,128)(2,1)S(1)}, bf16[1,128,4096]{2,1,0:T(8,128)(2,1)}, u32[]{:S(2)}) copy-start(bf16[1,128,4096]{2,1,0:T(8,128)(2,1)} %param.15) | copy-start | bytes 3145732
  75.3 9.4 %collective-permute-start.7 = (bf16[32,48,128]{2,1,0:T(8,128)(2,1)S(1)}, bf16[32,48,128]{2,1,0:T(8,128)(2,1)S(1)}, u32[]{:S(2)}, u32[]{:S(2)}) collective-permute-start(bf16[32,48,128]{2,1,0:T(8,128)(2,1)S(1)} %get-tuple-element.37), channel_id=1, source_target_pairs={{0,32},{32,0},{1,33},{33,1},{2,34},{34,2},{3,35},{35,3},{4,36},{36... | collective-permute-start | bytes 1179656 | tf_op jit(solution)/shard_map/ppermute | solution.py:343
  136.1 8.5 %collective-permute-start.8 = (bf16[32,48,128]{2,1,0:T(8,128)(2,1)S(1)}, bf16[32,48,128]{2,1,0:T(8,128)(2,1)S(1)}, u32[]{:S(2)}, u32[]{:S(2)}) collective-permute-start(bf16[32,48,128]{2,1,0:T(8,128)(2,1)S(1)} %all_to_all.23.kept_ref), channel_id=1, source_target_pairs={{0,32},{32,0},{1,33},{33,1},{2,34},{34,2},{3,35},{35,3},{4,36},{36... | collective-permute-start | bytes 1179656 | tf_op jit(solution)/shard_map/ppermute | solution.py:351

commit v4 on v3

--- a/solution.py
+++ b/solution.py
@@ -55,23 +55,13 @@
     )
 
 
-def query_kernel(low_any, query_any, query_up_any, outgrad_any, out_up_any, frozen_any, out_down_any,
-                 q_ref, grad_ref, back_out_ref,
-                 low_ref, query_ref, query_up_ref, outgrad_ref, out_up_ref, frozen_ref, out_down_ref, sems):
-    pairs = ((outgrad_any, outgrad_ref), (out_up_any, out_up_ref), (low_any, low_ref), (query_up_any, query_up_ref),
-             (query_any, query_ref), (out_down_any, out_down_ref), (frozen_any, frozen_ref))
-    copies = [pltpu.make_async_copy(a, b, sems.at[i]) for i, (a, b) in enumerate(pairs)]
-    for copy in copies:
-        copy.start()
-    for copy in copies[:5]:
-        copy.wait()
-    back_out = dot(out_up_ref[...], outgrad_ref[...], NT).astype(BF)
-    back_out_ref[...] = back_out
+def query_kernel(low_ref, query_ref, query_up_ref, outgrad_ref, out_up_ref, frozen_ref, out_down_ref,
+                 q_ref, grad_ref, back_out_ref):
     q_ref[...] = (
         query_ref[...].astype(F32) + 0.5 * dot(low_ref[pl.ds(0, RANK), :], query_up_ref[...], TN)
     ).astype(BF)
-    for copy in copies[5:]:
-        copy.wait()
+    back_out = dot(out_up_ref[...], outgrad_ref[...], NT).astype(BF)
+    back_out_ref[...] = back_out
     grad_ref[...] = (
         frozen_ref[...].astype(F32) + 0.5 * dot(back_out, out_down_ref[...], TN)
     ).astype(BF)
@@ -279,31 +269,17 @@
 
     blocks = {0: pack}
     up, down = chain_pairs(length)
-    for step in range(1, 3):
+    for step in range(1, 5):
         blocks[step] = lax.ppermute(blocks[step - 1], seq, up[step - 1])
-        blocks[8 - step] = lax.ppermute(blocks[(9 - step) % SPAN], seq, down[step - 1])
+        if step < 4:
+            blocks[8 - step] = lax.ppermute(blocks[(9 - step) % SPAN], seq, down[step - 1])
 
     q, grad, back_out = call(
         query_kernel, "query",
         (shape((ROWS, QUERY_COLUMNS)), shape((ROWS, QUERY_COLUMNS)), shape((RANK, ROWS))),
         (low, frozen_query_state[0], query_up_weight, outgrad, output_up_weight, frozen_output_gradient[0], out_down),
-        scratch=(
-            pltpu.VMEM((3 * RANK, ROWS), BF),
-            pltpu.VMEM((ROWS, QUERY_COLUMNS), BF),
-            pltpu.VMEM((RANK, QUERY_COLUMNS), BF),
-            pltpu.VMEM((ROWS, WIDTH), BF),
-            pltpu.VMEM((RANK, WIDTH), BF),
-            pltpu.VMEM((ROWS, QUERY_COLUMNS), BF),
-            pltpu.VMEM((RANK, QUERY_COLUMNS), BF),
-            pltpu.SemaphoreType.DMA((7,)),
-        ),
-        flops=10**8, size=4 * 10**6, limit=56 << 20, kind=pl.BlockSpec(memory_space=pl.ANY),
-    )
-
-    blocks[2], _ = lax.optimization_barrier((blocks[2], back_out))
-    blocks[3] = lax.ppermute(blocks[2], seq, up[2])
-    blocks[5] = lax.ppermute(blocks[6], seq, down[2])
-    blocks[4] = lax.ppermute(blocks[3], seq, up[3])
+        flops=10**8, size=4 * 10**6,
+    )
 
     window = SPAN * ROWS
     parts, back_query, low_out, query_term, keyval_term, out_term = call(

time: 146 us -> 144 us (0.986)
  starting transfers between devices: 42 us -> 39.7 us
  Pallas kernels: 17.3 us -> 15.1 us
    ppermute x3 -> x0, starting transfers between devices: 8.79 us -> none  [the longest x1 7.43 us: per_device(): blocks[5] = lax.ppermute(blocks[6], seq, down[2])]
    ppermute x2 -> x3, starting transfers between devices: 13.3 us -> 18.4 us  [per_device(): lax.ppermute(blocks[(9 - step) % SPAN], seq, down[step - 1])]
    ppermute x2 -> x3, waiting for transfers between devices: 5.37 us -> 8.92 us  [per_device(): lax.ppermute(blocks[(9 - step) % SPAN], seq, down[step - 1])]
    ppermute x3 -> x0, waiting for transfers between devices: 2.94 us -> none  [the longest x1 2.93 us: per_device(): blocks[5] = lax.ppermute(blocks[6], seq, down[2])]
    pallas_call x5, Pallas kernels: 17.3 us -> 15.1 us  [call(): pl.pallas_call(kernel, name=name, out_shape=outs, in_specs=specs, out_spe...]
    ppermute x2 -> x4, starting transfers between devices: 4.73 us -> 6.09 us  [per_device(): blocks[step] = lax.ppermute(blocks[step - 1], seq, up[step - 1])]
    unnamed x20 -> x24, local copies, waits for them, and re-layouts: 2.12 us -> 3.45 us
  transfers between devices with their start and end apart: 9 -> 9, of which waited for: 5 -> 4; matrix products, arithmetic and copies ran while one was open for 0% -> 0% of each run, Pallas kernels for 2% -> 1%
where the time goes in v4:
time: 144 us; the launch traced here: 143 us
  blocking collectives  72 us (50%)
  starting transfers between devices  39.7 us (28%)
  Pallas kernels  15.1 us (10%)
  waiting for transfers between devices  11.6 us (8%)
  local copies, waits for them, and re-layouts  3.52 us (2%)
    all_to_all x1, blocking collectives, per_device(): parts = lax.all_to_all(parts, seq, 0, 0, tiled=False)  20.9 us
    ppermute x3, starting transfers between devices, per_device(): lax.ppermute(blocks[(9 - step) % SPAN], seq, down[step - 1])  18.4 us
    all_to_all x1, blocking collectives, per_device(): lax.all_to_all(jnp.broadcast_to(total, half), seq, 0, 0, tiled=False)  17.7 us
    all_to_all x1, blocking collectives, per_device(): lax.all_to_all(jnp.broadcast_to(total, (depth, *total.shape)), 'z', 0, 0,...  17.4 us
    all_to_all x1, blocking collectives, per_device(): total = lax.all_to_all(total, seq, 0, 0, tiled=False)  16 us
    pallas_call x5, Pallas kernels, call(): pl.pallas_call(kernel, name=name, out_shape=outs, in_specs=specs, out_spe...  15.1 us
    ppermute x3, waiting for transfers between devices, per_device(): lax.ppermute(blocks[(9 - step) % SPAN], seq, down[step - 1])  8.92 us
    ppermute x1, starting transfers between devices, per_device(): lax.ppermute(sent, 'core', swap).astype(F32)  8.03 us
  transfers between devices with their start and end apart: 9, of which 4 were waited for; matrix products, arithmetic and copies ran while one was open for 0% of the time, Pallas kernels for 1%

profile of v4, /device:TPU:1, one launch (start us, length us, event | category | flops | bytes accessed | tf_op | source)
XLA Modules:
  0.0 143.0 jit_solution(5651014942128975455)
XLA Ops:
  0.7 3.0 %keyval.1 = (bf16[48,128]{1,0:T(8,128)(2,1)}, bf16[144,1024]{1,0:T(8,128)(2,1)}) custom-call(bf16[128,4096]{1,0:T(8,128)(2,1)} %bitcast.11, bf16[48,4096]{1,0:T(8,128)(2,1)} %bitcast.19, bf16[128,1024]{1,0:T(8,128)(2,1)} %bitcast.20, bf16[2,16,512]{2,1,0:T(8,128)(2,1)} %up_ref.1, s32[1,128]{1,0:T(1,128)} %doc_any.1), custom_call_target="tpu_custom_call" | custom-call | flops 100000000 | bytes 2000000 | tf_op jit(solution)/shard_map/keyval/pallas_call | solution.py:208
  3.7 4.1 %collective-permute-start = (bf16[144,1024]{1,0:T(8,128)(2,1)}, bf16[144,1024]{1,0:T(8,128)(2,1)S(1)}, u32[]{:S(2)}, u32[]{:S(2)}) collective-permute-start(bf16[144,1024]{1,0:T(8,128)(2,1)} %get-tuple-element.27.rest_0_), channel_id=1, source_target_pairs={{0,1},{1,2},{2,3},{3,4},{4,5},{5,6},{6,7},{7,8},{8,9},{9,10},{10,1... | collective-permute-start | bytes 884744 | tf_op jit(solution)/shard_map/ppermute | solution.py:273
  7.7 4.2 %collective-permute-start.4 = (bf16[144,1024]{1,0:T(8,128)(2,1)}, bf16[144,1024]{1,0:T(8,128)(2,1)S(1)}, u32[]{:S(2)}, u32[]{:S(2)}) collective-permute-start(bf16[144,1024]{1,0:T(8,128)(2,1)} %get-tuple-element.27.rest_0_), channel_id=1, source_target_pairs={{0,7},{1,8},{2,9},{3,10},{4,11},{5,12},{6,13},{7,14},{8,15},{9,16}... | collective-permute-start | bytes 884744 | tf_op jit(solution)/shard_map/ppermute | solution.py:275
  11.9 0.0 collective-permute-done.rest_1_
  12.0 0.7 collective-permute-start.1
  12.6 4.9 %collective-permute-done.4.rest_7_ = bf16[144,1024]{1,0:T(8,128)(2,1)S(1)} collective-permute-done((bf16[144,1024]{1,0:T(8,128)(2,1)}, bf16[144,1024]{1,0:T(8,128)(2,1)S(1)}, u32[]{:S(2)}, u32[]{:S(2)}) %collective-permute-start.4) | collective-permute-done | bytes 294944 | tf_op jit(solution)/shard_map/ppermute | solution.py:275
  17.5 6.8 %collective-permute-start.5 = (bf16[144,1024]{1,0:T(8,128)(2,1)S(1)}, bf16[144,1024]{1,0:T(8,128)(2,1)S(1)}, u32[]{:S(2)}, u32[]{:S(2)}) collective-permute-start(bf16[144,1024]{1,0:T(8,128)(2,1)S(1)} %collective-permute-done.4.rest_7_), channel_id=1, source_target_pairs={{0,31},{1,0},{7,6},{8,7},{9,8},{10,9},{11,10},{12,11},{13,12},{14,... | collective-permute-start | bytes 884744 | tf_op jit(solution)/shard_map/ppermute | solution.py:275
  24.3 0.7 collective-permute-start.2
  25.0 4.0 %collective-permute-done.5.rest_6_ = bf16[144,1024]{1,0:T(8,128)(2,1)S(1)} collective-permute-done((bf16[144,1024]{1,0:T(8,128)(2,1)S(1)}, bf16[144,1024]{1,0:T(8,128)(2,1)S(1)}, u32[]{:S(2)}, u32[]{:S(2)}) %collective-permute-start.5) | collective-permute-done | bytes 294944 | tf_op jit(solution)/shard_map/ppermute | solution.py:275
  29.0 7.4 %collective-permute-start.6 = (bf16[144,1024]{1,0:T(8,128)(2,1)S(1)}, bf16[144,1024]{1,0:T(8,128)(2,1)S(1)}, u32[]{:S(2)}, u32[]{:S(2)}) collective-permute-start(bf16[144,1024]{1,0:T(8,128)(2,1)S(1)} %collective-permute-done.5.rest_6_), channel_id=1, source_target_pairs={{0,31},{6,5},{7,6},{8,7},{9,8},{10,9},{11,10},{12,11},{13,12},{14,... | collective-permute-start | bytes 884744 | tf_op jit(solution)/shard_map/ppermute | solution.py:275
  36.5 0.7 collective-permute-start.3
  37.2 0.0 copy-start.3
  37.2 1.0 copy-done.3
  38.2 0.8 copy-done.5
  39.1 0.8 copy-done.7
  39.9 0.7 copy-done.10
  40.6 1.1 query.1
  41.8 0.0 copy-start
  41.9 9.6 %attention.1 = (bf16[32,32,128]{2,1,0:T(8,128)(2,1)S(1)}, bf16[16,128]{1,0:T(8,128)(2,1)S(1)}, bf16[16,128]{1,0:T(8,128)(2,1)S(1)}, f32[16,2048]{1,0:T(8,128)S(1...) custom-call(bf16[48,128]{1,0:T(8,128)(2,1)S(1)} %copy-done.10, bf16[128,2048]{1,0:T(8,128)(2,1)S(1)} %get-tuple-element.24.q_ref, ...), custom_call_target="tpu_custom_call" | custom-call | flops 4000000000 | bytes 4000000 | tf_op jit(solution)/shard_map/attention/pallas_call | solution.py:208
  51.4 20.9 %all_to_all.20.parts_ref = bf16[32,32,128]{2,1,0:T(8,128)(2,1)S(1)} all-to-all(bf16[32,32,128]{2,1,0:T(8,128)(2,1)S(1)} %get-tuple-element.29), channel_id=1, replica_groups=mesh['z'=8,'core'=2,'x'=4,'y'=8] {'x','y'}, dimensions={0} | all-to-all | bytes 524288 | tf_op jit(solution)/shard_map/all_to_all | solution.py:308
  72.3 0.4 terms.1
  72.7 8.0 %collective-permute-start.7 = (bf16[32,48,128]{2,1,0:T(8,128)(2,1)S(1)}, bf16[32,48,128]{2,1,0:T(8,128)(2,1)S(1)}, u32[]{:S(2)}, u32[]{:S(2)}) collective-permute-start(bf16[32,48,128]{2,1,0:T(8,128)(2,1)S(1)} %get-tuple-element.35), channel_id=1, source_target_pairs={{0,32},{32,0},{1,33},{33,1},{2,34},{34,2},{3,35},{35,3},{4,36},{36... | collective-permute-start | bytes 1179656 | tf_op jit(solution)/shard_map/ppermute | solution.py:319
  80.8 1.3 collective-permute-done.7
  82.1 0.1 add_convert_fusion
  82.2 16.0 %all_to_all.21 = bf16[32,48,128]{2,1,0:T(8,128)(2,1)S(1)} all-to-all(bf16[32,48,128]{2,1,0:T(8,128)(2,1)S(1)} %add_convert_fusion), channel_id=1, replica_groups=mesh['z'=8,'core'=2,'x'=4,'y'=8] {'x','y'}, dimensions={0} | all-to-all | bytes 786432 | tf_op jit(solution)/shard_map/all_to_all | solution.py:320
  98.2 0.1 reduce_sum.21
  98.3 17.4 %all_to_all.22 = bf16[8,48,128]{2,1,0:T(8,128)(2,1)S(1)} all-to-all(bf16[8,48,128]{2,1,0:T(8,128)(2,1)S(1)} %broadcast_in_dim.6), channel_id=1, replica_groups=mesh['z'=8,'core'=2,'x'=4,'y'=8] {'z'}, dimensions={0} | all-to-all | bytes 196608 | tf_op jit(solution)/shard_map/all_to_all | solution.py:323
  115.7 0.1 broadcast_in_dim.7
  115.8 17.7 %all_to_all.23.kept_ref = bf16[32,48,128]{2,1,0:T(8,128)(2,1)S(1)} all-to-all(bf16[32,48,128]{2,1,0:T(8,128)(2,1)S(1)} %broadcast_in_dim.7), channel_id=1, replica_groups=mesh['z'=8,'core'=2,'x'=4,'y'=8] {'x','y'}, dimensions={0} | all-to-all | bytes 786432 | tf_op jit(solution)/shard_map/all_to_all | solution.py:326
  133.5 7.2 %collective-permute-start.8 = (bf16[32,48,128]{2,1,0:T(8,128)(2,1)S(1)}, bf16[32,48,128]{2,1,0:T(8,128)(2,1)S(1)}, u32[]{:S(2)}, u32[]{:S(2)}) collective-permute-start(bf16[32,48,128]{2,1,0:T(8,128)(2,1)S(1)} %all_to_all.23.kept_ref), channel_id=1, source_target_pairs={{0,32},{32,0},{1,33},{33,1},{2,34},{34,2},{3,35},{35,3},{4,36},{36... | collective-permute-start | bytes 1179656 | tf_op jit(solution)/shard_map/ppermute | solution.py:327
  140.7 1.3 collective-permute-done.8.sent_ref
  142.0 1.0 unpack.1
  (25 shorter events, 0.1 us)
Async XLA Ops:
  0.6 36.5 %copy-start.1 = (bf16[1,128,4096]{2,1,0:T(8,128)(2,1)S(1)}, bf16[1,128,4096]{2,1,0:T(8,128)(2,1)}, u32[]{:S(2)}) copy-start(bf16[1,128,4096]{2,1,0:T(8,128)(2,1)} %param.15) | copy-start | bytes 3145732
  0.6 36.5 %copy-start.2 = (bf16[1,128,2048]{2,1,0:T(8,128)(2,1)S(1)}, bf16[1,128,2048]{2,1,0:T(8,128)(2,1)}, u32[]{:S(2)}) copy-start(bf16[1,128,2048]{2,1,0:T(8,128)(2,1)} %param.13) | copy-start | bytes 1572868
  0.7 36.5 %copy-start.4 = (bf16[16,4096]{1,0:T(8,128)(2,1)S(1)}, bf16[16,4096]{1,0:T(8,128)(2,1)}, u32[]{:S(2)}) copy-start(bf16[16,4096]{1,0:T(8,128)(2,1)} %out_up_ref.1) | copy-start | bytes 393220
  3.7 8.3 %collective-permute-start = (bf16[144,1024]{1,0:T(8,128)(2,1)}, bf16[144,1024]{1,0:T(8,128)(2,1)S(1)}, u32[]{:S(2)}, u32[]{:S(2)}) collective-permute-start(bf16[144,1024]{1,0:T(8,128)(2,1)} %get-tuple-element.27.rest_0_), channel_id=1, source_target_pairs={{0,1},{1,2},{2,3},{3,4},{4,5},{5,6},{6,7},{7,8},{8,9},{9,10},{10,1... | collective-permute-start | bytes 884744 | tf_op jit(solution)/shard_map/ppermute | solution.py:273
  7.7 9.8 %collective-permute-start.4 = (bf16[144,1024]{1,0:T(8,128)(2,1)}, bf16[144,1024]{1,0:T(8,128)(2,1)S(1)}, u32[]{:S(2)}, u32[]{:S(2)}) collective-permute-start(bf16[144,1024]{1,0:T(8,128)(2,1)} %get-tuple-element.27.rest_0_), channel_id=1, source_target_pairs={{0,7},{1,8},{2,9},{3,10},{4,11},{5,12},{6,13},{7,14},{8,15},{9,16}... | collective-permute-start | bytes 884744 | tf_op jit(solution)/shard_map/ppermute | solution.py:275
  12.0 12.3 %collective-permute-start.1 = (bf16[144,1024]{1,0:T(8,128)(2,1)S(1)}, bf16[144,1024]{1,0:T(8,128)(2,1)S(1)}, u32[]{:S(2)}, u32[]{:S(2)}) collective-permute-start(bf16[144,1024]{1,0:T(8,128)(2,1)S(1)} %collective-permute-done.rest_1_), channel_id=1, source_target_pairs={{1,2},{2,3},{3,4},{4,5},{5,6},{6,7},{7,8},{8,9},{9,10},{10,11},{11... | collective-permute-start | bytes 884744 | tf_op jit(solution)/shard_map/ppermute | solution.py:273
  17.5 11.5 %collective-permute-start.5 = (bf16[144,1024]{1,0:T(8,128)(2,1)S(1)}, bf16[144,1024]{1,0:T(8,128)(2,1)S(1)}, u32[]{:S(2)}, u32[]{:S(2)}) collective-permute-start(bf16[144,1024]{1,0:T(8,128)(2,1)S(1)} %collective-permute-done.4.rest_7_), channel_id=1, source_target_pairs={{0,31},{1,0},{7,6},{8,7},{9,8},{10,9},{11,10},{12,11},{13,12},{14,... | collective-permute-start | bytes 884744 | tf_op jit(solution)/shard_map/ppermute | solution.py:275
  24.3 12.2 %collective-permute-start.2 = (bf16[144,1024]{1,0:T(8,128)(2,1)S(1)}, bf16[144,1024]{1,0:T(8,128)(2,1)S(1)}, u32[]{:S(2)}, u32[]{:S(2)}) collective-permute-start(bf16[144,1024]{1,0:T(8,128)(2,1)S(1)} %collective-permute-done.1.rest_2_), channel_id=1, source_target_pairs={{2,3},{3,4},{4,5},{5,6},{6,7},{7,8},{8,9},{9,10},{10,11},{11,12},{... | collective-permute-start | bytes 884744 | tf_op jit(solution)/shard_map/ppermute | solution.py:273
  29.0 12.8 %collective-permute-start.6 = (bf16[144,1024]{1,0:T(8,128)(2,1)S(1)}, bf16[144,1024]{1,0:T(8,128)(2,1)S(1)}, u32[]{:S(2)}, u32[]{:S(2)}) collective-permute-start(bf16[144,1024]{1,0:T(8,128)(2,1)S(1)} %collective-permute-done.5.rest_6_), channel_id=1, source_target_pairs={{0,31},{6,5},{7,6},{8,7},{9,8},{10,9},{11,10},{12,11},{13,12},{14,... | collective-permute-start | bytes 884744 | tf_op jit(solution)/shard_map/ppermute | solution.py:275
  36.5 5.3 %collective-permute-start.3 = (bf16[144,1024]{1,0:T(8,128)(2,1)S(1)}, bf16[144,1024]{1,0:T(8,128)(2,1)S(1)}, u32[]{:S(2)}, u32[]{:S(2)}) collective-permute-start(bf16[144,1024]{1,0:T(8,128)(2,1)S(1)} %collective-permute-done.2.rest_3_), channel_id=1, source_target_pairs={{3,4},{4,5},{5,6},{6,7},{7,8},{8,9},{9,10},{10,11},{11,12},{12,13}... | collective-permute-start | bytes 884744 | tf_op jit(solution)/shard_map/ppermute | solution.py:273
  37.2 1.0 copy-start.3
  38.2 0.8 copy-start.5
  39.1 0.8 copy-start.7
  39.9 0.7 copy-start.10
  40.6 1.2 copy-start.6
  40.6 1.2 copy-start.8
  40.6 1.2 copy-start.9
  40.6 1.2 copy-start.11
  41.8 30.4 %copy-start = (bf16[1,128,4096]{2,1,0:T(8,128)(2,1)S(1)}, bf16[1,128,4096]{2,1,0:T(8,128)(2,1)}, u32[]{:S(2)}) copy-start(bf16[1,128,4096]{2,1,0:T(8,128)(2,1)} %param.11) | copy-start | bytes 3145732
  72.7 9.4 %collective-permute-start.7 = (bf16[32,48,128]{2,1,0:T(8,128)(2,1)S(1)}, bf16[32,48,128]{2,1,0:T(8,128)(2,1)S(1)}, u32[]{:S(2)}, u32[]{:S(2)}) collective-permute-start(bf16[32,48,128]{2,1,0:T(8,128)(2,1)S(1)} %get-tuple-element.35), channel_id=1, source_target_pairs={{0,32},{32,0},{1,33},{33,1},{2,34},{34,2},{3,35},{35,3},{4,36},{36... | collective-permute-start | bytes 1179656 | tf_op jit(solution)/shard_map/ppermute | solution.py:319
  133.5 8.5 %collective-permute-start.8 = (bf16[32,48,128]{2,1,0:T(8,128)(2,1)S(1)}, bf16[32,48,128]{2,1,0:T(8,128)(2,1)S(1)}, u32[]{:S(2)}, u32[]{:S(2)}) collective-permute-start(bf16[32,48,128]{2,1,0:T(8,128)(2,1)S(1)} %all_to_all.23.kept_ref), channel_id=1, source_target_pairs={{0,32},{32,0},{1,33},{33,1},{2,34},{34,2},{3,35},{35,3},{4,36},{36... | collective-permute-start | bytes 1179656 | tf_op jit(solution)/shard_map/ppermute | solution.py:327

commit v5 on v4

--- a/solution.py
+++ b/solution.py
@@ -73,6 +73,8 @@
     parts_ref, back_query_ref, low_out_ref, query_term_ref, keyval_term_ref, out_term_ref = rest[SPAN : SPAN + 6]
     bias, keys, values, low_keys, low_values, back_parts = rest[SPAN + 6 :]
     position = lax.axis_index("x") * SPAN + lax.axis_index("y")
+    core = lax.axis_index("core")
+    offsets = [0] + [s + core * (SPAN - 2 * s) for s in (1, 2, 3, 4)] + [SPAN - s + core * (2 * s - SPAN) for s in (1, 2, 3)]
     own = blocks[0][pl.ds(ROWS, RANK), pl.ds(2 * ROWS, ROWS)][:1]
     own = jnp.broadcast_to(own.astype(F32), (ROWS, ROWS))
     row = lax.broadcasted_iota(jnp.int32, (ROWS, ROWS), 0)
@@ -87,7 +89,7 @@
         if o == 0:
             seen = seen & (row <= col)
         else:
-            seen = seen & (jnp.broadcast_to(position, (ROWS, ROWS)) >= o)
+            seen = seen & (jnp.broadcast_to(position - offsets[o], (ROWS, ROWS)) >= 0)
         one = jnp.where(seen, 0.0, -1e30)
         for i in range(GROUP):
             bias[span, pl.ds(i*ROWS, ROWS)] = one
@@ -140,7 +142,7 @@
     low_out_ref[...] = low_out.astype(BF)
     parts_ref[...] = jnp.zeros_like(parts_ref)
     for o in range(SPAN):
-        parts_ref[lax.rem(position + (DEVICES - o), DEVICES)] = back_parts[:, pl.ds(o * ROWS, ROWS)].astype(BF)
+        parts_ref[lax.rem(position + (DEVICES - offsets[o]), DEVICES)] = back_parts[:, pl.ds(o * ROWS, ROWS)].astype(BF)
 
 
 def term_kernel(x_ref, outgrad_ref, back_query_ref, parts_ref, low_out_ref,
@@ -221,16 +223,22 @@
     return jax.ShapeDtypeStruct(dims, dtype)
 
 
-def chain_pairs(length):
-    up = [[(i, i + 1) for i in range(step, length - 1)] for step in range(SPAN // 2)]
-    down, wanted = [], {(place - 5, place) for place in range(5, length)}
-    for _ in range(2):
-        down.insert(0, sorted(((place + 1) % length, place) for _, place in wanted))
-        earlier = {(block, (place + 1) % length) for block, place in wanted}
-        offset = 5 + len(down)
-        wanted = earlier | {(place - offset, place) for place in range(offset, length)}
-    down.insert(0, sorted(wanted))
-    return up, down
+def pairs_up(length, steps):
+    return [[(i, i + 1) for i in range(step, length - 1)] for step in range(steps)]
+
+
+def pairs_down(length, steps):
+    last = SPAN - steps
+    pairs, wanted = [], {(place - last, place) for place in range(last, length)}
+    for offset in range(last + 1, SPAN):
+        pairs.insert(0, sorted(((place + 1) % length, place) for _, place in wanted))
+        wanted = {(block, (place + 1) % length) for block, place in wanted}
+        wanted |= {(place - offset, place) for place in range(offset, length)}
+    return [sorted(wanted)] + pairs
+
+
+def both_cores(length, first, second):
+    return [a + [(i + length, j + length) for i, j in b] for a, b in zip(first, second, strict=True)]
 
 
 def per_device(
@@ -267,12 +275,16 @@
         flops=10**8, size=2 * 10**6, limit=56 << 20, kind=pl.BlockSpec(memory_space=pl.ANY),
     )
 
-    blocks = {0: pack}
-    up, down = chain_pairs(length)
-    for step in range(1, 5):
-        blocks[step] = lax.ppermute(blocks[step - 1], seq, up[step - 1])
-        if step < 4:
-            blocks[8 - step] = lax.ppermute(blocks[(9 - step) % SPAN], seq, down[step - 1])
+    half_span = SPAN // 2
+    long = both_cores(length, pairs_up(length, half_span), pairs_down(length, half_span))
+    short = both_cores(length, pairs_down(length, half_span - 1), pairs_up(length, half_span - 1))
+    places = ("core", *seq)
+    first, second = [pack], [pack]
+    for step in range(half_span):
+        first.append(lax.ppermute(first[-1], places, long[step]))
+        if step < half_span - 1:
+            second.append(lax.ppermute(second[-1], places, short[step]))
+    blocks = first + second[1:]
 
     q, grad, back_out = call(
         query_kernel, "query",
@@ -293,7 +305,7 @@
             shape((RANK, QUERY_COLUMNS), F32),
         ),
         (low, q, grad, back_out, query_up_weight, keyvalue_up_weight, out_down,
-         *[blocks[o] for o in range(SPAN)]),
+         *blocks),
         scratch=(
             pltpu.VMEM((window, GROUP * ROWS), F32),
             pltpu.VMEM((window, HEAD_SIZE), BF),

time: 144 us -> 147 us (1.021)
  starting transfers between devices: 39.7 us -> 48 us
  blocking collectives: 72 us -> 66.4 us
    ppermute x7, starting transfers between devices: 24.5 us -> 30.3 us  [the longest x4 27.6 us: per_device(): first.append(lax.ppermute(first[-1], places, long[step]))]
    all_to_all x1, blocking collectives: 20.9 us -> 15.3 us  [per_device(): parts = lax.all_to_all(parts, seq, 0, 0, tiled=False)]
    ppermute x1, starting transfers between devices: 8.03 us -> 10.6 us  [per_device(): lax.ppermute(sent, 'core', swap).astype(F32)]
  transfers between devices with their start and end apart: 9 -> 9, of which waited for: 4 -> 5; matrix products, arithmetic and copies ran while one was open for 0% -> 0% of each run, Pallas kernels for 1% -> 1%
where the time goes in v5:
time: 147 us; the launch traced here: 146 us
  blocking collectives  66.4 us (45%)
  starting transfers between devices  48 us (33%)
  Pallas kernels  15.2 us (10%)
  waiting for transfers between devices  11.9 us (8%)
  local copies, waits for them, and re-layouts  3.52 us (2%)
    ppermute x4, starting transfers between devices, per_device(): first.append(lax.ppermute(first[-1], places, long[step]))  27.6 us
    all_to_all x1, blocking collectives, per_device(): lax.all_to_all(jnp.broadcast_to(total, half), seq, 0, 0, tiled=False)  17.7 us
    all_to_all x1, blocking collectives, per_device(): lax.all_to_all(jnp.broadcast_to(total, (depth, *total.shape)), 'z', 0, 0,...  17.4 us
    all_to_all x1, blocking collectives, per_device(): total = lax.all_to_all(total, seq, 0, 0, tiled=False)  16 us
    all_to_all x1, blocking collectives, per_device(): parts = lax.all_to_all(parts, seq, 0, 0, tiled=False)  15.3 us
    pallas_call x5, Pallas kernels, call(): pl.pallas_call(kernel, name=name, out_shape=outs, in_specs=specs, out_spe...  15.2 us
    ppermute x1, starting transfers between devices, per_device(): lax.ppermute(sent, 'core', swap).astype(F32)  10.6 us
    ppermute x4, waiting for transfers between devices, per_device(): first.append(lax.ppermute(first[-1], places, long[step]))  9.19 us
  transfers between devices with their start and end apart: 9, of which 5 were waited for; matrix products, arithmetic and copies ran while one was open for 0% of the time, Pallas kernels for 1%

profile of v5, /device:TPU:1, one launch (start us, length us, event | category | flops | bytes accessed | tf_op | source)
XLA Modules:
  0.0 146.1 jit_solution(15537172719760925681)
XLA Ops:
  0.7 3.0 %keyval.1 = (bf16[48,128]{1,0:T(8,128)(2,1)}, bf16[144,1024]{1,0:T(8,128)(2,1)}) custom-call(bf16[128,4096]{1,0:T(8,128)(2,1)} %bitcast.11, bf16[48,4096]{1,0:T(8,128)(2,1)} %bitcast.19, bf16[128,1024]{1,0:T(8,128)(2,1)} %bitcast.20, bf16[2,16,512]{2,1,0:T(8,128)(2,1)} %up_ref.1, s32[1,128]{1,0:T(1,128)} %doc_any.1), custom_call_target="tpu_custom_call" | custom-call | flops 100000000 | bytes 2000000 | tf_op jit(solution)/shard_map/keyval/pallas_call | solution.py:210
  3.7 5.9 %collective-permute-start = (bf16[144,1024]{1,0:T(8,128)(2,1)}, bf16[144,1024]{1,0:T(8,128)(2,1)S(1)}, u32[]{:S(2)}, u32[]{:S(2)}) collective-permute-start(bf16[144,1024]{1,0:T(8,128)(2,1)} %get-tuple-element.27.rest_0_), channel_id=1, source_target_pairs={{0,1},{1,2},{2,3},{3,4},{4,5},{5,6},{6,7},{7,8},{8,9},{9,10},{10,1... | collective-permute-start | bytes 884744 | tf_op jit(solution)/shard_map/ppermute | solution.py:284
  9.6 1.3 collective-permute-start.4
  10.9 3.3 %collective-permute-done.rest_1_ = bf16[144,1024]{1,0:T(8,128)(2,1)S(1)} collective-permute-done((bf16[144,1024]{1,0:T(8,128)(2,1)}, bf16[144,1024]{1,0:T(8,128)(2,1)S(1)}, u32[]{:S(2)}, u32[]{:S(2)}) %collective-permute-start) | collective-permute-done | bytes 294944 | tf_op jit(solution)/shard_map/ppermute | solution.py:284
  14.2 7.4 %collective-permute-start.1 = (bf16[144,1024]{1,0:T(8,128)(2,1)S(1)}, bf16[144,1024]{1,0:T(8,128)(2,1)S(1)}, u32[]{:S(2)}, u32[]{:S(2)}) collective-permute-start(bf16[144,1024]{1,0:T(8,128)(2,1)S(1)} %collective-permute-done.rest_1_), channel_id=1, source_target_pairs={{1,2},{2,3},{3,4},{4,5},{5,6},{6,7},{7,8},{8,9},{9,10},{10,11},{11... | collective-permute-start | bytes 884744 | tf_op jit(solution)/shard_map/ppermute | solution.py:284
  21.7 0.7 collective-permute-start.5
  22.3 2.9 %collective-permute-done.1.rest_2_ = bf16[144,1024]{1,0:T(8,128)(2,1)S(1)} collective-permute-done((bf16[144,1024]{1,0:T(8,128)(2,1)S(1)}, bf16[144,1024]{1,0:T(8,128)(2,1)S(1)}, u32[]{:S(2)}, u32[]{:S(2)}) %collective-permute-start.1) | collective-permute-done | bytes 294944 | tf_op jit(solution)/shard_map/ppermute | solution.py:284
  25.3 7.1 %collective-permute-start.2 = (bf16[144,1024]{1,0:T(8,128)(2,1)S(1)}, bf16[144,1024]{1,0:T(8,128)(2,1)S(1)}, u32[]{:S(2)}, u32[]{:S(2)}) collective-permute-start(bf16[144,1024]{1,0:T(8,128)(2,1)S(1)} %collective-permute-done.1.rest_2_), channel_id=1, source_target_pairs={{2,3},{3,4},{4,5},{5,6},{6,7},{7,8},{8,9},{9,10},{10,11},{11,12},{... | collective-permute-start | bytes 884744 | tf_op jit(solution)/shard_map/ppermute | solution.py:284
  32.4 0.7 collective-permute-start.6
  33.1 2.9 %collective-permute-done.2.rest_3_ = bf16[144,1024]{1,0:T(8,128)(2,1)S(1)} collective-permute-done((bf16[144,1024]{1,0:T(8,128)(2,1)S(1)}, bf16[144,1024]{1,0:T(8,128)(2,1)S(1)}, u32[]{:S(2)}, u32[]{:S(2)}) %collective-permute-start.2) | collective-permute-done | bytes 294944 | tf_op jit(solution)/shard_map/ppermute | solution.py:284
  36.1 7.1 %collective-permute-start.3 = (bf16[144,1024]{1,0:T(8,128)(2,1)S(1)}, bf16[144,1024]{1,0:T(8,128)(2,1)S(1)}, u32[]{:S(2)}, u32[]{:S(2)}) collective-permute-start(bf16[144,1024]{1,0:T(8,128)(2,1)S(1)} %collective-permute-done.2.rest_3_), channel_id=1, source_target_pairs={{3,4},{4,5},{5,6},{6,7},{7,8},{8,9},{9,10},{10,11},{11,12},{12,13}... | collective-permute-start | bytes 884744 | tf_op jit(solution)/shard_map/ppermute | solution.py:284
  43.2 0.0 copy-start.3
  43.3 1.0 copy-done.3
  44.3 0.8 copy-done.5
  45.1 0.8 copy-done.7
  46.0 0.7 copy-done.10
  46.7 1.1 query.1
  47.9 0.0 copy-start
  47.9 9.6 %attention.1 = (bf16[32,32,128]{2,1,0:T(8,128)(2,1)S(1)}, bf16[16,128]{1,0:T(8,128)(2,1)S(1)}, bf16[16,128]{1,0:T(8,128)(2,1)S(1)}, f32[16,2048]{1,0:T(8,128)S(1...) custom-call(bf16[48,128]{1,0:T(8,128)(2,1)S(1)} %copy-done.10, bf16[128,2048]{1,0:T(8,128)(2,1)S(1)} %get-tuple-element.24.q_ref, ...), custom_call_target="tpu_custom_call" | custom-call | flops 4000000000 | bytes 4000000 | tf_op jit(solution)/shard_map/attention/pallas_call | solution.py:210
  57.5 15.3 %all_to_all.20.parts_ref = bf16[32,32,128]{2,1,0:T(8,128)(2,1)S(1)} all-to-all(bf16[32,32,128]{2,1,0:T(8,128)(2,1)S(1)} %get-tuple-element.29), channel_id=1, replica_groups=mesh['z'=8,'core'=2,'x'=4,'y'=8] {'x','y'}, dimensions={0} | all-to-all | bytes 524288 | tf_op jit(solution)/shard_map/all_to_all | solution.py:320
  72.8 0.4 terms.1
  73.3 10.6 %collective-permute-start.7 = (bf16[32,48,128]{2,1,0:T(8,128)(2,1)S(1)}, bf16[32,48,128]{2,1,0:T(8,128)(2,1)S(1)}, u32[]{:S(2)}, u32[]{:S(2)}) collective-permute-start(bf16[32,48,128]{2,1,0:T(8,128)(2,1)S(1)} %get-tuple-element.35), channel_id=1, source_target_pairs={{0,32},{32,0},{1,33},{33,1},{2,34},{34,2},{3,35},{35,3},{4,36},{36... | collective-permute-start | bytes 1179656 | tf_op jit(solution)/shard_map/ppermute | solution.py:331
  83.9 1.3 collective-permute-done.7
  85.2 0.1 add_convert_fusion
  85.4 16.0 %all_to_all.21 = bf16[32,48,128]{2,1,0:T(8,128)(2,1)S(1)} all-to-all(bf16[32,48,128]{2,1,0:T(8,128)(2,1)S(1)} %add_convert_fusion), channel_id=1, replica_groups=mesh['z'=8,'core'=2,'x'=4,'y'=8] {'x','y'}, dimensions={0} | all-to-all | bytes 786432 | tf_op jit(solution)/shard_map/all_to_all | solution.py:332
  101.3 0.1 reduce_sum.21
  101.4 17.4 %all_to_all.22 = bf16[8,48,128]{2,1,0:T(8,128)(2,1)S(1)} all-to-all(bf16[8,48,128]{2,1,0:T(8,128)(2,1)S(1)} %broadcast_in_dim.6), channel_id=1, replica_groups=mesh['z'=8,'core'=2,'x'=4,'y'=8] {'z'}, dimensions={0} | all-to-all | bytes 196608 | tf_op jit(solution)/shard_map/all_to_all | solution.py:335
  118.8 0.1 broadcast_in_dim.7
  118.9 17.7 %all_to_all.23.kept_ref = bf16[32,48,128]{2,1,0:T(8,128)(2,1)S(1)} all-to-all(bf16[32,48,128]{2,1,0:T(8,128)(2,1)S(1)} %broadcast_in_dim.7), channel_id=1, replica_groups=mesh['z'=8,'core'=2,'x'=4,'y'=8] {'x','y'}, dimensions={0} | all-to-all | bytes 786432 | tf_op jit(solution)/shard_map/all_to_all | solution.py:338
  136.6 7.2 %collective-permute-start.8 = (bf16[32,48,128]{2,1,0:T(8,128)(2,1)S(1)}, bf16[32,48,128]{2,1,0:T(8,128)(2,1)S(1)}, u32[]{:S(2)}, u32[]{:S(2)}) collective-permute-start(bf16[32,48,128]{2,1,0:T(8,128)(2,1)S(1)} %all_to_all.23.kept_ref), channel_id=1, source_target_pairs={{0,32},{32,0},{1,33},{33,1},{2,34},{34,2},{3,35},{35,3},{4,36},{36... | collective-permute-start | bytes 1179656 | tf_op jit(solution)/shard_map/ppermute | solution.py:339
  143.8 1.3 collective-permute-done.8.sent_ref
  145.1 1.0 unpack.1
  (25 shorter events, 0.1 us)
Async XLA Ops:
  0.6 42.6 %copy-start.1 = (bf16[1,128,4096]{2,1,0:T(8,128)(2,1)S(1)}, bf16[1,128,4096]{2,1,0:T(8,128)(2,1)}, u32[]{:S(2)}) copy-start(bf16[1,128,4096]{2,1,0:T(8,128)(2,1)} %param.15) | copy-start | bytes 3145732
  0.6 42.6 %copy-start.2 = (bf16[1,128,2048]{2,1,0:T(8,128)(2,1)S(1)}, bf16[1,128,2048]{2,1,0:T(8,128)(2,1)}, u32[]{:S(2)}) copy-start(bf16[1,128,2048]{2,1,0:T(8,128)(2,1)} %param.13) | copy-start | bytes 1572868
  0.7 42.6 %copy-start.4 = (bf16[16,4096]{1,0:T(8,128)(2,1)S(1)}, bf16[16,4096]{1,0:T(8,128)(2,1)}, u32[]{:S(2)}) copy-start(bf16[16,4096]{1,0:T(8,128)(2,1)} %out_up_ref.1) | copy-start | bytes 393220
  3.7 10.6 %collective-permute-start = (bf16[144,1024]{1,0:T(8,128)(2,1)}, bf16[144,1024]{1,0:T(8,128)(2,1)S(1)}, u32[]{:S(2)}, u32[]{:S(2)}) collective-permute-start(bf16[144,1024]{1,0:T(8,128)(2,1)} %get-tuple-element.27.rest_0_), channel_id=1, source_target_pairs={{0,1},{1,2},{2,3},{3,4},{4,5},{5,6},{6,7},{7,8},{8,9},{9,10},{10,1... | collective-permute-start | bytes 884744 | tf_op jit(solution)/shard_map/ppermute | solution.py:284
  9.6 12.0 %collective-permute-start.4 = (bf16[144,1024]{1,0:T(8,128)(2,1)}, bf16[144,1024]{1,0:T(8,128)(2,1)S(1)}, u32[]{:S(2)}, u32[]{:S(2)}) collective-permute-start(bf16[144,1024]{1,0:T(8,128)(2,1)} %get-tuple-element.27.rest_0_), channel_id=1, source_target_pairs={{0,7},{1,8},{2,9},{3,10},{4,11},{5,12},{6,13},{7,14},{8,15},{9,16}... | collective-permute-start | bytes 884744 | tf_op jit(solution)/shard_map/ppermute | solution.py:286
  14.2 11.1 %collective-permute-start.1 = (bf16[144,1024]{1,0:T(8,128)(2,1)S(1)}, bf16[144,1024]{1,0:T(8,128)(2,1)S(1)}, u32[]{:S(2)}, u32[]{:S(2)}) collective-permute-start(bf16[144,1024]{1,0:T(8,128)(2,1)S(1)} %collective-permute-done.rest_1_), channel_id=1, source_target_pairs={{1,2},{2,3},{3,4},{4,5},{5,6},{6,7},{7,8},{8,9},{9,10},{10,11},{11... | collective-permute-start | bytes 884744 | tf_op jit(solution)/shard_map/ppermute | solution.py:284
  21.7 10.8 %collective-permute-start.5 = (bf16[144,1024]{1,0:T(8,128)(2,1)S(1)}, bf16[144,1024]{1,0:T(8,128)(2,1)S(1)}, u32[]{:S(2)}, u32[]{:S(2)}) collective-permute-start(bf16[144,1024]{1,0:T(8,128)(2,1)S(1)} %collective-permute-done.4.rest_5_), channel_id=1, source_target_pairs={{0,31},{1,0},{7,6},{8,7},{9,8},{10,9},{11,10},{12,11},{13,12},{14,... | collective-permute-start | bytes 884744 | tf_op jit(solution)/shard_map/ppermute | solution.py:286
  25.3 10.8 %collective-permute-start.2 = (bf16[144,1024]{1,0:T(8,128)(2,1)S(1)}, bf16[144,1024]{1,0:T(8,128)(2,1)S(1)}, u32[]{:S(2)}, u32[]{:S(2)}) collective-permute-start(bf16[144,1024]{1,0:T(8,128)(2,1)S(1)} %collective-permute-done.1.rest_2_), channel_id=1, source_target_pairs={{2,3},{3,4},{4,5},{5,6},{6,7},{7,8},{8,9},{9,10},{10,11},{11,12},{... | collective-permute-start | bytes 884744 | tf_op jit(solution)/shard_map/ppermute | solution.py:284
  32.4 15.4 %collective-permute-start.6 = (bf16[144,1024]{1,0:T(8,128)(2,1)S(1)}, bf16[144,1024]{1,0:T(8,128)(2,1)S(1)}, u32[]{:S(2)}, u32[]{:S(2)}) collective-permute-start(bf16[144,1024]{1,0:T(8,128)(2,1)S(1)} %collective-permute-done.5.rest_6_), channel_id=1, source_target_pairs={{0,31},{6,5},{7,6},{8,7},{9,8},{10,9},{11,10},{12,11},{13,12},{14,... | collective-permute-start | bytes 884744 | tf_op jit(solution)/shard_map/ppermute | solution.py:286
  36.1 11.8 %collective-permute-start.3 = (bf16[144,1024]{1,0:T(8,128)(2,1)S(1)}, bf16[144,1024]{1,0:T(8,128)(2,1)S(1)}, u32[]{:S(2)}, u32[]{:S(2)}) collective-permute-start(bf16[144,1024]{1,0:T(8,128)(2,1)S(1)} %collective-permute-done.2.rest_3_), channel_id=1, source_target_pairs={{3,4},{4,5},{5,6},{6,7},{7,8},{8,9},{9,10},{10,11},{11,12},{12,13}... | collective-permute-start | bytes 884744 | tf_op jit(solution)/shard_map/ppermute | solution.py:284
  43.2 1.0 copy-start.3
  44.3 0.8 copy-start.5
  45.1 0.8 copy-start.7
  46.0 0.7 copy-start.10
  46.7 1.2 copy-start.6
  46.7 1.2 copy-start.8
  46.7 1.2 copy-start.9
  46.7 1.2 copy-start.11
  47.9 24.9 %copy-start = (bf16[1,128,4096]{2,1,0:T(8,128)(2,1)S(1)}, bf16[1,128,4096]{2,1,0:T(8,128)(2,1)}, u32[]{:S(2)}) copy-start(bf16[1,128,4096]{2,1,0:T(8,128)(2,1)} %param.11) | copy-start | bytes 3145732
  73.3 12.0 %collective-permute-start.7 = (bf16[32,48,128]{2,1,0:T(8,128)(2,1)S(1)}, bf16[32,48,128]{2,1,0:T(8,128)(2,1)S(1)}, u32[]{:S(2)}, u32[]{:S(2)}) collective-permute-start(bf16[32,48,128]{2,1,0:T(8,128)(2,1)S(1)} %get-tuple-element.35), channel_id=1, source_target_pairs={{0,32},{32,0},{1,33},{33,1},{2,34},{34,2},{3,35},{35,3},{4,36},{36... | collective-permute-start | bytes 1179656 | tf_op jit(solution)/shard_map/ppermute | solution.py:331
  136.6 8.5 %collective-permute-start.8 = (bf16[32,48,128]{2,1,0:T(8,128)(2,1)S(1)}, bf16[32,48,128]{2,1,0:T(8,128)(2,1)S(1)}, u32[]{:S(2)}, u32[]{:S(2)}) collective-permute-start(bf16[32,48,128]{2,1,0:T(8,128)(2,1)S(1)} %all_to_all.23.kept_ref), channel_id=1, source_target_pairs={{0,32},{32,0},{1,33},{33,1},{2,34},{34,2},{3,35},{35,3},{4,36},{36... | collective-permute-start | bytes 1179656 | tf_op jit(solution)/shard_map/ppermute | solution.py:339

commit v6 on v4

--- a/solution.py
+++ b/solution.py
@@ -1,3 +1,5 @@
+import functools
+
 import jax
 import jax.numpy as jnp
 from jax import lax
@@ -95,11 +97,12 @@
     low_zero = low_ref[pl.ds(0, RANK), :]
     back_out = back_out_ref[...]
 
-    def one_group(g, sums):
+    def one_group(count, g, sums):
         back_query, low_out = sums
+        near = pl.ds(0, count * ROWS)
         at = pl.ds(pl.multiple_of(g * HEAD_SIZE, HEAD_SIZE), HEAD_SIZE)
         value_at = pl.ds(pl.multiple_of(KEY_COLUMNS + g * HEAD_SIZE, HEAD_SIZE), HEAD_SIZE)
-        for o in range(SPAN):
+        for o in range(count):
             span = pl.ds(o * ROWS, ROWS)
             keys[span, :] = blocks[o][pl.ds(0, ROWS), at]
             values[span, :] = blocks[o][pl.ds(0, ROWS), value_at]
@@ -108,8 +111,8 @@
         grad = jnp.concatenate([grad_ref[:, h] for h in heads], axis=0)
         qT = jnp.transpose(q.astype(F32))
         gradT = jnp.transpose(grad.astype(F32))
-        k, v = keys[...], values[...]
-        scores = dot(k, qT.astype(BF)) * (INVERSE * LOG2E) + bias[...]
+        k, v = keys[near, :], values[near, :]
+        scores = dot(k, qT.astype(BF)) * (INVERSE * LOG2E) + bias[near, :]
         powers = jnp.exp2(scores - jnp.max(scores, axis=0, keepdims=True))
         recip = 1.0 / jnp.sum(powers, axis=0, keepdims=True)
         powers = powers.astype(BF)
@@ -122,10 +125,10 @@
         scaled_grad = jnp.transpose(gradT * recip).astype(BF)
         dkeys = dot(dscores, scaled_q).astype(BF)
         dvalues = dot(powers, scaled_grad).astype(BF)
-        back_parts[pl.ds(0, RANK), :] += dot(up_ref[0, :, at], dkeys, NT)
-        back_parts[pl.ds(RANK, RANK), :] += dot(up_ref[1, :, at], dvalues, NT)
-        keyval_term_ref[pl.ds(0, RANK), at] = dot(low_keys[...], dkeys)
-        keyval_term_ref[pl.ds(RANK, RANK), at] = dot(low_values[...], dvalues)
+        back_parts[pl.ds(0, RANK), near] += dot(up_ref[0, :, at], dkeys, NT)
+        back_parts[pl.ds(RANK, RANK), near] += dot(up_ref[1, :, at], dvalues, NT)
+        keyval_term_ref[pl.ds(0, RANK), at] = dot(low_keys[:, near], dkeys)
+        keyval_term_ref[pl.ds(RANK, RANK), at] = dot(low_values[:, near], dvalues)
         for i, h in enumerate(heads):
             mine = slice(i * ROWS, (i + 1) * ROWS)
             query_term_ref[:, h] = dot(low_zero, dq[:, mine], NT)
@@ -134,10 +137,19 @@
             low_out = low_out + dot(out_down_ref[:, h], attn[:, mine])
         return back_query, low_out
 
-    zero = jnp.zeros((RANK, ROWS), F32)
-    back_query, low_out = lax.fori_loop(0, KEY_HEADS, one_group, (zero, zero), unroll=True)
-    back_query_ref[...] = back_query.astype(BF)
-    low_out_ref[...] = low_out.astype(BF)
+    def all_groups(count):
+        zero = jnp.zeros((RANK, ROWS), F32)
+        back_query, low_out = lax.fori_loop(
+            0, KEY_HEADS, functools.partial(one_group, count), (zero, zero), unroll=True
+        )
+        back_query_ref[...] = back_query.astype(BF)
+        low_out_ref[...] = low_out.astype(BF)
+
+    beyond_two = jnp.max(bias[pl.ds(2 * ROWS, 6 * ROWS), pl.ds(0, ROWS)]) > -1.0
+    beyond_four = jnp.max(bias[pl.ds(4 * ROWS, 4 * ROWS), pl.ds(0, ROWS)]) > -1.0
+    pl.when(jnp.logical_not(beyond_two))(lambda: all_groups(2))
+    pl.when(jnp.logical_and(beyond_two, jnp.logical_not(beyond_four)))(lambda: all_groups(4))
+    pl.when(beyond_four)(lambda: all_groups(8))
     parts_ref[...] = jnp.zeros_like(parts_ref)
     for o in range(SPAN):
         parts_ref[lax.rem(position + (DEVICES - o), DEVICES)] = back_parts[:, pl.ds(o * ROWS, ROWS)].astype(BF)

time: 144 us -> 144 us (level)
  Pallas kernels: 15.1 us -> 10.5 us
  blocking collectives: 72 us -> 75.8 us
    pallas_call x5, Pallas kernels: 15.1 us -> 10.5 us  [call(): pl.pallas_call(kernel, name=name, out_shape=outs, in_specs=specs, out_spe...]
    all_to_all x1, blocking collectives: 20.9 us -> 25 us  [per_device(): parts = lax.all_to_all(parts, seq, 0, 0, tiled=False)]
where the time goes in v6:
time: 144 us; the launch traced here: 143 us
  blocking collectives  75.8 us (53%)
  starting transfers between devices  40.6 us (28%)
  waiting for transfers between devices  11.6 us (8%)
  Pallas kernels  10.5 us (7%)
  local copies, waits for them, and re-layouts  3.52 us (2%)
    all_to_all x1, blocking collectives, per_device(): parts = lax.all_to_all(parts, seq, 0, 0, tiled=False)  25 us
    ppermute x3, starting transfers between devices, per_device(): lax.ppermute(blocks[(9 - step) % SPAN], seq, down[step - 1])  18.4 us
    all_to_all x1, blocking collectives, per_device(): lax.all_to_all(jnp.broadcast_to(total, half), seq, 0, 0, tiled=False)  17.7 us
    all_to_all x1, blocking collectives, per_device(): lax.all_to_all(jnp.broadcast_to(total, (depth, *total.shape)), 'z', 0, 0,...  17.1 us
    all_to_all x1, blocking collectives, per_device(): total = lax.all_to_all(total, seq, 0, 0, tiled=False)  16 us
    pallas_call x5, Pallas kernels, call(): pl.pallas_call(kernel, name=name, out_shape=outs, in_specs=specs, out_spe...  10.5 us
    ppermute x1, starting transfers between devices, per_device(): lax.ppermute(sent, 'core', swap).astype(F32)  8.96 us
    ppermute x3, waiting for transfers between devices, per_device(): lax.ppermute(blocks[(9 - step) % SPAN], seq, down[step - 1])  8.91 us
  transfers between devices with their start and end apart: 9, of which 4 were waited for; matrix products, arithmetic and copies ran while one was open for 0% of the time, Pallas kernels for 1%

profile of v6, /device:TPU:1, one launch (start us, length us, event | category | flops | bytes accessed | tf_op | source)
XLA Modules:
  0.0 143.1 jit_solution(13456558009164764135)
XLA Ops:
  0.7 3.0 %keyval.1 = (bf16[48,128]{1,0:T(8,128)(2,1)}, bf16[144,1024]{1,0:T(8,128)(2,1)}) custom-call(bf16[128,4096]{1,0:T(8,128)(2,1)} %bitcast.11, bf16[48,4096]{1,0:T(8,128)(2,1)} %bitcast.19, bf16[128,1024]{1,0:T(8,128)(2,1)} %bitcast.20, bf16[2,16,512]{2,1,0:T(8,128)(2,1)} %up_ref.1, s32[1,128]{1,0:T(1,128)} %doc_any.1), custom_call_target="tpu_custom_call" | custom-call | flops 100000000 | bytes 2000000 | tf_op jit(solution)/shard_map/keyval/pallas_call | solution.py:220
  3.7 4.0 %collective-permute-start = (bf16[144,1024]{1,0:T(8,128)(2,1)}, bf16[144,1024]{1,0:T(8,128)(2,1)S(1)}, u32[]{:S(2)}, u32[]{:S(2)}) collective-permute-start(bf16[144,1024]{1,0:T(8,128)(2,1)} %get-tuple-element.27.rest_0_), channel_id=1, source_target_pairs={{0,1},{1,2},{2,3},{3,4},{4,5},{5,6},{6,7},{7,8},{8,9},{9,10},{10,1... | collective-permute-start | bytes 884744 | tf_op jit(solution)/shard_map/ppermute | solution.py:285
  7.7 4.2 %collective-permute-start.4 = (bf16[144,1024]{1,0:T(8,128)(2,1)}, bf16[144,1024]{1,0:T(8,128)(2,1)S(1)}, u32[]{:S(2)}, u32[]{:S(2)}) collective-permute-start(bf16[144,1024]{1,0:T(8,128)(2,1)} %get-tuple-element.27.rest_0_), channel_id=1, source_target_pairs={{0,7},{1,8},{2,9},{3,10},{4,11},{5,12},{6,13},{7,14},{8,15},{9,16}... | collective-permute-start | bytes 884744 | tf_op jit(solution)/shard_map/ppermute | solution.py:287
  12.0 0.7 collective-permute-start.1
  12.7 4.9 %collective-permute-done.4.rest_7_ = bf16[144,1024]{1,0:T(8,128)(2,1)S(1)} collective-permute-done((bf16[144,1024]{1,0:T(8,128)(2,1)}, bf16[144,1024]{1,0:T(8,128)(2,1)S(1)}, u32[]{:S(2)}, u32[]{:S(2)}) %collective-permute-start.4) | collective-permute-done | bytes 294944 | tf_op jit(solution)/shard_map/ppermute | solution.py:287
  17.5 6.8 %collective-permute-start.5 = (bf16[144,1024]{1,0:T(8,128)(2,1)S(1)}, bf16[144,1024]{1,0:T(8,128)(2,1)S(1)}, u32[]{:S(2)}, u32[]{:S(2)}) collective-permute-start(bf16[144,1024]{1,0:T(8,128)(2,1)S(1)} %collective-permute-done.4.rest_7_), channel_id=1, source_target_pairs={{0,31},{1,0},{7,6},{8,7},{9,8},{10,9},{11,10},{12,11},{13,12},{14,... | collective-permute-start | bytes 884744 | tf_op jit(solution)/shard_map/ppermute | solution.py:287
  24.3 0.0 collective-permute-done.1.rest_2_
  24.3 0.7 collective-permute-start.2
  25.0 4.0 %collective-permute-done.5.rest_6_ = bf16[144,1024]{1,0:T(8,128)(2,1)S(1)} collective-permute-done((bf16[144,1024]{1,0:T(8,128)(2,1)S(1)}, bf16[144,1024]{1,0:T(8,128)(2,1)S(1)}, u32[]{:S(2)}, u32[]{:S(2)}) %collective-permute-start.5) | collective-permute-done | bytes 294944 | tf_op jit(solution)/shard_map/ppermute | solution.py:287
  29.0 7.4 %collective-permute-start.6 = (bf16[144,1024]{1,0:T(8,128)(2,1)S(1)}, bf16[144,1024]{1,0:T(8,128)(2,1)S(1)}, u32[]{:S(2)}, u32[]{:S(2)}) collective-permute-start(bf16[144,1024]{1,0:T(8,128)(2,1)S(1)} %collective-permute-done.5.rest_6_), channel_id=1, source_target_pairs={{0,31},{6,5},{7,6},{8,7},{9,8},{10,9},{11,10},{12,11},{13,12},{14,... | collective-permute-start | bytes 884744 | tf_op jit(solution)/shard_map/ppermute | solution.py:287
  36.5 0.7 collective-permute-start.3
  37.2 0.0 copy-start.3
  37.2 1.0 copy-done.3
  38.2 0.8 copy-done.5
  39.1 0.8 copy-done.7
  39.9 0.7 copy-done.10
  40.6 1.1 query.1
  41.8 0.0 copy-start
  41.9 4.9 %attention.1 = (bf16[32,32,128]{2,1,0:T(8,128)(2,1)S(1)}, bf16[16,128]{1,0:T(8,128)(2,1)S(1)}, bf16[16,128]{1,0:T(8,128)(2,1)S(1)}, f32[16,2048]{1,0:T(8,128)S(1...) custom-call(bf16[48,128]{1,0:T(8,128)(2,1)S(1)} %copy-done.10, bf16[128,2048]{1,0:T(8,128)(2,1)S(1)} %get-tuple-element.24.q_ref, ...), custom_call_target="tpu_custom_call" | custom-call | flops 4000000000 | bytes 4000000 | tf_op jit(solution)/shard_map/attention/pallas_call | solution.py:220
  46.8 25.0 %all_to_all.20.parts_ref = bf16[32,32,128]{2,1,0:T(8,128)(2,1)S(1)} all-to-all(bf16[32,32,128]{2,1,0:T(8,128)(2,1)S(1)} %get-tuple-element.29), channel_id=1, replica_groups=mesh['z'=8,'core'=2,'x'=4,'y'=8] {'x','y'}, dimensions={0} | all-to-all | bytes 524288 | tf_op jit(solution)/shard_map/all_to_all | solution.py:320
  71.8 0.4 terms.1
  72.2 9.0 %collective-permute-start.7 = (bf16[32,48,128]{2,1,0:T(8,128)(2,1)S(1)}, bf16[32,48,128]{2,1,0:T(8,128)(2,1)S(1)}, u32[]{:S(2)}, u32[]{:S(2)}) collective-permute-start(bf16[32,48,128]{2,1,0:T(8,128)(2,1)S(1)} %get-tuple-element.35), channel_id=1, source_target_pairs={{0,32},{32,0},{1,33},{33,1},{2,34},{34,2},{3,35},{35,3},{4,36},{36... | collective-permute-start | bytes 1179656 | tf_op jit(solution)/shard_map/ppermute | solution.py:331
  81.2 1.3 collective-permute-done.7
  82.5 0.1 add_convert_fusion
  82.7 16.0 %all_to_all.21 = bf16[32,48,128]{2,1,0:T(8,128)(2,1)S(1)} all-to-all(bf16[32,48,128]{2,1,0:T(8,128)(2,1)S(1)} %add_convert_fusion), channel_id=1, replica_groups=mesh['z'=8,'core'=2,'x'=4,'y'=8] {'x','y'}, dimensions={0} | all-to-all | bytes 786432 | tf_op jit(solution)/shard_map/all_to_all | solution.py:332
  98.6 0.1 reduce_sum.21
  98.7 17.1 %all_to_all.22 = bf16[8,48,128]{2,1,0:T(8,128)(2,1)S(1)} all-to-all(bf16[8,48,128]{2,1,0:T(8,128)(2,1)S(1)} %broadcast_in_dim.6), channel_id=1, replica_groups=mesh['z'=8,'core'=2,'x'=4,'y'=8] {'z'}, dimensions={0} | all-to-all | bytes 196608 | tf_op jit(solution)/shard_map/all_to_all | solution.py:335
  115.9 0.1 broadcast_in_dim.7
  115.9 17.7 %all_to_all.23.kept_ref = bf16[32,48,128]{2,1,0:T(8,128)(2,1)S(1)} all-to-all(bf16[32,48,128]{2,1,0:T(8,128)(2,1)S(1)} %broadcast_in_dim.7), channel_id=1, replica_groups=mesh['z'=8,'core'=2,'x'=4,'y'=8] {'x','y'}, dimensions={0} | all-to-all | bytes 786432 | tf_op jit(solution)/shard_map/all_to_all | solution.py:338
  133.6 7.2 %collective-permute-start.8 = (bf16[32,48,128]{2,1,0:T(8,128)(2,1)S(1)}, bf16[32,48,128]{2,1,0:T(8,128)(2,1)S(1)}, u32[]{:S(2)}, u32[]{:S(2)}) collective-permute-start(bf16[32,48,128]{2,1,0:T(8,128)(2,1)S(1)} %all_to_all.23.kept_ref), channel_id=1, source_target_pairs={{0,32},{32,0},{1,33},{33,1},{2,34},{34,2},{3,35},{35,3},{4,36},{36... | collective-permute-start | bytes 1179656 | tf_op jit(solution)/shard_map/ppermute | solution.py:339
  140.8 1.3 collective-permute-done.8.sent_ref
  142.1 1.0 unpack.1
  (25 shorter events, 0.1 us)
Async XLA Ops:
  0.6 36.5 %copy-start.1 = (bf16[1,128,4096]{2,1,0:T(8,128)(2,1)S(1)}, bf16[1,128,4096]{2,1,0:T(8,128)(2,1)}, u32[]{:S(2)}) copy-start(bf16[1,128,4096]{2,1,0:T(8,128)(2,1)} %param.15) | copy-start | bytes 3145732
  0.6 36.5 %copy-start.2 = (bf16[1,128,2048]{2,1,0:T(8,128)(2,1)S(1)}, bf16[1,128,2048]{2,1,0:T(8,128)(2,1)}, u32[]{:S(2)}) copy-start(bf16[1,128,2048]{2,1,0:T(8,128)(2,1)} %param.13) | copy-start | bytes 1572868
  0.7 36.5 %copy-start.4 = (bf16[16,4096]{1,0:T(8,128)(2,1)S(1)}, bf16[16,4096]{1,0:T(8,128)(2,1)}, u32[]{:S(2)}) copy-start(bf16[16,4096]{1,0:T(8,128)(2,1)} %out_up_ref.1) | copy-start | bytes 393220
  3.7 8.3 %collective-permute-start = (bf16[144,1024]{1,0:T(8,128)(2,1)}, bf16[144,1024]{1,0:T(8,128)(2,1)S(1)}, u32[]{:S(2)}, u32[]{:S(2)}) collective-permute-start(bf16[144,1024]{1,0:T(8,128)(2,1)} %get-tuple-element.27.rest_0_), channel_id=1, source_target_pairs={{0,1},{1,2},{2,3},{3,4},{4,5},{5,6},{6,7},{7,8},{8,9},{9,10},{10,1... | collective-permute-start | bytes 884744 | tf_op jit(solution)/shard_map/ppermute | solution.py:285
  7.7 9.8 %collective-permute-start.4 = (bf16[144,1024]{1,0:T(8,128)(2,1)}, bf16[144,1024]{1,0:T(8,128)(2,1)S(1)}, u32[]{:S(2)}, u32[]{:S(2)}) collective-permute-start(bf16[144,1024]{1,0:T(8,128)(2,1)} %get-tuple-element.27.rest_0_), channel_id=1, source_target_pairs={{0,7},{1,8},{2,9},{3,10},{4,11},{5,12},{6,13},{7,14},{8,15},{9,16}... | collective-permute-start | bytes 884744 | tf_op jit(solution)/shard_map/ppermute | solution.py:287
  12.0 12.3 %collective-permute-start.1 = (bf16[144,1024]{1,0:T(8,128)(2,1)S(1)}, bf16[144,1024]{1,0:T(8,128)(2,1)S(1)}, u32[]{:S(2)}, u32[]{:S(2)}) collective-permute-start(bf16[144,1024]{1,0:T(8,128)(2,1)S(1)} %collective-permute-done.rest_1_), channel_id=1, source_target_pairs={{1,2},{2,3},{3,4},{4,5},{5,6},{6,7},{7,8},{8,9},{9,10},{10,11},{11... | collective-permute-start | bytes 884744 | tf_op jit(solution)/shard_map/ppermute | solution.py:285
  17.5 11.5 %collective-permute-start.5 = (bf16[144,1024]{1,0:T(8,128)(2,1)S(1)}, bf16[144,1024]{1,0:T(8,128)(2,1)S(1)}, u32[]{:S(2)}, u32[]{:S(2)}) collective-permute-start(bf16[144,1024]{1,0:T(8,128)(2,1)S(1)} %collective-permute-done.4.rest_7_), channel_id=1, source_target_pairs={{0,31},{1,0},{7,6},{8,7},{9,8},{10,9},{11,10},{12,11},{13,12},{14,... | collective-permute-start | bytes 884744 | tf_op jit(solution)/shard_map/ppermute | solution.py:287
  24.3 12.2 %collective-permute-start.2 = (bf16[144,1024]{1,0:T(8,128)(2,1)S(1)}, bf16[144,1024]{1,0:T(8,128)(2,1)S(1)}, u32[]{:S(2)}, u32[]{:S(2)}) collective-permute-start(bf16[144,1024]{1,0:T(8,128)(2,1)S(1)} %collective-permute-done.1.rest_2_), channel_id=1, source_target_pairs={{2,3},{3,4},{4,5},{5,6},{6,7},{7,8},{8,9},{9,10},{10,11},{11,12},{... | collective-permute-start | bytes 884744 | tf_op jit(solution)/shard_map/ppermute | solution.py:285
  29.0 12.8 %collective-permute-start.6 = (bf16[144,1024]{1,0:T(8,128)(2,1)S(1)}, bf16[144,1024]{1,0:T(8,128)(2,1)S(1)}, u32[]{:S(2)}, u32[]{:S(2)}) collective-permute-start(bf16[144,1024]{1,0:T(8,128)(2,1)S(1)} %collective-permute-done.5.rest_6_), channel_id=1, source_target_pairs={{0,31},{6,5},{7,6},{8,7},{9,8},{10,9},{11,10},{12,11},{13,12},{14,... | collective-permute-start | bytes 884744 | tf_op jit(solution)/shard_map/ppermute | solution.py:287
  36.5 5.3 %collective-permute-start.3 = (bf16[144,1024]{1,0:T(8,128)(2,1)S(1)}, bf16[144,1024]{1,0:T(8,128)(2,1)S(1)}, u32[]{:S(2)}, u32[]{:S(2)}) collective-permute-start(bf16[144,1024]{1,0:T(8,128)(2,1)S(1)} %collective-permute-done.2.rest_3_), channel_id=1, source_target_pairs={{3,4},{4,5},{5,6},{6,7},{7,8},{8,9},{9,10},{10,11},{11,12},{12,13}... | collective-permute-start | bytes 884744 | tf_op jit(solution)/shard_map/ppermute | solution.py:285
  37.2 1.0 copy-start.3
  38.2 0.8 copy-start.5
  39.1 0.8 copy-start.7
  39.9 0.7 copy-start.10
  40.6 1.2 copy-start.6
  40.6 1.2 copy-start.8
  40.6 1.2 copy-start.9
  40.6 1.2 copy-start.11
  41.8 29.9 %copy-start = (bf16[1,128,4096]{2,1,0:T(8,128)(2,1)S(1)}, bf16[1,128,4096]{2,1,0:T(8,128)(2,1)}, u32[]{:S(2)}) copy-start(bf16[1,128,4096]{2,1,0:T(8,128)(2,1)} %param.11) | copy-start | bytes 3145732
  72.2 10.3 %collective-permute-start.7 = (bf16[32,48,128]{2,1,0:T(8,128)(2,1)S(1)}, bf16[32,48,128]{2,1,0:T(8,128)(2,1)S(1)}, u32[]{:S(2)}, u32[]{:S(2)}) collective-permute-start(bf16[32,48,128]{2,1,0:T(8,128)(2,1)S(1)} %get-tuple-element.35), channel_id=1, source_target_pairs={{0,32},{32,0},{1,33},{33,1},{2,34},{34,2},{3,35},{35,3},{4,36},{36... | collective-permute-start | bytes 1179656 | tf_op jit(solution)/shard_map/ppermute | solution.py:331
  133.6 8.5 %collective-permute-start.8 = (bf16[32,48,128]{2,1,0:T(8,128)(2,1)S(1)}, bf16[32,48,128]{2,1,0:T(8,128)(2,1)S(1)}, u32[]{:S(2)}, u32[]{:S(2)}) collective-permute-start(bf16[32,48,128]{2,1,0:T(8,128)(2,1)S(1)} %all_to_all.23.kept_ref), channel_id=1, source_target_pairs={{0,32},{32,0},{1,33},{33,1},{2,34},{34,2},{3,35},{35,3},{4,36},{36... | collective-permute-start | bytes 1179656 | tf_op jit(solution)/shard_map/ppermute | solution.py:339

commit v7 on v5

--- a/solution.py
+++ b/solution.py
@@ -73,8 +73,6 @@
     parts_ref, back_query_ref, low_out_ref, query_term_ref, keyval_term_ref, out_term_ref = rest[SPAN : SPAN + 6]
     bias, keys, values, low_keys, low_values, back_parts = rest[SPAN + 6 :]
     position = lax.axis_index("x") * SPAN + lax.axis_index("y")
-    core = lax.axis_index("core")
-    offsets = [0] + [s + core * (SPAN - 2 * s) for s in (1, 2, 3, 4)] + [SPAN - s + core * (2 * s - SPAN) for s in (1, 2, 3)]
     own = blocks[0][pl.ds(ROWS, RANK), pl.ds(2 * ROWS, ROWS)][:1]
     own = jnp.broadcast_to(own.astype(F32), (ROWS, ROWS))
     row = lax.broadcasted_iota(jnp.int32, (ROWS, ROWS), 0)
@@ -89,7 +87,7 @@
         if o == 0:
             seen = seen & (row <= col)
         else:
-            seen = seen & (jnp.broadcast_to(position - offsets[o], (ROWS, ROWS)) >= 0)
+            seen = seen & (jnp.broadcast_to(position, (ROWS, ROWS)) >= o)
         one = jnp.where(seen, 0.0, -1e30)
         for i in range(GROUP):
             bias[span, pl.ds(i*ROWS, ROWS)] = one
@@ -142,7 +140,7 @@
     low_out_ref[...] = low_out.astype(BF)
     parts_ref[...] = jnp.zeros_like(parts_ref)
     for o in range(SPAN):
-        parts_ref[lax.rem(position + (DEVICES - offsets[o]), DEVICES)] = back_parts[:, pl.ds(o * ROWS, ROWS)].astype(BF)
+        parts_ref[lax.rem(position + (DEVICES - o), DEVICES)] = back_parts[:, pl.ds(o * ROWS, ROWS)].astype(BF)
 
 
 def term_kernel(x_ref, outgrad_ref, back_query_ref, parts_ref, low_out_ref,
@@ -235,10 +233,6 @@
         wanted = {(block, (place + 1) % length) for block, place in wanted}
         wanted |= {(place - offset, place) for place in range(offset, length)}
     return [sorted(wanted)] + pairs
-
-
-def both_cores(length, first, second):
-    return [a + [(i + length, j + length) for i, j in b] for a, b in zip(first, second, strict=True)]
 
 
 def per_device(
@@ -275,16 +269,12 @@
         flops=10**8, size=2 * 10**6, limit=56 << 20, kind=pl.BlockSpec(memory_space=pl.ANY),
     )
 
-    half_span = SPAN // 2
-    long = both_cores(length, pairs_up(length, half_span), pairs_down(length, half_span))
-    short = both_cores(length, pairs_down(length, half_span - 1), pairs_up(length, half_span - 1))
-    places = ("core", *seq)
-    first, second = [pack], [pack]
-    for step in range(half_span):
-        first.append(lax.ppermute(first[-1], places, long[step]))
-        if step < half_span - 1:
-            second.append(lax.ppermute(second[-1], places, short[step]))
-    blocks = first + second[1:]
+    blocks = {0: pack}
+    up, down = pairs_up(length, 3), pairs_down(length, 4)
+    for step in range(1, 5):
+        blocks[8 - step] = lax.ppermute(blocks[(9 - step) % SPAN], seq, down[step - 1])
+        if step < 4:
+            blocks[step] = lax.ppermute(blocks[step - 1], seq, up[step - 1])
 
     q, grad, back_out = call(
         query_kernel, "query",
@@ -305,7 +295,7 @@
             shape((RANK, QUERY_COLUMNS), F32),
         ),
         (low, q, grad, back_out, query_up_weight, keyvalue_up_weight, out_down,
-         *blocks),
+         *[blocks[o] for o in range(SPAN)]),
         scratch=(
             pltpu.VMEM((window, GROUP * ROWS), F32),
             pltpu.VMEM((window, HEAD_SIZE), BF),

time: 147 us -> 147 us (level)
    ppermute x1, starting transfers between devices: 10.6 us -> 7.89 us  [per_device(): lax.ppermute(sent, 'core', swap).astype(F32)]
    ppermute x7, starting transfers between devices: 30.3 us -> 32.4 us  [the longest x4 29.7 us: per_device(): lax.ppermute(blocks[(9 - step) % SPAN], seq, down[step - 1])]
where the time goes in v7:
time: 147 us
  blocking collectives  66.4 us (45%)
  starting transfers between devices  47.4 us (32%)
  Pallas kernels  15.1 us (10%)
  waiting for transfers between devices  12.9 us (9%)
  local copies, waits for them, and re-layouts  3.52 us (2%)
    ppermute x4, starting transfers between devices, per_device(): lax.ppermute(blocks[(9 - step) % SPAN], seq, down[step - 1])  29.7 us
    all_to_all x1, blocking collectives, per_device(): lax.all_to_all(jnp.broadcast_to(total, half), seq, 0, 0, tiled=False)  17.7 us
    all_to_all x1, blocking collectives, per_device(): lax.all_to_all(jnp.broadcast_to(total, (depth, *total.shape)), 'z', 0, 0,...  17.4 us
    all_to_all x1, blocking collectives, per_device(): total = lax.all_to_all(total, seq, 0, 0, tiled=False)  16 us
    all_to_all x1, blocking collectives, per_device(): parts = lax.all_to_all(parts, seq, 0, 0, tiled=False)  15.3 us
    pallas_call x5, Pallas kernels, call(): pl.pallas_call(kernel, name=name, out_shape=outs, in_specs=specs, out_spe...  15.1 us
    ppermute x4, waiting for transfers between devices, per_device(): lax.ppermute(blocks[(9 - step) % SPAN], seq, down[step - 1])  10.3 us
    ppermute x1, starting transfers between devices, per_device(): lax.ppermute(sent, 'core', swap).astype(F32)  7.89 us
  transfers between devices with their start and end apart: 9, of which 5 were waited for; matrix products, arithmetic and copies ran while one was open for 0% of the time, Pallas kernels for 1%

profile of v7, /device:TPU:1, one launch (start us, length us, event | category | flops | bytes accessed | tf_op | source)
XLA Modules:
  0.0 146.5 jit_solution(11107321805497004814)
XLA Ops:
  0.7 3.0 %keyval.1 = (bf16[48,128]{1,0:T(8,128)(2,1)}, bf16[144,1024]{1,0:T(8,128)(2,1)}) custom-call(bf16[128,4096]{1,0:T(8,128)(2,1)} %bitcast.11, bf16[48,4096]{1,0:T(8,128)(2,1)} %bitcast.19, bf16[128,1024]{1,0:T(8,128)(2,1)} %bitcast.20, bf16[2,16,512]{2,1,0:T(8,128)(2,1)} %up_ref.1, s32[1,128]{1,0:T(1,128)} %doc_any.1), custom_call_target="tpu_custom_call" | custom-call | flops 100000000 | bytes 2000000 | tf_op jit(solution)/shard_map/keyval/pallas_call | solution.py:208
  3.7 5.9 %collective-permute-start.3 = (bf16[144,1024]{1,0:T(8,128)(2,1)}, bf16[144,1024]{1,0:T(8,128)(2,1)S(1)}, u32[]{:S(2)}, u32[]{:S(2)}) collective-permute-start(bf16[144,1024]{1,0:T(8,128)(2,1)} %get-tuple-element.27.rest_0_), channel_id=1, source_target_pairs={{0,7},{1,8},{2,9},{3,10},{4,11},{5,12},{6,13},{7,14},{8,15},{9,16}... | collective-permute-start | bytes 884744 | tf_op jit(solution)/shard_map/ppermute | solution.py:275
  9.6 1.3 collective-permute-start
  10.9 3.3 %collective-permute-done.3.rest_7_ = bf16[144,1024]{1,0:T(8,128)(2,1)S(1)} collective-permute-done((bf16[144,1024]{1,0:T(8,128)(2,1)}, bf16[144,1024]{1,0:T(8,128)(2,1)S(1)}, u32[]{:S(2)}, u32[]{:S(2)}) %collective-permute-start.3) | collective-permute-done | bytes 294944 | tf_op jit(solution)/shard_map/ppermute | solution.py:275
  14.2 8.8 %collective-permute-start.4 = (bf16[144,1024]{1,0:T(8,128)(2,1)S(1)}, bf16[144,1024]{1,0:T(8,128)(2,1)S(1)}, u32[]{:S(2)}, u32[]{:S(2)}) collective-permute-start(bf16[144,1024]{1,0:T(8,128)(2,1)S(1)} %collective-permute-done.3.rest_7_), channel_id=1, source_target_pairs={{0,31},{1,0},{2,1},{7,6},{8,7},{9,8},{10,9},{11,10},{12,11},{13,12... | collective-permute-start | bytes 884744 | tf_op jit(solution)/shard_map/ppermute | solution.py:275
  23.0 0.7 collective-permute-start.1
  23.7 4.0 %collective-permute-done.4.rest_6_ = bf16[144,1024]{1,0:T(8,128)(2,1)S(1)} collective-permute-done((bf16[144,1024]{1,0:T(8,128)(2,1)S(1)}, bf16[144,1024]{1,0:T(8,128)(2,1)S(1)}, u32[]{:S(2)}, u32[]{:S(2)}) %collective-permute-start.4) | collective-permute-done | bytes 294944 | tf_op jit(solution)/shard_map/ppermute | solution.py:275
  27.7 7.4 %collective-permute-start.5 = (bf16[144,1024]{1,0:T(8,128)(2,1)S(1)}, bf16[144,1024]{1,0:T(8,128)(2,1)S(1)}, u32[]{:S(2)}, u32[]{:S(2)}) collective-permute-start(bf16[144,1024]{1,0:T(8,128)(2,1)S(1)} %collective-permute-done.4.rest_6_), channel_id=1, source_target_pairs={{0,31},{1,0},{6,5},{7,6},{8,7},{9,8},{10,9},{11,10},{12,11},{13,12... | collective-permute-start | bytes 884744 | tf_op jit(solution)/shard_map/ppermute | solution.py:275
  35.2 0.7 collective-permute-start.2
  35.9 2.9 %collective-permute-done.5.rest_5_ = bf16[144,1024]{1,0:T(8,128)(2,1)S(1)} collective-permute-done((bf16[144,1024]{1,0:T(8,128)(2,1)S(1)}, bf16[144,1024]{1,0:T(8,128)(2,1)S(1)}, u32[]{:S(2)}, u32[]{:S(2)}) %collective-permute-start.5) | collective-permute-done | bytes 294944 | tf_op jit(solution)/shard_map/ppermute | solution.py:275
  38.8 7.6 %collective-permute-start.6 = (bf16[144,1024]{1,0:T(8,128)(2,1)S(1)}, bf16[144,1024]{1,0:T(8,128)(2,1)S(1)}, u32[]{:S(2)}, u32[]{:S(2)}) collective-permute-start(bf16[144,1024]{1,0:T(8,128)(2,1)S(1)} %collective-permute-done.5.rest_5_), channel_id=1, source_target_pairs={{0,31},{5,4},{6,5},{7,6},{8,7},{9,8},{10,9},{11,10},{12,11},{13,12... | collective-permute-start | bytes 884744 | tf_op jit(solution)/shard_map/ppermute | solution.py:275
  46.4 0.0 copy-start.3
  46.4 1.0 copy-done.3
  47.5 0.8 copy-done.5
  48.3 0.8 copy-done.7
  49.2 0.7 copy-done.10
  49.9 1.1 query.1
  51.1 0.0 copy-start
  51.1 9.6 %attention.1 = (bf16[32,32,128]{2,1,0:T(8,128)(2,1)S(1)}, bf16[16,128]{1,0:T(8,128)(2,1)S(1)}, bf16[16,128]{1,0:T(8,128)(2,1)S(1)}, f32[16,2048]{1,0:T(8,128)S(1...) custom-call(bf16[48,128]{1,0:T(8,128)(2,1)S(1)} %copy-done.10, bf16[128,2048]{1,0:T(8,128)(2,1)S(1)} %get-tuple-element.24.q_ref, ...), custom_call_target="tpu_custom_call" | custom-call | flops 4000000000 | bytes 4000000 | tf_op jit(solution)/shard_map/attention/pallas_call | solution.py:208
  60.7 15.3 %all_to_all.20.parts_ref = bf16[32,32,128]{2,1,0:T(8,128)(2,1)S(1)} all-to-all(bf16[32,32,128]{2,1,0:T(8,128)(2,1)S(1)} %get-tuple-element.29), channel_id=1, replica_groups=mesh['z'=8,'core'=2,'x'=4,'y'=8] {'x','y'}, dimensions={0} | all-to-all | bytes 524288 | tf_op jit(solution)/shard_map/all_to_all | solution.py:310
  76.0 0.4 terms.1
  76.4 7.9 %collective-permute-start.7 = (bf16[32,48,128]{2,1,0:T(8,128)(2,1)S(1)}, bf16[32,48,128]{2,1,0:T(8,128)(2,1)S(1)}, u32[]{:S(2)}, u32[]{:S(2)}) collective-permute-start(bf16[32,48,128]{2,1,0:T(8,128)(2,1)S(1)} %get-tuple-element.35), channel_id=1, source_target_pairs={{0,32},{32,0},{1,33},{33,1},{2,34},{34,2},{3,35},{35,3},{4,36},{36... | collective-permute-start | bytes 1179656 | tf_op jit(solution)/shard_map/ppermute | solution.py:321
  84.3 1.3 collective-permute-done.7
  85.7 0.1 add_convert_fusion
  85.8 16.0 %all_to_all.21 = bf16[32,48,128]{2,1,0:T(8,128)(2,1)S(1)} all-to-all(bf16[32,48,128]{2,1,0:T(8,128)(2,1)S(1)} %add_convert_fusion), channel_id=1, replica_groups=mesh['z'=8,'core'=2,'x'=4,'y'=8] {'x','y'}, dimensions={0} | all-to-all | bytes 786432 | tf_op jit(solution)/shard_map/all_to_all | solution.py:322
  101.7 0.1 reduce_sum.21
  101.8 17.4 %all_to_all.22 = bf16[8,48,128]{2,1,0:T(8,128)(2,1)S(1)} all-to-all(bf16[8,48,128]{2,1,0:T(8,128)(2,1)S(1)} %broadcast_in_dim.6), channel_id=1, replica_groups=mesh['z'=8,'core'=2,'x'=4,'y'=8] {'z'}, dimensions={0} | all-to-all | bytes 196608 | tf_op jit(solution)/shard_map/all_to_all | solution.py:325
  119.3 0.1 broadcast_in_dim.7
  119.3 17.7 %all_to_all.23.kept_ref = bf16[32,48,128]{2,1,0:T(8,128)(2,1)S(1)} all-to-all(bf16[32,48,128]{2,1,0:T(8,128)(2,1)S(1)} %broadcast_in_dim.7), channel_id=1, replica_groups=mesh['z'=8,'core'=2,'x'=4,'y'=8] {'x','y'}, dimensions={0} | all-to-all | bytes 786432 | tf_op jit(solution)/shard_map/all_to_all | solution.py:328
  137.0 7.2 %collective-permute-start.8 = (bf16[32,48,128]{2,1,0:T(8,128)(2,1)S(1)}, bf16[32,48,128]{2,1,0:T(8,128)(2,1)S(1)}, u32[]{:S(2)}, u32[]{:S(2)}) collective-permute-start(bf16[32,48,128]{2,1,0:T(8,128)(2,1)S(1)} %all_to_all.23.kept_ref), channel_id=1, source_target_pairs={{0,32},{32,0},{1,33},{33,1},{2,34},{34,2},{3,35},{35,3},{4,36},{36... | collective-permute-start | bytes 1179656 | tf_op jit(solution)/shard_map/ppermute | solution.py:329
  144.2 1.3 collective-permute-done.8.sent_ref
  145.5 1.0 unpack.1
  (25 shorter events, 0.1 us)
Async XLA Ops:
  0.6 45.8 %copy-start.1 = (bf16[1,128,4096]{2,1,0:T(8,128)(2,1)S(1)}, bf16[1,128,4096]{2,1,0:T(8,128)(2,1)}, u32[]{:S(2)}) copy-start(bf16[1,128,4096]{2,1,0:T(8,128)(2,1)} %param.15) | copy-start | bytes 3145732
  0.6 45.8 %copy-start.2 = (bf16[1,128,2048]{2,1,0:T(8,128)(2,1)S(1)}, bf16[1,128,2048]{2,1,0:T(8,128)(2,1)}, u32[]{:S(2)}) copy-start(bf16[1,128,2048]{2,1,0:T(8,128)(2,1)} %param.13) | copy-start | bytes 1572868
  0.7 45.8 %copy-start.4 = (bf16[16,4096]{1,0:T(8,128)(2,1)S(1)}, bf16[16,4096]{1,0:T(8,128)(2,1)}, u32[]{:S(2)}) copy-start(bf16[16,4096]{1,0:T(8,128)(2,1)} %out_up_ref.1) | copy-start | bytes 393220
  3.7 10.6 %collective-permute-start.3 = (bf16[144,1024]{1,0:T(8,128)(2,1)}, bf16[144,1024]{1,0:T(8,128)(2,1)S(1)}, u32[]{:S(2)}, u32[]{:S(2)}) collective-permute-start(bf16[144,1024]{1,0:T(8,128)(2,1)} %get-tuple-element.27.rest_0_), channel_id=1, source_target_pairs={{0,7},{1,8},{2,9},{3,10},{4,11},{5,12},{6,13},{7,14},{8,15},{9,16}... | collective-permute-start | bytes 884744 | tf_op jit(solution)/shard_map/ppermute | solution.py:275
  9.6 13.4 %collective-permute-start = (bf16[144,1024]{1,0:T(8,128)(2,1)}, bf16[144,1024]{1,0:T(8,128)(2,1)S(1)}, u32[]{:S(2)}, u32[]{:S(2)}) collective-permute-start(bf16[144,1024]{1,0:T(8,128)(2,1)} %get-tuple-element.27.rest_0_), channel_id=1, source_target_pairs={{0,1},{1,2},{2,3},{3,4},{4,5},{5,6},{6,7},{7,8},{8,9},{9,10},{10,1... | collective-permute-start | bytes 884744 | tf_op jit(solution)/shard_map/ppermute | solution.py:277
  14.2 13.5 %collective-permute-start.4 = (bf16[144,1024]{1,0:T(8,128)(2,1)S(1)}, bf16[144,1024]{1,0:T(8,128)(2,1)S(1)}, u32[]{:S(2)}, u32[]{:S(2)}) collective-permute-start(bf16[144,1024]{1,0:T(8,128)(2,1)S(1)} %collective-permute-done.3.rest_7_), channel_id=1, source_target_pairs={{0,31},{1,0},{2,1},{7,6},{8,7},{9,8},{10,9},{11,10},{12,11},{13,12... | collective-permute-start | bytes 884744 | tf_op jit(solution)/shard_map/ppermute | solution.py:275
  23.0 12.1 %collective-permute-start.1 = (bf16[144,1024]{1,0:T(8,128)(2,1)S(1)}, bf16[144,1024]{1,0:T(8,128)(2,1)S(1)}, u32[]{:S(2)}, u32[]{:S(2)}) collective-permute-start(bf16[144,1024]{1,0:T(8,128)(2,1)S(1)} %collective-permute-done.rest_1_), channel_id=1, source_target_pairs={{1,2},{2,3},{3,4},{4,5},{5,6},{6,7},{7,8},{8,9},{9,10},{10,11},{11... | collective-permute-start | bytes 884744 | tf_op jit(solution)/shard_map/ppermute | solution.py:277
  27.7 11.1 %collective-permute-start.5 = (bf16[144,1024]{1,0:T(8,128)(2,1)S(1)}, bf16[144,1024]{1,0:T(8,128)(2,1)S(1)}, u32[]{:S(2)}, u32[]{:S(2)}) collective-permute-start(bf16[144,1024]{1,0:T(8,128)(2,1)S(1)} %collective-permute-done.4.rest_6_), channel_id=1, source_target_pairs={{0,31},{1,0},{6,5},{7,6},{8,7},{9,8},{10,9},{11,10},{12,11},{13,12... | collective-permute-start | bytes 884744 | tf_op jit(solution)/shard_map/ppermute | solution.py:275
  35.2 15.9 %collective-permute-start.2 = (bf16[144,1024]{1,0:T(8,128)(2,1)S(1)}, bf16[144,1024]{1,0:T(8,128)(2,1)S(1)}, u32[]{:S(2)}, u32[]{:S(2)}) collective-permute-start(bf16[144,1024]{1,0:T(8,128)(2,1)S(1)} %collective-permute-done.1.rest_2_), channel_id=1, source_target_pairs={{2,3},{3,4},{4,5},{5,6},{6,7},{7,8},{8,9},{9,10},{10,11},{11,12},{... | collective-permute-start | bytes 884744 | tf_op jit(solution)/shard_map/ppermute | solution.py:277
  38.8 12.2 %collective-permute-start.6 = (bf16[144,1024]{1,0:T(8,128)(2,1)S(1)}, bf16[144,1024]{1,0:T(8,128)(2,1)S(1)}, u32[]{:S(2)}, u32[]{:S(2)}) collective-permute-start(bf16[144,1024]{1,0:T(8,128)(2,1)S(1)} %collective-permute-done.5.rest_5_), channel_id=1, source_target_pairs={{0,31},{5,4},{6,5},{7,6},{8,7},{9,8},{10,9},{11,10},{12,11},{13,12... | collective-permute-start | bytes 884744 | tf_op jit(solution)/shard_map/ppermute | solution.py:275
  46.4 1.0 copy-start.3
  47.5 0.8 copy-start.5
  48.3 0.8 copy-start.7
  49.2 0.7 copy-start.10
  49.9 1.2 copy-start.6
  49.9 1.2 copy-start.8
  49.9 1.2 copy-start.9
  49.9 1.2 copy-start.11
  51.1 24.9 %copy-start = (bf16[1,128,4096]{2,1,0:T(8,128)(2,1)S(1)}, bf16[1,128,4096]{2,1,0:T(8,128)(2,1)}, u32[]{:S(2)}) copy-start(bf16[1,128,4096]{2,1,0:T(8,128)(2,1)} %param.11) | copy-start | bytes 3145732
  76.4 9.2 %collective-permute-start.7 = (bf16[32,48,128]{2,1,0:T(8,128)(2,1)S(1)}, bf16[32,48,128]{2,1,0:T(8,128)(2,1)S(1)}, u32[]{:S(2)}, u32[]{:S(2)}) collective-permute-start(bf16[32,48,128]{2,1,0:T(8,128)(2,1)S(1)} %get-tuple-element.35), channel_id=1, source_target_pairs={{0,32},{32,0},{1,33},{33,1},{2,34},{34,2},{3,35},{35,3},{4,36},{36... | collective-permute-start | bytes 1179656 | tf_op jit(solution)/shard_map/ppermute | solution.py:321
  137.0 8.5 %collective-permute-start.8 = (bf16[32,48,128]{2,1,0:T(8,128)(2,1)S(1)}, bf16[32,48,128]{2,1,0:T(8,128)(2,1)S(1)}, u32[]{:S(2)}, u32[]{:S(2)}) collective-permute-start(bf16[32,48,128]{2,1,0:T(8,128)(2,1)S(1)} %all_to_all.23.kept_ref), channel_id=1, source_target_pairs={{0,32},{32,0},{1,33},{33,1},{2,34},{34,2},{3,35},{35,3},{4,36},{36... | collective-permute-start | bytes 1179656 | tf_op jit(solution)/shard_map/ppermute | solution.py:329
